TPU v7x, 32 devices: a whole 2x2x4 slice. The times are simulated.
32 devices in a mesh: fsdp: 2 (over x), ctx: 4 (over y, core), tp: 4 (over z).
Axes of the slice: x: 2, y: 2, z: 4, core: 2. Of those that a mesh axis runs over, the one named last changes fastest.
Arguments:
- tokens: bfloat16 [2, 2048, 2304], P('fsdp', 'ctx'), may hold values from -6 to 6
- q_weight: bfloat16 [2304, 2048], P(('fsdp', 'ctx'), 'tp'), as said below
- key_weight: bfloat16 [2304, 1024], P(('fsdp', 'ctx'), 'tp'), may hold values from -0.125 to 0.125
- value_weight: bfloat16 [2304, 1024], P(('fsdp', 'ctx'), 'tp'), may hold values from -0.125 to 0.125
- out_weight: bfloat16 [2048, 2304], P('tp', ('fsdp', 'ctx')), may hold values from -0.125 to 0.125
- gate_weight: bfloat16 [2304, 9216], P(('fsdp', 'ctx'), 'tp'), may hold values from -0.125 to 0.125
- up_weight: bfloat16 [2304, 9216], P(('fsdp', 'ctx'), 'tp'), may hold values from -0.125 to 0.125
- down_weight: bfloat16 [9216, 2304], P('tp', ('fsdp', 'ctx')), may hold values from -0.0625 to 0.0625
- gain_attn_in: bfloat16 [2304], P(('fsdp', 'ctx')), may hold values from 0.099609375 to 1.8984375
- gain_attn_out: bfloat16 [2304], P(('fsdp', 'ctx')), may hold values from 0.099609375 to 1.8984375
- gain_mlp_in: bfloat16 [2304], P(('fsdp', 'ctx')), may hold values from 0.099609375 to 1.8984375
- gain_mlp_out: bfloat16 [2304], P(('fsdp', 'ctx')), may hold values from 0.099609375 to 1.8984375
- segment_ids: int32 [2, 2048], P('fsdp'), may hold values from 0 to 4, as said below
- block_order: int32 [2, 8], P('fsdp'), may hold values from 0 to 7, as said below
- cotangent: bfloat16 [2, 2048, 2304], P('fsdp', 'ctx'), may hold values from -6 to 6
Outputs:
- layer_out: bfloat16 [2, 2048, 2304], P('fsdp', 'ctx')
- grad_tokens: float32 [2, 2048, 2304], P('fsdp', 'ctx')
- grad_q_weight: float32 [2304, 2048], P(('fsdp', 'ctx'), 'tp')
- grad_key_weight: float32 [2304, 1024], P(('fsdp', 'ctx'), 'tp')
- grad_value_weight: float32 [2304, 1024], P(('fsdp', 'ctx'), 'tp')
- grad_out_weight: float32 [2048, 2304], P('tp', ('fsdp', 'ctx'))
- grad_gate_weight: float32 [2304, 9216], P(('fsdp', 'ctx'), 'tp')
- grad_up_weight: float32 [2304, 9216], P(('fsdp', 'ctx'), 'tp')
- grad_down_weight: float32 [9216, 2304], P('tp', ('fsdp', 'ctx'))
- grad_gain_attn_in: float32 [2304], P(('fsdp', 'ctx'))
- grad_gain_attn_out: float32 [2304], P(('fsdp', 'ctx'))
- grad_gain_mlp_in: float32 [2304], P(('fsdp', 'ctx'))
- grad_gain_mlp_out: float32 [2304], P(('fsdp', 'ctx'))
Inputs may be any that keep to these rules, and one draw needn't show every extreme that they name: `segment_ids`: along each sequence the ids never fall; every one of the 5 documents is present; document 0 covers at least the first 1024 positions. `block_order`: each row is a permutation of the 8 blocks; stored blocks 2j and 2j + 1 hold true blocks b and 7 - b for some b. `q_weight`: every entry is at most 24 / sqrt(2304) in magnitude.
All inputs are finite; a program needn't handle non-finite values.
Results may differ from a plain program's by a relative error of at most 0.023.
The roundings to bfloat16 on the way count: a program that leaves them out, or rounds other values in their place, can miss the bound.
Values may be sent and summed in bfloat16 or wider, within the bound.
No kernel may reach another device: no remote copies, remote signals or barrier semaphores. Data moves between devices by JAX's collectives and lax.ppermute only.
A program may use at most 256 MiB of HBM per device.

v0:
```python
import jax
import jax.numpy as jnp
from jax import lax
from jax.sharding import PartitionSpec as P

HEAD_DIM = 256
BLOCK = 256


EPS = 1e-06
CAP = 50.0
THETA = 10000.0


def normalize(values, gain):
    return (
        values
        * lax.rsqrt(jnp.mean(values * values, axis=-1, keepdims=True) + EPS)
        * gain.astype(jnp.float32)
    )


def normalize_back(values, gain, upstream):
    inverse = lax.rsqrt(jnp.mean(values * values, axis=-1, keepdims=True) + EPS)
    scaled = upstream * gain.astype(jnp.float32)
    d_values = inverse * scaled - values * inverse * inverse * inverse * jnp.mean(
        scaled * values, axis=-1, keepdims=True
    )
    d_gain = jnp.sum(upstream * values * inverse, axis=0)
    return (d_values, d_gain)


def angles_for(positions, width):
    half = width // 2
    freqs = THETA ** (-jnp.arange(half, dtype=jnp.float32) * 2.0 / width)
    angles = positions.astype(jnp.float32)[:, None] * freqs[None, :]
    return (jnp.cos(angles)[:, None, :], jnp.sin(angles)[:, None, :], half)


def rotate(values, positions):
    cosine, sine, half = angles_for(positions, values.shape[-1])
    first = values[..., :half]
    second = values[..., half:]
    return jnp.concatenate(
        [first * cosine - second * sine, second * cosine + first * sine], axis=-1
    )


def rotate_back(grads, positions):
    cosine, sine, half = angles_for(positions, grads.shape[-1])
    first = grads[..., :half]
    second = grads[..., half:]
    return jnp.concatenate(
        [first * cosine + second * sine, second * cosine - first * sine], axis=-1
    )


def outer(left, right):
    return lax.dot_general(
        left, right, (((0,), (0,)), ((), ())), preferred_element_type=jnp.float32
    )


def times_transposed(left, right):
    return lax.dot_general(
        left, right, (((1,), (1,)), ((), ())), preferred_element_type=jnp.float32
    )


def masked_scores(query_block, pos_block, seg_block, keys_all, key_pos, key_seg):
    scores = jnp.einsum("rd,kd->rk", query_block, keys_all, preferred_element_type=jnp.float32)
    bent = jnp.tanh(scores / CAP)
    allowed = (seg_block[:, None] == key_seg[None, :]) & (
        (pos_block // BLOCK)[:, None] >= (key_pos // BLOCK)[None, :]
    )
    return (jnp.where(allowed, CAP * bent, -1e30), bent)


def per_device(
    tokens,
    q_weight,
    key_weight,
    value_weight,
    out_weight,
    gate_weight,
    up_weight,
    down_weight,
    gain_attn_in,
    gain_attn_out,
    gain_mlp_in,
    gain_mlp_out,
    segment_ids,
    block_order,
    cotangent,
):
    inputs = tokens[0].astype(jnp.float32)
    tok_count = inputs.shape[0]
    q_full, key_full, value_full, out_full, gain_one, gain_two = (
        lax.all_gather(q_weight, ("fsdp", "ctx"), axis=0, tiled=True),
        lax.all_gather(key_weight, ("fsdp", "ctx"), axis=0, tiled=True),
        lax.all_gather(value_weight, ("fsdp", "ctx"), axis=0, tiled=True),
        lax.all_gather(out_weight, ("fsdp", "ctx"), axis=1, tiled=True),
        lax.all_gather(gain_attn_in, ("fsdp", "ctx"), axis=0, tiled=True),
        lax.all_gather(gain_attn_out, ("fsdp", "ctx"), axis=0, tiled=True),
    )
    order = block_order[0]
    within = jnp.arange(BLOCK, dtype=jnp.int32)
    key_pos = (order[:, None] * BLOCK + within[None, :]).reshape(-1)
    key_seg = segment_ids[0].reshape(-1, BLOCK)[order].reshape(-1)
    start = lax.axis_index("ctx") * tok_count
    query_pos = lax.dynamic_slice_in_dim(key_pos, start, tok_count)
    query_seg = lax.dynamic_slice_in_dim(key_seg, start, tok_count)
    normed_attn = normalize(inputs, gain_one).astype(jnp.bfloat16)
    q_lin = jnp.dot(normed_attn, q_full, preferred_element_type=jnp.float32)
    heads_local = q_lin.shape[1] // HEAD_DIM
    scale = HEAD_DIM ** (-0.5)
    queries = (rotate(q_lin.reshape(tok_count, heads_local, HEAD_DIM), query_pos) * scale).astype(
        jnp.bfloat16
    )
    key_lin = jnp.dot(normed_attn, key_full, preferred_element_type=jnp.float32)
    keys_own = rotate(key_lin[:, None, :], query_pos)[:, 0, :].astype(jnp.bfloat16)
    values_own = jnp.dot(normed_attn, value_full, preferred_element_type=jnp.float32).astype(
        jnp.bfloat16
    )
    keys_all, values_all = (
        lax.all_gather(keys_own, "ctx", axis=0, tiled=True),
        lax.all_gather(values_own, "ctx", axis=0, tiled=True),
    )
    rows = min(512, tok_count)
    blocks = tok_count // rows
    query_items = queries.transpose(1, 0, 2)
    pos_items = jnp.tile(query_pos.reshape(blocks, rows), (heads_local, 1))
    seg_items = jnp.tile(query_seg.reshape(blocks, rows), (heads_local, 1))

    def forward_item(item):
        query_block, pos_block, seg_block = item
        masked, bent = masked_scores(query_block, pos_block, seg_block, keys_all, key_pos, key_seg)
        highest = jnp.max(masked, axis=-1, keepdims=True)
        expo = jnp.exp(masked - highest)
        total = jnp.sum(expo, axis=-1, keepdims=True)
        weights = (expo / total).astype(jnp.bfloat16)
        output = jnp.einsum("rk,kd->rd", weights, values_all, preferred_element_type=jnp.float32)
        return (output, (highest + jnp.log(total))[:, 0])

    outputs, logsums = lax.map(forward_item, (query_items, pos_items, seg_items))
    attended = (
        outputs.transpose(1, 0, 2).reshape(tok_count, heads_local * HEAD_DIM).astype(jnp.bfloat16)
    )
    branch_attn = lax.psum(jnp.dot(attended, out_full, preferred_element_type=jnp.float32), "tp")
    resid = inputs + normalize(branch_attn, gain_two)
    gate_full, up_full, down_full, gain_three, gain_four = (
        lax.all_gather(gate_weight, ("fsdp", "ctx"), axis=0, tiled=True),
        lax.all_gather(up_weight, ("fsdp", "ctx"), axis=0, tiled=True),
        lax.all_gather(down_weight, ("fsdp", "ctx"), axis=1, tiled=True),
        lax.all_gather(gain_mlp_in, ("fsdp", "ctx"), axis=0, tiled=True),
        lax.all_gather(gain_mlp_out, ("fsdp", "ctx"), axis=0, tiled=True),
    )
    normed_mlp = normalize(resid, gain_three).astype(jnp.bfloat16)
    gate_lin = jnp.dot(normed_mlp, gate_full, preferred_element_type=jnp.float32)
    up_lin = jnp.dot(normed_mlp, up_full, preferred_element_type=jnp.float32)
    activ = (jax.nn.gelu(gate_lin, approximate=True) * up_lin).astype(jnp.bfloat16)
    branch_mlp = lax.psum(jnp.dot(activ, down_full, preferred_element_type=jnp.float32), "tp")
    layer_out = resid + normalize(branch_mlp, gain_four)
    upstream = cotangent[0].astype(jnp.float32)
    d_branch_mlp, grad_gain_four = normalize_back(branch_mlp, gain_four, upstream)
    d_mlp_low = d_branch_mlp.astype(jnp.bfloat16)
    grad_down = outer(activ, d_mlp_low)
    d_activ = times_transposed(d_mlp_low, down_full)
    unused_value, gelu_pullback = jax.vjp(
        lambda gate_in, up_in: jax.nn.gelu(gate_in, approximate=True) * up_in, gate_lin, up_lin
    )
    d_gate, d_up = gelu_pullback(d_activ)
    d_gate_low = d_gate.astype(jnp.bfloat16)
    d_up_low = d_up.astype(jnp.bfloat16)
    grad_gate = outer(normed_mlp, d_gate_low)
    grad_up = outer(normed_mlp, d_up_low)
    d_normed_mlp = lax.psum(
        times_transposed(d_gate_low, gate_full) + times_transposed(d_up_low, up_full), "tp"
    )
    d_resid_mlp, grad_gain_three = normalize_back(resid, gain_three, d_normed_mlp)
    d_resid = upstream + d_resid_mlp
    d_branch_attn, grad_gain_two = normalize_back(branch_attn, gain_two, d_resid)
    d_attn_low = d_branch_attn.astype(jnp.bfloat16)
    grad_out = outer(attended, d_attn_low)
    d_attended = times_transposed(d_attn_low, out_full).astype(jnp.bfloat16)
    d_items = d_attended.reshape(tok_count, heads_local, HEAD_DIM).transpose(1, 0, 2)

    def backward_item(sums, item):
        query_block, pos_block, seg_block, d_out, logsum = item
        masked, bent = masked_scores(query_block, pos_block, seg_block, keys_all, key_pos, key_seg)
        probs = jnp.exp(masked - logsum[:, None])
        weights = probs.astype(jnp.bfloat16)
        d_weights = jnp.einsum("rd,kd->rk", d_out, values_all, preferred_element_type=jnp.float32)
        d_values_sum = sums[1] + jnp.einsum(
            "rk,rd->kd", weights, d_out, preferred_element_type=jnp.float32
        )
        inner = jnp.sum(probs * d_weights, axis=-1, keepdims=True)
        d_scores = (probs * (d_weights - inner) * (1.0 - bent * bent)).astype(jnp.bfloat16)
        d_query = jnp.einsum("rk,kd->rd", d_scores, keys_all, preferred_element_type=jnp.float32)
        d_keys_sum = sums[0] + jnp.einsum(
            "rk,rd->kd", d_scores, query_block, preferred_element_type=jnp.float32
        )
        return ((d_keys_sum, d_values_sum), d_query)

    zeros_kv = jnp.zeros(keys_all.shape, jnp.float32)
    (d_keys_every, d_values_every), d_query_items = lax.scan(
        backward_item, (zeros_kv, zeros_kv), (query_items, pos_items, seg_items, d_items, logsums)
    )
    d_keys_rot, d_values_mine = (
        lax.psum_scatter(d_keys_every, "ctx", scatter_dimension=0, tiled=True),
        lax.psum_scatter(d_values_every, "ctx", scatter_dimension=0, tiled=True),
    )
    d_key_lin = rotate_back(d_keys_rot[:, None, :], query_pos)[:, 0, :].astype(jnp.bfloat16)
    d_value_lin = d_values_mine.astype(jnp.bfloat16)
    d_queries = d_query_items.transpose(1, 0, 2)
    d_q_lin = (
        rotate_back(d_queries * scale, query_pos)
        .reshape(tok_count, heads_local * HEAD_DIM)
        .astype(jnp.bfloat16)
    )
    grad_query = outer(normed_attn, d_q_lin)
    grad_key = outer(normed_attn, d_key_lin)
    grad_value = outer(normed_attn, d_value_lin)
    d_normed_attn = lax.psum(
        (
            times_transposed(d_q_lin, q_full)
            + times_transposed(d_key_lin, key_full)
            + times_transposed(d_value_lin, value_full)
        ).astype(jnp.bfloat16),
        "tp",
    ).astype(jnp.float32)
    d_tokens_attn, grad_gain_one = normalize_back(inputs, gain_one, d_normed_attn)
    grad_tokens = d_resid + d_tokens_attn
    every_grad = (
        lax.psum_scatter(
            grad_query.astype(jnp.bfloat16), ("fsdp", "ctx"), scatter_dimension=0, tiled=True
        ).astype(jnp.float32),
        lax.psum_scatter(
            grad_key.astype(jnp.bfloat16), ("fsdp", "ctx"), scatter_dimension=0, tiled=True
        ).astype(jnp.float32),
        lax.psum_scatter(
            grad_value.astype(jnp.bfloat16), ("fsdp", "ctx"), scatter_dimension=0, tiled=True
        ).astype(jnp.float32),
        lax.psum_scatter(
            grad_out.astype(jnp.bfloat16), ("fsdp", "ctx"), scatter_dimension=1, tiled=True
        ).astype(jnp.float32),
        lax.psum_scatter(
            grad_gain_one.astype(jnp.bfloat16), ("fsdp", "ctx"), scatter_dimension=0, tiled=True
        ).astype(jnp.float32),
        lax.psum_scatter(
            grad_gain_two.astype(jnp.bfloat16), ("fsdp", "ctx"), scatter_dimension=0, tiled=True
        ).astype(jnp.float32),
        lax.psum_scatter(
            grad_gate.astype(jnp.bfloat16), ("fsdp", "ctx"), scatter_dimension=0, tiled=True
        ).astype(jnp.float32),
        lax.psum_scatter(
            grad_up.astype(jnp.bfloat16), ("fsdp", "ctx"), scatter_dimension=0, tiled=True
        ).astype(jnp.float32),
        lax.psum_scatter(
            grad_down.astype(jnp.bfloat16), ("fsdp", "ctx"), scatter_dimension=1, tiled=True
        ).astype(jnp.float32),
        lax.psum_scatter(
            grad_gain_three.astype(jnp.bfloat16), ("fsdp", "ctx"), scatter_dimension=0, tiled=True
        ).astype(jnp.float32),
        lax.psum_scatter(
            grad_gain_four.astype(jnp.bfloat16), ("fsdp", "ctx"), scatter_dimension=0, tiled=True
        ).astype(jnp.float32),
    )
    attn_results = every_grad[:6]
    mlp_results = every_grad[6:]
    return (
        layer_out.astype(jnp.bfloat16)[None],
        grad_tokens[None],
        attn_results[0],
        attn_results[1],
        attn_results[2],
        attn_results[3],
        mlp_results[0],
        mlp_results[1],
        mlp_results[2],
        attn_results[4],
        attn_results[5],
        mlp_results[3],
        mlp_results[4],
    )


def solution(mesh):
    return jax.shard_map(
        per_device,
        mesh=mesh,
        in_specs=(
            P("fsdp", "ctx", None),
            P(("fsdp", "ctx"), "tp"),
            P(("fsdp", "ctx"), "tp"),
            P(("fsdp", "ctx"), "tp"),
            P("tp", ("fsdp", "ctx")),
            P(("fsdp", "ctx"), "tp"),
            P(("fsdp", "ctx"), "tp"),
            P("tp", ("fsdp", "ctx")),
            P(("fsdp", "ctx")),
            P(("fsdp", "ctx")),
            P(("fsdp", "ctx")),
            P(("fsdp", "ctx")),
            P("fsdp", None),
            P("fsdp", None),
            P("fsdp", "ctx", None),
        ),
        out_specs=(
            P("fsdp", "ctx", None),
            P("fsdp", "ctx", None),
            P(("fsdp", "ctx"), "tp"),
            P(("fsdp", "ctx"), "tp"),
            P(("fsdp", "ctx"), "tp"),
            P("tp", ("fsdp", "ctx")),
            P(("fsdp", "ctx"), "tp"),
            P(("fsdp", "ctx"), "tp"),
            P("tp", ("fsdp", "ctx")),
            P(("fsdp", "ctx")),
            P(("fsdp", "ctx")),
            P(("fsdp", "ctx")),
            P(("fsdp", "ctx")),
        ),
        check_vma=False,
    )
```

profile of v0, /device:TPU:0, one launch (start us, length us, event | category | flops | bytes accessed | tf_op | source)
XLA Modules:
  0.0 1594.2 jit_solution(6297504366629576011)
XLA Ops:
  14.2 25.8 %all-reduce.9 = (bf16[2304]{0:T(1024)(128)(2,1)S(1)}, bf16[2304]{0:T(1024)(128)(2,1)S(1)}, bf16[2304]{0:T(1024)(128)(2,1)S(1)}, bf16[2304]{0:T(1024)(128)(2,1)S(1)}) all-reduce(bf16[2304]{0:T(1024)(128)(2,1)S(1)} %dynamic-update-slice, bf16[2304]{0:T(1024)(128)(2,1)S(1)} %dynamic-update-slice.1, ...), channel_id=1, replica_groups=mesh['fsdp'=2,'ctx'=4,'tp'=4] {'fsdp','ctx'}, use_global_device_ids=true, to_apply=%add | all-reduce | flops 9216 | bytes 36864
  48.9 14.0 all-gather.15.cloned.1.call-done
  83.3 29.3 %all-gather.11.cloned.1.call-done = bf16[2304,512]{1,0:T(8,128)(2,1)} async-done(((bf16[288,512]{1,0:T(8,128)(2,1)}), bf16[2304,512]{1,0:T(8,128)(2,1)}) %all-gather.11.cloned.1.call-update) | async-done | bytes 2359312 | tf_op jit(solution)/shard_map/all_gather | solution.py:99
  131.3 20.2 %while.39 = (s32[]{:T(128)}, bf16[2,512,256]{1,2,0:T(8,128)(2,1)}, f32[2,512]{1,0:T(2,128)S(1)}, s32[2,512]{1,0:T(2,128)S(1)}, s32[8,256]{1,0:T(8,128)S(1)}, /*i...) while((s32[]{:T(128)}, bf16[2,512,256]{1,2,0:T(8,128)(2,1)}, ...), condition=%wide.region_4.5_spmd.clone.clone.clone, body=%wide.region_1.4_spmd.clone.clone.sunk.clone | while | flops 1086364672 | bytes 32425128 | solution.py:145
  169.8 169.9 %all-reduce.15.cloned.1.call-done = f32[512,2304]{1,0:T(8,128)} async-done(((f32[512,2304]{1,0:T(8,128)}), f32[512,2304]{1,0:T(8,128)}) %all-reduce.15.cloned.1.call-update) | async-done | bytes 4718608 | tf_op jit(solution)/shard_map/psum | solution.py:149
  347.2 57.2 %all-gather.21.cloned.1.call-done = bf16[2304,2304]{1,0:T(8,128)(2,1)} async-done(((bf16[288,2304]{1,0:T(8,128)(2,1)}), bf16[2304,2304]{1,0:T(8,128)(2,1)}) %all-gather.21.cloned.1.call-update) | async-done | bytes 10616848 | tf_op jit(solution)/shard_map/all_gather | solution.py:152
  415.7 54.5 %all-gather.23.cloned.1.call-done = bf16[2304,2304]{1,0:T(8,128)(2,1)} async-done(((bf16[288,2304]{1,0:T(8,128)(2,1)}), bf16[2304,2304]{1,0:T(8,128)(2,1)}) %all-gather.23.cloned.1.call-update) | async-done | bytes 10616848 | tf_op jit(solution)/shard_map/all_gather | solution.py:153
  470.2 12.5 multiply_convert_fusion.2
  482.7 53.1 %all-gather.25.cloned.1.call-done = bf16[2304,2304]{0,1:T(8,128)(2,1)} async-done(((bf16[2304,288]{0,1:T(8,128)(2,1)}), bf16[2304,2304]{0,1:T(8,128)(2,1)}) %all-gather.25.cloned.1.call-update) | async-done | bytes 10616848 | tf_op jit(solution)/shard_map/all_gather | solution.py:154
  547.9 171.6 %all-reduce.17.cloned.1.call-done = f32[512,2304]{1,0:T(8,128)} async-done(((f32[512,2304]{1,0:T(8,128)}), f32[512,2304]{1,0:T(8,128)}) %all-reduce.17.cloned.1.call-update) | async-done | bytes 4718608 | tf_op jit(solution)/shard_map/psum | solution.py:162
  730.7 14.7 multiply_convert_fusion.1
  755.0 12.2 convolution_add_fusion.4
  767.4 170.8 %all-reduce.19.cloned.1.call-done = f32[512,2304]{1,0:T(8,128)} async-done(((f32[512,2304]{1,0:T(8,128)}), f32[512,2304]{1,0:T(8,128)}) %all-reduce.19.cloned.1.call-update) | async-done | bytes 4718608 | tf_op jit(solution)/shard_map/psum | solution.py:177
  955.8 34.3 %while.40 = (s32[]{:T(128)}, f32[2048,256]{1,0:T(8,128)}, f32[2048,256]{1,0:T(8,128)}, f32[2,512,256]{1,2,0:T(8,128)}, s32[2,512]{1,0:T(2,128)S(1)}, /*index=5*/...) while((s32[]{:T(128)}, f32[2048,256]{1,0:T(8,128)}, ...), condition=%wide.region_16.17_spmd.clone.clone.clone.clone, body=%wide.region_14.16_spmd.clone.clone.clone.sunk.clone | while | flops 2717948928 | bytes 95113088 | solution.py:206
  1003.6 20.0 %reduce-scatter.10.cloned.1.call-done = f32[512,256]{0,1:T(8,128)} async-done(((f32[2048,256]{0,1:T(8,128)}), f32[512,256]{0,1:T(8,128)}) %reduce-scatter.10.cloned.1.call-update) | async-done | bytes 524304 | tf_op jit(solution)/shard_map/reduce_scatter | solution.py:210
  1028.2 29.4 %reduce-scatter.12.cloned.1.call-done = f32[512,256]{1,0:T(8,128)} async-done(((f32[2048,256]{1,0:T(8,128)}), f32[512,256]{1,0:T(8,128)}) %reduce-scatter.12.cloned.1.call-update) | async-done | bytes 524304 | tf_op jit(solution)/shard_map/reduce_scatter | solution.py:211
  1105.1 44.2 %reduce-scatter.20.cloned.1.call-done = bf16[512,288]{0,1:T(8,128)(2,1)} async-done(((bf16[512,2304]{0,1:T(8,128)(2,1)}), bf16[512,288]{0,1:T(8,128)(2,1)}) %reduce-scatter.20.cloned.1.call-update) | async-done | bytes 294928 | tf_op jit(solution)/shard_map/reduce_scatter | solution.py:244
  1151.2 38.0 %reduce-scatter.16.cloned.1.call-done = bf16[288,256]{1,0:T(8,128)(2,1)} async-done(((bf16[2304,256]{1,0:T(8,128)(2,1)}), bf16[288,256]{1,0:T(8,128)(2,1)}) %reduce-scatter.16.cloned.1.call-update) | async-done | bytes 147472 | tf_op jit(solution)/shard_map/reduce_scatter | solution.py:238
  1190.9 38.6 %reduce-scatter.18.cloned.1.call-done = bf16[288,256]{1,0:T(8,128)(2,1)} async-done(((bf16[2304,256]{1,0:T(8,128)(2,1)}), bf16[288,256]{1,0:T(8,128)(2,1)}) %reduce-scatter.18.cloned.1.call-update) | async-done | bytes 147472 | tf_op jit(solution)/shard_map/reduce_scatter | solution.py:241
  1231.1 96.9 %all-reduce.21.cloned.1.call-done = bf16[512,2304]{1,0:T(8,128)(2,1)} async-done(((bf16[512,2304]{1,0:T(8,128)(2,1)}), bf16[512,2304]{1,0:T(8,128)(2,1)}) %all-reduce.21.cloned.1.call-update) | async-done | bytes 2359312 | tf_op jit(solution)/shard_map/psum | solution.py:224
  1331.5 24.0 %all-reduce.8 = (bf16[2304]{0:T(1024)(128)(2,1)S(1)}, bf16[2304]{0:T(1024)(128)(2,1)S(1)}, bf16[2304]{0:T(1024)(128)(2,1)S(1)}, bf16[2304]{0:T(1024)(128)(2,1)S(1)}) all-reduce(bf16[2304]{0:T(1024)(128)(2,1)S(1)} %get-tuple-element.658, ...), channel_id=12, replica_groups=mesh['fsdp'=2,'ctx'=4,'tp'=4] {'fsdp','ctx'}, use_global_device_ids=true, to_apply=%region_29.30.clone | all-reduce | flops 9216 | bytes 36864
  1364.3 48.4 %reduce-scatter.26.cloned.1.call-done = bf16[2304,288]{0,1:T(8,128)(2,1)} async-done(((bf16[2304,2304]{0,1:T(8,128)(2,1)}), bf16[2304,288]{0,1:T(8,128)(2,1)}) %reduce-scatter.26.cloned.1.call-update) | async-done | bytes 1327120 | tf_op jit(solution)/shard_map/reduce_scatter | solution.py:259
  1415.7 82.8 %reduce-scatter.22.cloned.1.call-done = bf16[288,2304]{1,0:T(8,128)(2,1)} async-done(((bf16[2304,2304]{1,0:T(8,128)(2,1)}), bf16[288,2304]{1,0:T(8,128)(2,1)}) %reduce-scatter.22.cloned.1.call-update) | async-done | bytes 1327120 | tf_op jit(solution)/shard_map/reduce_scatter | solution.py:253
  1501.5 82.8 %reduce-scatter.24.cloned.1.call-done = bf16[288,2304]{1,0:T(8,128)(2,1)} async-done(((bf16[2304,2304]{1,0:T(8,128)(2,1)}), bf16[288,2304]{1,0:T(8,128)(2,1)}) %reduce-scatter.24.cloned.1.call-update) | async-done | bytes 1327120 | tf_op jit(solution)/shard_map/reduce_scatter | solution.py:256
  (338 shorter events, 286.5 us)
Async XLA Ops:
  7.2 36.0 %all-gather.13.cloned.1.call-start = ((), (), s32[]{:S(2)}) async-start(), calls=%async_computation.10 | async-start | bytes 1327104 | tf_op jit(solution)/shard_map/all_gather | solution.py:100
  7.9 55.0 %all-gather.15.cloned.1.call-start = ((), (), s32[]{:S(2)}) async-start(), calls=%async_computation.11 | async-start | bytes 1327104 | tf_op jit(solution)/shard_map/all_gather | solution.py:101
  8.7 73.2 %all-gather.27.cloned.1.call-start = ((), (), s32[]{:S(2)}) async-start(), calls=%async_computation.30 | async-start | bytes 1310720 | tf_op jit(solution)/shard_map/all_gather | solution.py:126
  48.2 64.4 %all-gather.11.cloned.1.call-start = ((), (), s32[]{:S(2)}) async-start(), calls=%async_computation.9 | async-start | bytes 2654208 | tf_op jit(solution)/shard_map/all_gather | solution.py:99
  48.8 82.5 %all-gather.17.cloned.1.call-start = ((), (), s32[]{:S(2)}) async-start(), calls=%async_computation.12 | async-start | bytes 1310720 | tf_op jit(solution)/shard_map/all_gather | solution.py:127
  65.7 96.4 %all-gather.19.cloned.1.call-start = ((), (), s32[]{:S(2)}) async-start(), calls=%async_computation.13 | async-start | bytes 2654208 | tf_op jit(solution)/shard_map/all_gather | solution.py:102
  66.3 273.4 %all-reduce.15.cloned.1.call-start = ((), (), s32[]{:S(2)}) async-start(), calls=%async_computation.14 | async-start | bytes 9437184 | tf_op jit(solution)/shard_map/psum | solution.py:149
  167.7 236.8 %all-gather.21.cloned.1.call-start = ((), (), s32[]{:S(2)}) async-start(), calls=%async_computation.15 | async-start | bytes 11943936 | tf_op jit(solution)/shard_map/all_gather | solution.py:152
  168.4 301.8 %all-gather.23.cloned.1.call-start = ((), (), s32[]{:S(2)}) async-start(), calls=%async_computation.16 | async-start | bytes 11943936 | tf_op jit(solution)/shard_map/all_gather | solution.py:153
  169.2 366.6 %all-gather.25.cloned.1.call-start = ((), (), s32[]{:S(2)}) async-start(), calls=%async_computation.17 | async-start | bytes 11943936 | tf_op jit(solution)/shard_map/all_gather | solution.py:154
  169.7 549.8 %all-reduce.17.cloned.1.call-start = ((), (), s32[]{:S(2)}) async-start(), calls=%async_computation.18 | async-start | bytes 9437184 | tf_op jit(solution)/shard_map/psum | solution.py:162
  547.5 390.8 %all-reduce.19.cloned.1.call-start = ((), (), s32[]{:S(2)}) async-start(), calls=%async_computation.19 | async-start | bytes 9437184 | tf_op jit(solution)/shard_map/psum | solution.py:177
  767.2 256.4 %reduce-scatter.10.cloned.1.call-start = ((), (), s32[]{:S(2)}) async-start(), calls=%async_computation.20 | async-start | bytes 2621440 | tf_op jit(solution)/shard_map/reduce_scatter | solution.py:210
  993.0 64.5 %reduce-scatter.12.cloned.1.call-start = ((), (), s32[]{:S(2)}) async-start(), calls=%async_computation.21 | async-start | bytes 2621440 | tf_op jit(solution)/shard_map/reduce_scatter | solution.py:211
  993.6 109.7 %reduce-scatter.14.cloned.1.call-start = ((), (), s32[]{:S(2)}) async-start(), calls=%async_computation.23 | async-start | bytes 2654208 | tf_op jit(solution)/shard_map/reduce_scatter | solution.py:235
  998.6 150.7 %reduce-scatter.20.cloned.1.call-start = ((), (), s32[]{:S(2)}) async-start(), calls=%async_computation.26 | async-start | bytes 2654208 | tf_op jit(solution)/shard_map/reduce_scatter | solution.py:244
  1003.6 185.7 %reduce-scatter.16.cloned.1.call-start = ((), (), s32[]{:S(2)}) async-start(), calls=%async_computation.24 | async-start | bytes 1327104 | tf_op jit(solution)/shard_map/reduce_scatter | solution.py:238
  1028.2 201.3 %reduce-scatter.18.cloned.1.call-start = ((), (), s32[]{:S(2)}) async-start(), calls=%async_computation.25 | async-start | bytes 1327104 | tf_op jit(solution)/shard_map/reduce_scatter | solution.py:241
  1060.7 267.4 %all-reduce.21.cloned.1.call-start = ((), (), s32[]{:S(2)}) async-start(), calls=%async_computation.22 | async-start | bytes 4718592 | tf_op jit(solution)/shard_map/psum | solution.py:224
  1066.7 346.0 %reduce-scatter.26.cloned.1.call-start = ((), (), s32[]{:S(2)}) async-start(), calls=%async_computation.29 | async-start | bytes 11943936 | tf_op jit(solution)/shard_map/reduce_scatter | solution.py:259
  1077.4 421.0 %reduce-scatter.22.cloned.1.call-start = ((), (), s32[]{:S(2)}) async-start(), calls=%async_computation.27 | async-start | bytes 11943936 | tf_op jit(solution)/shard_map/reduce_scatter | solution.py:253
  1087.8 496.4 %reduce-scatter.24.cloned.1.call-start = ((), (), s32[]{:S(2)}) async-start(), calls=%async_computation.28 | async-start | bytes 11943936 | tf_op jit(solution)/shard_map/reduce_scatter | solution.py:256
  1098.4 233.1 %copy-start.39 = (bf16[2304]{0:T(1024)(128)(2,1)S(1)}, bf16[2304]{0:T(1024)(128)(2,1)}, u32[]{:S(2)}) copy-start(bf16[2304]{0:T(1024)(128)(2,1)} %get-tuple-element.654) | copy-start | bytes 13828
  1098.4 233.0 %copy-start.40 = (bf16[2304]{0:T(1024)(128)(2,1)S(1)}, bf16[2304]{0:T(1024)(128)(2,1)}, u32[]{:S(2)}) copy-start(bf16[2304]{0:T(1024)(128)(2,1)} %get-tuple-element.656) | copy-start | bytes 13828
  (64 other events, 1126.3 us)
Sparse Core Ops, SparseCore 0:
  9.9 26.9 all-gather.12
  38.7 24.1 all-gather.14
  65.0 16.7 all-gather.26
  83.6 28.9 all-gather.10
  114.6 16.7 all-gather.16
  133.1 29.0 all-gather.18
  167.7 171.9 all-reduce.14
  341.6 62.7 all-gather.20
  406.3 63.8 all-gather.22
  471.9 63.8 all-gather.24
  547.6 171.9 all-reduce.16
  767.3 170.9 all-reduce.18
  993.1 30.4 reduce-scatter.9
  1026.1 31.3 reduce-scatter.11
  1060.8 42.4 reduce-scatter.13
  1106.8 42.4 reduce-scatter.19
  1152.4 36.7 reduce-scatter.15
  1192.6 36.7 reduce-scatter.17
  1232.4 95.5 all-reduce.20
  1331.4 81.2 reduce-scatter.25
  1416.2 82.2 reduce-scatter.21
  1502.0 82.1 reduce-scatter.23
where the time goes:
time: 1600 us; the launch traced here: 1590 us
  waiting for transfers between devices  1240 us (78%)
  matrix products  178 us (11%)
  other arithmetic  77.6 us (5%)
  blocking collectives  49.8 us (3%)
  local copies, waits for them, and re-layouts  29.6 us (2%)
  between operations  16.6 us (1%)
    psum x1, waiting for transfers between devices, per_device(): lax.psum(jnp.dot(activ, down_full, preferred_element_type=jnp.float32), '...  172 us
    psum x1, waiting for transfers between devices, per_device(): lax.psum(times_transposed(d_gate_low, gate_full) + times_transposed(d_up_...  171 us
    psum x1, waiting for transfers between devices, per_device(): lax.psum(jnp.dot(attended, out_full, preferred_element_type=jnp.float32),...  170 us
    psum x1, waiting for transfers between devices, per_device(): lax.psum((times_transposed(d_q_lin, q_full) + times_transposed(d_key_lin,...  96.9 us
    reduce_scatter x1, waiting for transfers between devices, per_device(): lax.psum_scatter(grad_gate.astype(jnp.bfloat16), ('fsdp', 'ctx'), scatter...  82.8 us
    reduce_scatter x1, waiting for transfers between devices, per_device(): lax.psum_scatter(grad_up.astype(jnp.bfloat16), ('fsdp', 'ctx'), scatter_d...  82.8 us
    all_gather x1, waiting for transfers between devices, per_device(): lax.all_gather(gate_weight, ('fsdp', 'ctx'), axis=0, tiled=True)  57.2 us
    all_gather x1, waiting for transfers between devices, per_device(): lax.all_gather(up_weight, ('fsdp', 'ctx'), axis=0, tiled=True)  54.5 us
  transfers between devices with their start and end apart: 22, of which 21 were waited for; matrix products, arithmetic and copies ran while one was open for 10% of the time, Pallas kernels for 0%

commit v1 on v0

v1 whole, which is shorter than its diff:
```python
import functools

import jax
import jax.numpy as jnp
import numpy as np
from jax import lax
from jax.experimental import pallas as pl
from jax.experimental.pallas import tpu as pltpu
from jax.sharding import PartitionSpec as P

HEAD_DIM = 256
BLOCK = 256
EPS = 1e-06
CAP = 50.0
THETA = 10000.0
F32 = jnp.float32
BF16 = jnp.bfloat16


class Ring:
    def __init__(self, sizes, axes):
        self.axes = axes
        outer = sizes[axes[0]] if len(axes) == 2 else 1
        inner = sizes[axes[-1]] // 2
        order = []
        for row in range(outer):
            cols = range(inner) if row % 2 == 0 else reversed(range(inner))
            order += [row * inner + col for col in cols]
        self.order = np.array(order, np.int32)
        self.count = len(order)
        self.place = np.argsort(self.order).astype(np.int32)
        self.sibling = [(i, i ^ 1) for i in range(2 * self.count)]

    def pairs(self, sign):
        out = []
        for pos in range(self.count):
            for core in range(2):
                step = sign if core == 0 else -sign
                there = self.order[(pos + step) % self.count]
                out.append((int(self.order[pos]) * 2 + core, int(there) * 2 + core))
        return out

    def locate(self):
        me = lax.axis_index(self.axes)
        core = me % 2
        pos = jnp.asarray(self.place)[me // 2]
        return pos, core

    def owner(self, pos, core, label):
        step = jnp.where(core == 0, label, -label)
        return jnp.asarray(self.order)[(pos + step) % self.count] * 2 + core

    def swap(self, value):
        return lax.ppermute(value, self.axes, self.sibling)


def put(buffer, piece, index):
    starts = (index * piece.shape[0],) + (0,) * (buffer.ndim - 1)
    return lax.dynamic_update_slice(buffer, piece, starts)


def gather(ring, shard):
    pos, core = ring.locate()
    whole = jnp.zeros((2 * ring.count * shard.shape[0],) + shard.shape[1:], shard.dtype)
    piece = shard
    for label in range(ring.count):
        if label:
            piece = lax.ppermute(piece, ring.axes, ring.pairs(-1))
        other = ring.swap(piece)
        whole = put(whole, piece, ring.owner(pos, core, label))
        whole = put(whole, other, ring.owner(pos, 1 - core, label))
    return whole


def scatter(ring, value, wire):
    pos, core = ring.locate()
    rows = value.shape[0] // (2 * ring.count)

    def block(kind, label):
        start = ring.owner(pos, kind, label) * rows
        return lax.dynamic_slice_in_dim(value, start, rows).astype(wire)

    def both(label):
        count = ring.count
        theirs = block(1 - core, label)
        return block(core, label % count).astype(F32) + ring.swap(theirs).astype(F32)

    total = both(ring.count - 1) if ring.count > 1 else both(0)
    for label in range(ring.count - 2, -1, -1):
        got = lax.ppermute(total.astype(wire), ring.axes, ring.pairs(1))
        total = both(label) + got.astype(F32)
    return total


def tp_pairs(count):
    return [(i, (i + 1) % count) for i in range(count)]


def tp_scatter(part, count):
    here = lax.axis_index("tp")
    rows = part.shape[0] // count

    def chunk(back):
        return lax.dynamic_slice_in_dim(part, ((here - back) % count) * rows, rows)

    total = chunk(1).astype(F32)
    for step in range(1, count):
        got = lax.ppermute(total.astype(BF16), "tp", tp_pairs(count))
        total = chunk(step + 1).astype(F32) + got.astype(F32)
    return total


def tp_gather(own, count):
    here = lax.axis_index("tp")
    whole = put(jnp.zeros((count * own.shape[0],) + own.shape[1:], own.dtype), own, here)
    piece = own
    for step in range(1, count):
        piece = lax.ppermute(piece, "tp", tp_pairs(count))
        whole = put(whole, piece, (here - step) % count)
    return whole


def inverse_of(values):
    return lax.rsqrt(jnp.mean(values * values, axis=-1, keepdims=True) + EPS)


def norm_back(values, inverse, gain, upstream):
    scaled = upstream * gain
    d_values = inverse * scaled - values * (
        inverse * inverse * inverse * jnp.mean(scaled * values, axis=-1, keepdims=True)
    )
    return d_values, jnp.sum(upstream * values * inverse, axis=0)


def rotate(values, cosine, sine):
    half = values.shape[-1] // 2
    first, second = values[..., :half], values[..., half:]
    return jnp.concatenate(
        [first * cosine - second * sine, second * cosine + first * sine], axis=-1
    )


def dot(left, right):
    return jnp.dot(left, right, preferred_element_type=F32)


def dot_nt(left, right):
    return lax.dot_general(left, right, (((1,), (1,)), ((), ())), preferred_element_type=F32)


def dot_tn(left, right):
    return lax.dot_general(left, right, (((0,), (0,)), ((), ())), preferred_element_type=F32)


GELU_A = 0.7978845608028654
GELU_B = 0.044715


def gelu(gate):
    return 0.5 * gate * (1.0 + jnp.tanh(GELU_A * (gate + GELU_B * gate * gate * gate)))


def gelu_and_slope(gate):
    square = gate * gate
    bent = jnp.tanh(GELU_A * (gate + GELU_B * gate * square))
    half = 0.5 * (1.0 + bent)
    slope = half + 0.5 * gate * (1.0 - bent * bent) * GELU_A * (1.0 + 3.0 * GELU_B * square)
    return gate * half, slope


def stack_heads(ref, rows, first, count):
    return jnp.concatenate(
        [ref[rows, pl.ds((first + h) * HEAD_DIM, HEAD_DIM)] for h in range(count)], axis=0
    )


def attend_kernel(heads, info, q_ref, kv_ref, qseg_ref, kseg_ref, out_ref, inv_ref, p_ref):
    low, high = info[0], info[1]
    rows = heads * BLOCK
    every = pl.ds(0, BLOCK)
    query = stack_heads(q_ref, every, 0, heads)
    qseg = jnp.concatenate([qseg_ref[...]] * heads, axis=0)

    def first(j, acc):
        start = pl.multiple_of(info[2 + j] * BLOCK, BLOCK)
        scores = dot_nt(query, kv_ref[pl.ds(start, BLOCK), pl.ds(0, HEAD_DIM)])
        weight = jnp.exp(CAP * jnp.tanh(scores * (1.0 / CAP)))
        weight = jnp.where(qseg == kseg_ref[pl.ds(j, 1), :], weight, 0.0)
        p_ref[j] = weight
        return acc + weight[:, :128] + weight[:, 128:]

    acc = lax.fori_loop(low, high + 1, first, jnp.zeros((rows, 128), F32))
    inverse = 1.0 / jnp.sum(acc, axis=1, keepdims=True)
    inv_ref[...] = inverse

    def second(j, total):
        start = pl.multiple_of(info[2 + j] * BLOCK, BLOCK)
        low_probs = (p_ref[j] * inverse).astype(BF16)
        return total + dot(low_probs, kv_ref[pl.ds(start, BLOCK), pl.ds(HEAD_DIM, HEAD_DIM)])

    total = lax.fori_loop(low, high + 1, second, jnp.zeros((rows, HEAD_DIM), F32))
    for h in range(heads):
        out_ref[:, pl.ds(h * HEAD_DIM, HEAD_DIM)] = total[h * BLOCK : (h + 1) * BLOCK].astype(BF16)


def vmem():
    return pl.BlockSpec(memory_space=pltpu.VMEM)


def attend(info, queries, kv, qseg, kseg, heads):
    blocks = kseg.shape[0]
    return pl.pallas_call(
        functools.partial(attend_kernel, heads),
        out_shape=(
            jax.ShapeDtypeStruct((BLOCK, heads * HEAD_DIM), BF16),
            jax.ShapeDtypeStruct((heads * BLOCK, 1), F32),
        ),
        in_specs=[pl.BlockSpec(memory_space=pltpu.SMEM)] + [vmem()] * 4,
        out_specs=(vmem(), vmem()),
        scratch_shapes=[pltpu.VMEM((blocks, heads * BLOCK, BLOCK), F32)],
        compiler_params=pltpu.CompilerParams(vmem_limit_bytes=(24 if blocks <= 8 else 48) << 20),
        cost_estimate=pl.CostEstimate(
            flops=3 * heads * BLOCK * blocks * BLOCK * HEAD_DIM,
            bytes_accessed=4 << 20,
            transcendentals=heads * BLOCK * blocks * BLOCK,
        ),
        name="attend",
    )(info, queries, kv, qseg, kseg)


def attend_back_kernel(
    heads, each, info, q_ref, do_ref, kv_ref, inv_ref, qseg_ref, kseg_ref, dq_ref, dkv_ref,
    p_ref, g_ref, dp_ref,
):
    blocks_q = q_ref.shape[0] // BLOCK
    dkv_ref[...] = jnp.zeros(dkv_ref.shape, F32)
    keys = pl.ds(0, HEAD_DIM)
    vals = pl.ds(HEAD_DIM, HEAD_DIM)
    for i in range(blocks_q):
        low, high = info[2 * i], info[2 * i + 1]
        qrows = pl.ds(i * BLOCK, BLOCK)
        qseg = jnp.concatenate([qseg_ref[qrows, :]] * each, axis=0)
        for h in range(0, heads, each):
            query = stack_heads(q_ref, qrows, h, each)
            d_out = stack_heads(do_ref, qrows, h, each)
            inverse = inv_ref[pl.ds((i * heads + h) * BLOCK, each * BLOCK), :]

            def first(j, acc, query=query, d_out=d_out, inverse=inverse, qseg=qseg):
                start = pl.multiple_of(info[2 * blocks_q + j] * BLOCK, BLOCK)
                place = pl.ds(start, BLOCK)
                bent = jnp.tanh(dot_nt(query, kv_ref[place, keys]) * (1.0 / CAP))
                probs = jnp.exp(CAP * bent) * inverse
                probs = jnp.where(qseg == kseg_ref[pl.ds(j, 1), :], probs, 0.0)
                d_probs = dot_nt(d_out, kv_ref[place, vals])
                p_ref[j] = probs.astype(BF16)
                g_ref[j] = probs * (1.0 - bent * bent)
                dp_ref[j] = d_probs
                both = probs * d_probs
                return acc + both[:, :128] + both[:, 128:]

            acc = lax.fori_loop(low, high + 1, first, jnp.zeros((each * BLOCK, 128), F32))
            inner = jnp.sum(acc, axis=1, keepdims=True)

            def second(j, total, query=query, d_out=d_out, inner=inner):
                start = pl.multiple_of(info[2 * blocks_q + j] * BLOCK, BLOCK)
                place = pl.ds(start, BLOCK)
                d_scores = (g_ref[j] * (dp_ref[j] - inner)).astype(BF16)
                dkv_ref[place, keys] += dot_tn(d_scores, query)
                dkv_ref[place, vals] += dot_tn(p_ref[j], d_out)
                return total + dot(d_scores, kv_ref[place, keys])

            total = lax.fori_loop(
                low, high + 1, second, jnp.zeros((each * BLOCK, HEAD_DIM), F32)
            )
            for n in range(each):
                dq_ref[qrows, pl.ds((h + n) * HEAD_DIM, HEAD_DIM)] = total[
                    n * BLOCK : (n + 1) * BLOCK
                ]


def attend_back(info, queries, d_out, kv, inverse, qseg, kseg, heads):
    blocks = kseg.shape[0]
    each = heads if blocks <= 8 else 1
    tile = (blocks, each * BLOCK, BLOCK)
    return pl.pallas_call(
        functools.partial(attend_back_kernel, heads, each),
        out_shape=(
            jax.ShapeDtypeStruct(queries.shape, F32),
            jax.ShapeDtypeStruct(kv.shape, F32),
        ),
        in_specs=[pl.BlockSpec(memory_space=pltpu.SMEM)] + [vmem()] * 6,
        out_specs=(vmem(), vmem()),
        scratch_shapes=[pltpu.VMEM(tile, BF16), pltpu.VMEM(tile, F32), pltpu.VMEM(tile, F32)],
        compiler_params=pltpu.CompilerParams(vmem_limit_bytes=(32 if blocks <= 8 else 56) << 20),
        cost_estimate=pl.CostEstimate(
            flops=11 * heads * BLOCK * blocks * BLOCK * HEAD_DIM,
            bytes_accessed=10 << 20,
            transcendentals=2 * heads * BLOCK * blocks * BLOCK,
        ),
        name="attend_back",
    )(info, queries, d_out, kv, inverse, qseg, kseg)


def per_device(
    sizes,
    tokens,
    q_weight,
    key_weight,
    value_weight,
    out_weight,
    gate_weight,
    up_weight,
    down_weight,
    gain_attn_in,
    gain_attn_out,
    gain_mlp_in,
    gain_mlp_out,
    segment_ids,
    block_order,
    cotangent,
):
    tp = sizes["tp"]
    wide = Ring(sizes, ("fsdp", "ctx"))
    near = Ring(sizes, ("ctx",))
    group = 2 * wide.count
    here = lax.axis_index("tp")
    tok = tokens[0]
    count, width = tok.shape
    halves = count // BLOCK
    share = BLOCK // tp
    heads = q_weight.shape[1] // HEAD_DIM
    qcols = q_weight.shape[1]

    qkv_w = gather(wide, jnp.concatenate([q_weight, key_weight, value_weight], axis=1))
    out_w = gather(wide, out_weight.T)
    gains_own = jnp.stack([gain_attn_in, gain_attn_out, gain_mlp_in, gain_mlp_out])
    gains = gather(wide, gains_own[None]).astype(F32)
    gains = gains.transpose(1, 0, 2).reshape(4, width)
    gain_one, gain_two, gain_three, gain_four = (gains[i] for i in range(4))
    gate_w = gather(wide, gate_weight)
    up_w = gather(wide, up_weight)
    down_w = gather(wide, down_weight.T)

    order = block_order[0]
    blocks = order.shape[0]
    stored = jnp.argsort(order).astype(jnp.int32)
    segs = segment_ids[0].reshape(blocks, BLOCK)
    first_block = lax.axis_index("ctx") * halves
    high = lax.dynamic_slice_in_dim(order, first_block, halves)
    qsegs = segs[high]
    low = jnp.sum((segs[None, :, -1] < qsegs[:, :1]).astype(jnp.int32), axis=1)
    bounds = jnp.stack([low, high], axis=1).astype(jnp.int32)
    infos = [jnp.concatenate([bounds[i], stored]) for i in range(halves)]
    info_all = jnp.concatenate([bounds.reshape(-1), stored])
    qseg = qsegs.reshape(count, 1)

    spot = (high[:, None] * BLOCK + jnp.arange(BLOCK, dtype=jnp.int32)[None]).reshape(-1)
    half_dim = HEAD_DIM // 2
    freqs = THETA ** (-jnp.arange(half_dim, dtype=F32) * 2.0 / HEAD_DIM)
    angles = spot.astype(F32)[:, None] * freqs[None, :]
    cosine, sine = jnp.cos(angles), jnp.sin(angles)
    scale = HEAD_DIM**-0.5

    inputs = tok.astype(F32)
    inv_one = inverse_of(inputs)
    normed_attn = (inputs * inv_one * gain_one).astype(BF16)
    lin = dot(normed_attn, qkv_w)
    q_lin = lin[:, :qcols].reshape(count, heads, HEAD_DIM)
    queries = (rotate(q_lin, cosine[:, None], sine[:, None]) * scale).astype(BF16)
    queries = queries.reshape(count, qcols)
    keys = rotate(lin[:, qcols : qcols + HEAD_DIM], cosine, sine).astype(BF16)
    values = lin[:, qcols + HEAD_DIM :].astype(BF16)
    kv = gather(near, jnp.concatenate([keys, values], axis=1))

    def rows_of(array, i):
        return lax.slice_in_dim(array, i * BLOCK, (i + 1) * BLOCK)

    def share_of(array, i):
        return lax.dynamic_slice_in_dim(array, i * BLOCK + here * share, share).astype(F32)

    attended, inverse_sum, branch_attn, inv_two, resid, inv_three, normed_mlp = ([] for _ in range(7))
    for i in range(halves):
        out, inv = attend(infos[i], rows_of(queries, i), kv, rows_of(qseg, i), segs, heads)
        attended.append(out)
        inverse_sum.append(inv)
        branch = tp_scatter(dot_nt(out, out_w), tp)
        branch_attn.append(branch)
        inv_two.append(inverse_of(branch))
        resid.append(share_of(tok, i) + branch * inv_two[i] * gain_two)
        inv_three.append(inverse_of(resid[i]))
        normed_mlp.append(tp_gather((resid[i] * inv_three[i] * gain_three).astype(BF16), tp))

    gate_lin, up_lin, activ, layer_out, d_mlp_low, grad_four = ([] for _ in range(6))
    for i in range(halves):
        gate_lin.append(dot(normed_mlp[i], gate_w))
        up_lin.append(dot(normed_mlp[i], up_w))
        activ.append((gelu(gate_lin[i]) * up_lin[i]).astype(BF16))
        branch = tp_scatter(dot_nt(activ[i], down_w), tp)
        inv = inverse_of(branch)
        layer_out.append(tp_gather((resid[i] + branch * inv * gain_four).astype(BF16), tp))
        d_branch, d_gain = norm_back(branch, inv, gain_four, share_of(cotangent[0], i))
        grad_four.append(d_gain)
        d_mlp_low.append(tp_gather(d_branch.astype(BF16), tp))

    d_gate, d_up, d_resid, d_attn_low, grad_three, grad_two, d_attended = ([] for _ in range(7))
    for i in range(halves):
        d_activ = dot(d_mlp_low[i], down_w)
        bent, slope = gelu_and_slope(gate_lin[i])
        d_gate.append((d_activ * up_lin[i] * slope).astype(BF16))
        d_up.append((d_activ * bent).astype(BF16))
        d_normed = tp_scatter(dot_nt(d_gate[i], gate_w) + dot_nt(d_up[i], up_w), tp)
        d_in, d_gain = norm_back(resid[i], inv_three[i], gain_three, d_normed)
        grad_three.append(d_gain)
        d_resid.append(share_of(cotangent[0], i) + d_in)
        d_branch, d_gain = norm_back(branch_attn[i], inv_two[i], gain_two, d_resid[i])
        grad_two.append(d_gain)
        d_attn_low.append(tp_gather(d_branch.astype(BF16), tp))
        d_attended.append(dot(d_attn_low[i], out_w).astype(BF16))

    def joined(pieces):
        return jnp.concatenate(pieces, axis=0)

    normed_all = joined(normed_mlp)
    grad_down = scatter(wide, dot_tn(joined(d_mlp_low), joined(activ)).astype(BF16), BF16)
    grad_gate = scatter(wide, dot_tn(normed_all, joined(d_gate)).astype(BF16), BF16)
    grad_up = scatter(wide, dot_tn(normed_all, joined(d_up)).astype(BF16), BF16)
    grad_out = scatter(wide, dot_tn(joined(d_attn_low), joined(attended)).astype(BF16), BF16)

    d_queries, d_kv = attend_back(
        info_all, queries, joined(d_attended), kv, joined(inverse_sum), qseg, segs, heads
    )
    d_kv = scatter(near, d_kv, BF16)
    d_q_lin = rotate(
        d_queries.reshape(count, heads, HEAD_DIM) * scale, cosine[:, None], -sine[:, None]
    ).astype(BF16)
    d_key_lin = rotate(d_kv[:, :HEAD_DIM], cosine, -sine).astype(BF16)
    d_lin = jnp.concatenate(
        [d_q_lin.reshape(count, qcols), d_key_lin, d_kv[:, HEAD_DIM:].astype(BF16)], axis=1
    )
    d_normed_attn = dot_nt(d_lin, qkv_w)
    grad_qkv = scatter(wide, dot_tn(normed_attn, d_lin).astype(BF16), BF16)
    grad_one = jnp.sum(d_normed_attn * inputs * inv_one, axis=0)
    grad_tokens = []
    for i in range(halves):
        d_normed = tp_scatter(rows_of(d_normed_attn, i), tp)
        own = share_of(tok, i)
        d_in, unused = norm_back(own, inverse_of(own), gain_one, d_normed)
        grad_tokens.append(tp_gather((d_resid[i] + d_in).astype(BF16), tp))

    grad_gains = jnp.stack([grad_one, sum(grad_two), sum(grad_three), sum(grad_four)])
    grad_gains = grad_gains.reshape(4, group, width // group).transpose(1, 0, 2)
    grad_gains = scatter(wide, grad_gains, F32)[0]
    travelling = grad_gains
    for step in range(1, tp):
        travelling = lax.ppermute(travelling, "tp", tp_pairs(tp))
        grad_gains = grad_gains + travelling

    return (
        joined(layer_out)[None],
        joined(grad_tokens).astype(F32)[None],
        grad_qkv[:, :qcols],
        grad_qkv[:, qcols : qcols + HEAD_DIM],
        grad_qkv[:, qcols + HEAD_DIM :],
        grad_out.T,
        grad_gate,
        grad_up,
        grad_down.T,
        grad_gains[0],
        grad_gains[1],
        grad_gains[2],
        grad_gains[3],
    )


def solution(mesh):
    sizes = dict(mesh.shape)
    split = ("fsdp", "ctx")
    rows, cols = P(split, "tp"), P("tp", split)
    acts, ids = P("fsdp", "ctx", None), P("fsdp", None)
    return jax.shard_map(
        functools.partial(per_device, sizes),
        mesh=mesh,
        in_specs=(acts, rows, rows, rows, cols, rows, rows, cols)
        + (P(split),) * 4
        + (ids, ids, acts),
        out_specs=(acts, acts, rows, rows, rows, cols, rows, rows, cols) + (P(split),) * 4,
        check_vma=False,
    )
```

time: 1600 us -> 941 us (0.59)
  waiting for transfers between devices: 1240 us -> 491 us
  local copies, waits for them, and re-layouts: 29.6 us -> 129 us
  starting transfers between devices: 1.65 us -> 66 us
  blocking collectives: 49.8 us -> 0 us
  matrix products: 178 us -> 132 us
  Pallas kernels: 0 us -> 17.1 us
    psum x4 -> x0, waiting for transfers between devices: 609 us -> none  [the longest x1 172 us: per_device(): lax.psum(jnp.dot(activ, down_full, preferred_element_type=jnp.float32), '...]
    ppermute x0 -> x147, waiting for transfers between devices: none -> 491 us  [the longest x30 161 us: tp_gather(): piece = lax.ppermute(piece, 'tp', tp_pairs(count))]
    reduce_scatter x9 -> x0, waiting for transfers between devices: 388 us -> none  [the longest x1 82.8 us: per_device(): lax.psum_scatter(grad_gate.astype(jnp.bfloat16), ('fsdp', 'ctx'), scatter...]
    all_gather x9 -> x0, waiting for transfers between devices: 238 us -> none  [the longest x1 57.2 us: per_device(): lax.all_gather(gate_weight, ('fsdp', 'ctx'), axis=0, tiled=True)]
    ppermute x0 -> x147, starting transfers between devices: none -> 66 us  [the longest x19 21.6 us: gather(): piece = lax.ppermute(piece, ring.axes, ring.pairs(-1))]
    dynamic_update_slice x2 -> x80, local copies, waits for them, and re-layouts: 0.08 us -> 61 us  [put(): return lax.dynamic_update_slice(buffer, piece, starts)]
    unnamed x2 -> x0, blocking collectives: 49.8 us -> none
    dot_general x35 -> x23, matrix products: 178 us -> 132 us  [the longest x9 52.5 us: dot_nt(): lax.dot_general(left, right, (((1,), (1,)), ((), ())), preferred_element_...]
  transfers between devices with their start and end apart: 22 -> 147, of which waited for: 21 -> 77; matrix products, arithmetic and copies ran while one was open for 10% -> 33% of each run, Pallas kernels for 0% -> 2%
where the time goes in v1:
time: 941 us; the launch traced here: 932 us
  waiting for transfers between devices  491 us (52%)
  matrix products  132 us (14%)
  local copies, waits for them, and re-layouts  129 us (14%)
  other arithmetic  82.1 us (9%)
  starting transfers between devices  66 us (7%)
  Pallas kernels  17.1 us (2%)
  between operations  14 us (1%)
    ppermute x30, waiting for transfers between devices, tp_gather(): piece = lax.ppermute(piece, 'tp', tp_pairs(count))  161 us
    ppermute x24, waiting for transfers between devices, tp_scatter(): got = lax.ppermute(total.astype(BF16), 'tp', tp_pairs(count))  144 us
    ppermute x19, waiting for transfers between devices, scatter(): got = lax.ppermute(total.astype(wire), ring.axes, ring.pairs(1))  92.9 us
    ppermute x19, waiting for transfers between devices, gather(): piece = lax.ppermute(piece, ring.axes, ring.pairs(-1))  73.9 us
    dynamic_update_slice x80, local copies, waits for them, and re-layouts, put(): return lax.dynamic_update_slice(buffer, piece, starts)  61 us
    dot_general x9, matrix products, dot_nt(): lax.dot_general(left, right, (((1,), (1,)), ((), ())), preferred_element_...  52.5 us
    dot_general x9, matrix products, dot(): return jnp.dot(left, right, preferred_element_type=F32)  46.3 us
    dot_general x5, matrix products, dot_tn(): lax.dot_general(left, right, (((0,), (0,)), ((), ())), preferred_element_...  33.3 us
  transfers between devices with their start and end apart: 147, of which 77 were waited for; matrix products, arithmetic and copies ran while one was open for 33% of the time, Pallas kernels for 2%

profile of v1, /device:TPU:0, one launch (start us, length us, event | category | flops | bytes accessed | tf_op | source)
XLA Modules:
  0.0 931.8 jit_solution(11117996999309198774)
XLA Ops:
  83.8 11.3 %collective-permute-done.22 = bf16[288,512]{1,0:T(8,128)(2,1)S(1)} collective-permute-done((bf16[288,512]{1,0:T(8,128)(2,1)S(1)}, bf16[288,512]{1,0:T(8,128)(2,1)S(1)}, u32[]{:S(2)}, u32[]{:S(2)}) %collective-permute-start.22) | collective-permute-done | bytes 294944 | tf_op jit(solution)/shard_map/ppermute | solution.py:68
  121.2 9.5 %collective-permute-done.45 = bf16[288,2304]{1,0:T(8,128)(2,1)} collective-permute-done((bf16[288,2304]{1,0:T(8,128)(2,1)S(1)}, bf16[288,2304]{1,0:T(8,128)(2,1)}, u32[]{:S(2)}, u32[]{:S(2)}) %collective-permute-start.45) | collective-permute-done | bytes 1327136 | tf_op jit(solution)/shard_map/ppermute | solution.py:68
  174.7 10.5 %collective-permute-done.47 = bf16[288,2304]{1,0:T(8,128)(2,1)S(1)} collective-permute-done((bf16[288,2304]{1,0:T(8,128)(2,1)}, bf16[288,2304]{1,0:T(8,128)(2,1)S(1)}, u32[]{:S(2)}, u32[]{:S(2)}) %collective-permute-start.47) | collective-permute-done | bytes 1327136 | tf_op jit(solution)/shard_map/ppermute | solution.py:68
  241.6 9.5 %collective-permute-done.59 = bf16[64,2304]{1,0:T(8,128)(2,1)S(1)} collective-permute-done((bf16[64,2304]{1,0:T(8,128)(2,1)S(1)}, bf16[64,2304]{1,0:T(8,128)(2,1)S(1)}, u32[]{:S(2)}, u32[]{:S(2)}) %collective-permute-start.59) | collective-permute-done | bytes 294944 | tf_op jit(solution)/shard_map/ppermute | solution.py:108
  260.5 11.0 %collective-permute-done.27 = bf16[64,2304]{1,0:T(8,128)(2,1)S(1)} collective-permute-done((bf16[64,2304]{1,0:T(8,128)(2,1)S(1)}, bf16[64,2304]{1,0:T(8,128)(2,1)S(1)}, u32[]{:S(2)}, u32[]{:S(2)}) %collective-permute-start.27) | collective-permute-done | bytes 294944 | tf_op jit(solution)/shard_map/ppermute | solution.py:118
  326.8 9.3 fusion.22
  343.4 11.0 %collective-permute-done.63 = bf16[64,2304]{1,0:T(8,128)(2,1)S(1)} collective-permute-done((bf16[64,2304]{1,0:T(8,128)(2,1)S(1)}, bf16[64,2304]{1,0:T(8,128)(2,1)S(1)}, u32[]{:S(2)}, u32[]{:S(2)}) %collective-permute-start.63) | collective-permute-done | bytes 294944 | tf_op jit(solution)/shard_map/ppermute | solution.py:108
  471.6 9.0 multiply_convert_fusion.3
  490.2 10.2 %convolution_convert_fusion.1 = bf16[2304,2304]{1,0:T(8,128)(2,1)} fusion(bf16[256,2304]{1,0:T(8,128)(2,1)} %copy-done.84, bf16[256,2304]{1,0:T(8,128)(2,1)} %copy-done.85, bf16[256,2304]{1,0:T(8,128)(2,1)S(1)} %copy-done.60, bf16[256,2304]{1,0:T(8,128)(2,1)S(1)} %copy-done.58), kind=kOutput, calls=%fused_computation.2 | convolution fusion | flops 5450563584 | bytes 15335424 | tf_op jit(solution)/shard_map/dot_general | solution.py:152
  508.7 10.1 %convolution_convert_fusion.2 = bf16[2304,2304]{1,0:T(8,128)(2,1)} fusion(bf16[256,2304]{1,0:T(8,128)(2,1)} %get-tuple-element.113, bf16[256,2304]{1,0:T(8,128)(2,1)} %get-tuple-element.111, bf16[256,2304]{1,0:T(8,128)(2,1)} %copy-done.59, bf16[256,2304]{1,0:T(8,128)(2,1)S(1)} %copy-done.58), kind=kOutput, calls=%fused_computation.3 | convolution fusion | flops 5450563584 | bytes 15335424 | tf_op jit(solution)/shard_map/dot_general | solution.py:152
  546.9 9.0 collective-permute-done.73
  556.4 9.8 %collective-permute-done.82 = bf16[64,2304]{1,0:T(8,128)(2,1)S(1)} collective-permute-done((bf16[64,2304]{1,0:T(8,128)(2,1)S(1)}, bf16[64,2304]{1,0:T(8,128)(2,1)S(1)}, u32[]{:S(2)}, u32[]{:S(2)}) %collective-permute-start.82) | collective-permute-done | bytes 294944 | tf_op jit(solution)/shard_map/ppermute | solution.py:108
  566.3 9.2 collective-permute-done.74
  633.7 9.7 %attend_back.1 = (f32[512,512]{1,0:T(8,128)S(1)}, f32[2048,512]{1,0:T(8,128)S(1)}) custom-call(s32[12]{0:T(128)S(1)} %copy-done.6, bf16[512,512]{1,0:T(8,128)(2,1)S(1)} %bitcast.175, bf16[512,512]{1,0:T(8,128)(2,1)S(1)} %pad_maximum_fusion.5.do_ref, bf16[2048,512]{1,0:T(8,128)(2,1)S(1)} %constant_dynamic-update-slice_fusion.64.kv_ref, ...), custom_call_target="tpu_custom_call" | custom-call | flops 2952790016 | bytes 10485760 | tf_op jit(solution)/shard_map/attend_back/pallas_call | solution.py:285
  667.5 9.0 collective-permute-done.89
  732.4 9.3 collective-permute-done.96
  741.8 11.0 %collective-permute-done.90 = bf16[64,2304]{1,0:T(8,128)(2,1)S(1)} collective-permute-done((bf16[64,2304]{1,0:T(8,128)(2,1)S(1)}, bf16[64,2304]{1,0:T(8,128)(2,1)S(1)}, u32[]{:S(2)}, u32[]{:S(2)}) %collective-permute-start.90) | collective-permute-done | bytes 294944 | tf_op jit(solution)/shard_map/ppermute | solution.py:108
  752.8 11.1 %collective-permute-done.97 = bf16[64,2304]{1,0:T(8,128)(2,1)S(1)} collective-permute-done((bf16[64,2304]{1,0:T(8,128)(2,1)S(1)}, bf16[64,2304]{1,0:T(8,128)(2,1)S(1)}, u32[]{:S(2)}, u32[]{:S(2)}) %collective-permute-start.97) | collective-permute-done | bytes 294944 | tf_op jit(solution)/shard_map/ppermute | solution.py:108
  805.1 11.5 %collective-permute-done.128 = bf16[288,2304]{1,0:T(8,128)(2,1)S(1)} collective-permute-done((bf16[288,2304]{1,0:T(8,128)(2,1)S(1)}, bf16[288,2304]{1,0:T(8,128)(2,1)S(1)}, u32[]{:S(2)}, u32[]{:S(2)}) %collective-permute-start.128) | collective-permute-done | bytes 1327136 | tf_op jit(solution)/shard_map/ppermute | solution.py:90
  818.9 11.9 %collective-permute-done.121 = bf16[288,2304]{1,0:T(8,128)(2,1)S(1)} collective-permute-done((bf16[288,2304]{1,0:T(8,128)(2,1)S(1)}, bf16[288,2304]{1,0:T(8,128)(2,1)S(1)}, u32[]{:S(2)}, u32[]{:S(2)}) %collective-permute-start.121) | collective-permute-done | bytes 1327136 | tf_op jit(solution)/shard_map/ppermute | solution.py:90
  848.8 10.9 %collective-permute-done.94 = bf16[64,2304]{1,0:T(8,128)(2,1)S(1)} collective-permute-done((bf16[64,2304]{1,0:T(8,128)(2,1)S(1)}, bf16[64,2304]{1,0:T(8,128)(2,1)S(1)}, u32[]{:S(2)}, u32[]{:S(2)}) %collective-permute-start.94) | collective-permute-done | bytes 294944 | tf_op jit(solution)/shard_map/ppermute | solution.py:118
  883.6 12.6 %collective-permute-done.108 = bf16[288,1024]{1,0:T(8,128)(2,1)S(1)} collective-permute-done((bf16[288,1024]{1,0:T(8,128)(2,1)S(1)}, bf16[288,1024]{1,0:T(8,128)(2,1)S(1)}, u32[]{:S(2)}, u32[]{:S(2)}) %collective-permute-start.108) | collective-permute-done | bytes 589856 | tf_op jit(solution)/shard_map/ppermute | solution.py:90
  903.8 10.2 %collective-permute-done.129 = bf16[288,2304]{1,0:T(8,128)(2,1)S(1)} collective-permute-done((bf16[288,2304]{1,0:T(8,128)(2,1)S(1)}, bf16[288,2304]{1,0:T(8,128)(2,1)S(1)}, u32[]{:S(2)}, u32[]{:S(2)}) %collective-permute-start.129) | collective-permute-done | bytes 1327136 | tf_op jit(solution)/shard_map/ppermute | solution.py:90
  917.4 10.8 %collective-permute-done.122 = bf16[288,2304]{1,0:T(8,128)(2,1)S(1)} collective-permute-done((bf16[288,2304]{1,0:T(8,128)(2,1)S(1)}, bf16[288,2304]{1,0:T(8,128)(2,1)S(1)}, u32[]{:S(2)}, u32[]{:S(2)}) %collective-permute-start.122) | collective-permute-done | bytes 1327136 | tf_op jit(solution)/shard_map/ppermute | solution.py:90
  (772 shorter events, 670.4 us)
Async XLA Ops:
  5.5 68.4 %collective-permute-start.7 = (bf16[288,1024]{1,0:T(8,128)(2,1)}, bf16[288,1024]{1,0:T(8,128)(2,1)}, u32[]{:S(2)}, u32[]{:S(2)}) collective-permute-start(bf16[288,1024]{1,0:T(8,128)(2,1)} %constant_dynamic-update-slice_fusion.84), channel_id=1, source_target_pairs={{0,4},{4,0},{8,12},{12,8},{16,20},{20,16},{24,28},{28,24},{1,5},{5... | collective-permute-start | bytes 1769480 | tf_op jit(solution)/shard_map/ppermute | solution.py:54
  6.0 66.4 %collective-permute-start.8 = (bf16[288,1024]{1,0:T(8,128)(2,1)}, bf16[288,1024]{1,0:T(8,128)(2,1)}, u32[]{:S(2)}, u32[]{:S(2)}) collective-permute-start(bf16[288,1024]{1,0:T(8,128)(2,1)} %constant_dynamic-update-slice_fusion.84), channel_id=1, source_target_pairs={{0,16},{4,12},{8,0},{12,28},{24,8},{28,20},{16,24},{20,4},{1,17},{... | collective-permute-start | bytes 1769480 | tf_op jit(solution)/shard_map/ppermute | solution.py:68
  20.6 38.5 %collective-permute-start = (bf16[1,4,288]{2,1,0:T(4,128)(2,1)S(1)}, bf16[1,4,288]{2,1,0:T(4,128)(2,1)S(1)}, u32[]{:S(2)}, u32[]{:S(2)}) collective-permute-start(bf16[1,4,288]{2,1,0:T(4,128)(2,1)S(1)} %get-tuple-element.90), channel_id=1, source_target_pairs={{0,4},{4,0},{8,12},{12,8},{16,20},{20,16},{24,28},{28,24},{1,5},{5... | collective-permute-start | bytes 6920 | tf_op jit(solution)/shard_map/ppermute | solution.py:54
  20.9 37.7 %collective-permute-start.1 = (bf16[1,4,288]{2,1,0:T(4,128)(2,1)S(1)}, bf16[1,4,288]{2,1,0:T(4,128)(2,1)S(1)}, u32[]{:S(2)}, u32[]{:S(2)}) collective-permute-start(bf16[1,4,288]{2,1,0:T(4,128)(2,1)S(1)} %get-tuple-element.90), channel_id=1, source_target_pairs={{0,16},{4,12},{8,0},{12,28},{24,8},{28,20},{16,24},{20,4},{1,17},{... | collective-permute-start | bytes 6920 | tf_op jit(solution)/shard_map/ppermute | solution.py:68
  22.3 50.0 %collective-permute-start.17 = (bf16[288,512]{1,0:T(8,128)(2,1)}, bf16[288,512]{1,0:T(8,128)(2,1)S(1)}, u32[]{:S(2)}, u32[]{:S(2)}) collective-permute-start(bf16[288,512]{1,0:T(8,128)(2,1)} %bitcast.197), channel_id=1, source_target_pairs={{0,4},{4,0},{8,12},{12,8},{16,20},{20,16},{24,28},{28,24},{1,5},{5... | collective-permute-start | bytes 884744 | tf_op jit(solution)/shard_map/ppermute | solution.py:54
  169.7 48.1 %collective-permute-start.34 = (bf16[288,2304]{1,0:T(8,128)(2,1)}, bf16[288,2304]{1,0:T(8,128)(2,1)}, u32[]{:S(2)}, u32[]{:S(2)}) collective-permute-start(bf16[288,2304]{1,0:T(8,128)(2,1)} %collective-permute-done.33), channel_id=1, source_target_pairs={{0,4},{4,0},{8,12},{12,8},{16,20},{20,16},{24,28},{28,24},{1,5},{5... | collective-permute-start | bytes 3981320 | tf_op jit(solution)/shard_map/ppermute | solution.py:54
  172.2 50.9 %collective-permute-start.35 = (bf16[288,2304]{1,0:T(8,128)(2,1)}, bf16[288,2304]{1,0:T(8,128)(2,1)}, u32[]{:S(2)}, u32[]{:S(2)}) collective-permute-start(bf16[288,2304]{1,0:T(8,128)(2,1)} %collective-permute-done.33), channel_id=1, source_target_pairs={{0,16},{4,12},{8,0},{12,28},{24,8},{28,20},{16,24},{20,4},{1,17},{... | collective-permute-start | bytes 3981320 | tf_op jit(solution)/shard_map/ppermute | solution.py:68
  185.2 40.5 %collective-permute-start.41 = (bf16[288,2304]{1,0:T(8,128)(2,1)}, bf16[288,2304]{1,0:T(8,128)(2,1)}, u32[]{:S(2)}, u32[]{:S(2)}) collective-permute-start(bf16[288,2304]{1,0:T(8,128)(2,1)} %collective-permute-done.40), channel_id=1, source_target_pairs={{0,4},{4,0},{8,12},{12,8},{16,20},{20,16},{24,28},{28,24},{1,5},{5... | collective-permute-start | bytes 3981320 | tf_op jit(solution)/shard_map/ppermute | solution.py:54
  228.2 73.7 %collective-permute-start.36 = (bf16[288,2304]{1,0:T(8,128)(2,1)}, bf16[288,2304]{1,0:T(8,128)(2,1)S(1)}, u32[]{:S(2)}, u32[]{:S(2)}) collective-permute-start(bf16[288,2304]{1,0:T(8,128)(2,1)} %collective-permute-done.35), channel_id=1, source_target_pairs={{0,4},{4,0},{8,12},{12,8},{16,20},{20,16},{24,28},{28,24},{1,5},{5... | collective-permute-start | bytes 3981320 | tf_op jit(solution)/shard_map/ppermute | solution.py:54
  231.5 73.5 %collective-permute-start.43 = (bf16[288,2304]{1,0:T(8,128)(2,1)}, bf16[288,2304]{1,0:T(8,128)(2,1)S(1)}, u32[]{:S(2)}, u32[]{:S(2)}) collective-permute-start(bf16[288,2304]{1,0:T(8,128)(2,1)} %collective-permute-done.42), channel_id=1, source_target_pairs={{0,4},{4,0},{8,12},{12,8},{16,20},{20,16},{24,28},{28,24},{1,5},{5... | collective-permute-start | bytes 3981320 | tf_op jit(solution)/shard_map/ppermute | solution.py:54
  237.0 78.8 %collective-permute-start.50 = (bf16[288,2304]{1,0:T(8,128)(2,1)S(1)}, bf16[288,2304]{1,0:T(8,128)(2,1)S(1)}, u32[]{:S(2)}, u32[]{:S(2)}) collective-permute-start(bf16[288,2304]{1,0:T(8,128)(2,1)S(1)} %collective-permute-done.49), channel_id=1, source_target_pairs={{0,4},{4,0},{8,12},{12,8},{16,20},{20,16},{24,28},{28,24},{1,5},{5... | collective-permute-start | bytes 3981320 | tf_op jit(solution)/shard_map/ppermute | solution.py:54
  426.2 36.9 %collective-permute-start.71 = (bf16[64,2304]{1,0:T(8,128)(2,1)S(1)}, bf16[64,2304]{1,0:T(8,128)(2,1)S(1)}, u32[]{:S(2)}, u32[]{:S(2)}) collective-permute-start(bf16[64,2304]{1,0:T(8,128)(2,1)S(1)} %collective-permute-done.70), channel_id=1, source_target_pairs={{0,1},{1,2},{2,3},{3,0},{4,5},{5,6},{6,7},{7,4},{8,9},{9,10},{10,1... | collective-permute-start | bytes 884744 | tf_op jit(solution)/shard_map/ppermute | solution.py:118
  432.5 107.2 %collective-permute-start.56 = (bf16[64,2304]{1,0:T(8,128)(2,1)S(1)}, bf16[64,2304]{1,0:T(8,128)(2,1)}, u32[]{:S(2)}, u32[]{:S(2)}) collective-permute-start(bf16[64,2304]{1,0:T(8,128)(2,1)S(1)} %collective-permute-done.55), channel_id=1, source_target_pairs={{0,1},{1,2},{2,3},{3,0},{4,5},{5,6},{6,7},{7,4},{8,9},{9,10},{10,1... | collective-permute-start | bytes 884744 | tf_op jit(solution)/shard_map/ppermute | solution.py:118
  438.9 101.8 %collective-permute-start.68 = (bf16[64,2304]{1,0:T(8,128)(2,1)}, bf16[64,2304]{1,0:T(8,128)(2,1)}, u32[]{:S(2)}, u32[]{:S(2)}) collective-permute-start(bf16[64,2304]{1,0:T(8,128)(2,1)} %collective-permute-done.67), channel_id=1, source_target_pairs={{0,1},{1,2},{2,3},{3,0},{4,5},{5,6},{6,7},{7,4},{8,9},{9,10},{10,1... | collective-permute-start | bytes 884744 | tf_op jit(solution)/shard_map/ppermute | solution.py:118
  532.0 74.1 %collective-permute-start.133 = (bf16[288,2304]{1,0:T(8,128)(2,1)}, bf16[288,2304]{1,0:T(8,128)(2,1)}, u32[]{:S(2)}, u32[]{:S(2)}) collective-permute-start(bf16[288,2304]{1,0:T(8,128)(2,1)} %get-tuple-element.94), channel_id=1, source_target_pairs={{0,4},{4,0},{8,12},{12,8},{16,20},{20,16},{24,28},{28,24},{1,5},{5... | collective-permute-start | bytes 3981320 | tf_op jit(solution)/shard_map/ppermute | solution.py:54
  539.8 121.5 %collective-permute-start.132 = (bf16[288,2304]{1,0:T(8,128)(2,1)}, bf16[288,2304]{1,0:T(8,128)(2,1)}, u32[]{:S(2)}, u32[]{:S(2)}) collective-permute-start(bf16[288,2304]{1,0:T(8,128)(2,1)} %get-tuple-element.95), channel_id=1, source_target_pairs={{0,4},{4,0},{8,12},{12,8},{16,20},{20,16},{24,28},{28,24},{1,5},{5... | collective-permute-start | bytes 3981320 | tf_op jit(solution)/shard_map/ppermute | solution.py:54
  540.8 68.4 %collective-permute-start.126 = (bf16[288,2304]{1,0:T(8,128)(2,1)}, bf16[288,2304]{1,0:T(8,128)(2,1)}, u32[]{:S(2)}, u32[]{:S(2)}) collective-permute-start(bf16[288,2304]{1,0:T(8,128)(2,1)} %get-tuple-element.98), channel_id=1, source_target_pairs={{0,4},{4,0},{8,12},{12,8},{16,20},{20,16},{24,28},{28,24},{1,5},{5... | collective-permute-start | bytes 3981320 | tf_op jit(solution)/shard_map/ppermute | solution.py:54
  543.9 70.2 %collective-permute-start.119 = (bf16[288,2304]{1,0:T(8,128)(2,1)}, bf16[288,2304]{1,0:T(8,128)(2,1)}, u32[]{:S(2)}, u32[]{:S(2)}) collective-permute-start(bf16[288,2304]{1,0:T(8,128)(2,1)} %get-tuple-element.102), channel_id=1, source_target_pairs={{0,4},{4,0},{8,12},{12,8},{16,20},{20,16},{24,28},{28,24},{1,5},{5... | collective-permute-start | bytes 3981320 | tf_op jit(solution)/shard_map/ppermute | solution.py:54
  609.2 52.6 %collective-permute-start.134 = (bf16[288,2304]{1,0:T(8,128)(2,1)}, bf16[288,2304]{1,0:T(8,128)(2,1)}, u32[]{:S(2)}, u32[]{:S(2)}) collective-permute-start(bf16[288,2304]{1,0:T(8,128)(2,1)} %add_convert_fusion.2), channel_id=1, source_target_pairs={{0,8},{4,20},{8,24},{12,4},{24,16},{28,12},{16,0},{20,28},{1,9},{5... | collective-permute-start | bytes 3981320 | tf_op jit(solution)/shard_map/ppermute | solution.py:90
  653.4 139.3 %collective-permute-start.131 = (bf16[288,2304]{1,0:T(8,128)(2,1)}, bf16[288,2304]{1,0:T(8,128)(2,1)}, u32[]{:S(2)}, u32[]{:S(2)}) collective-permute-start(bf16[288,2304]{1,0:T(8,128)(2,1)} %get-tuple-element.96), channel_id=1, source_target_pairs={{0,4},{4,0},{8,12},{12,8},{16,20},{20,16},{24,28},{28,24},{1,5},{5... | collective-permute-start | bytes 3981320 | tf_op jit(solution)/shard_map/ppermute | solution.py:54
  686.6 212.2 %collective-permute-start.130 = (bf16[288,2304]{1,0:T(8,128)(2,1)}, bf16[288,2304]{1,0:T(8,128)(2,1)S(1)}, u32[]{:S(2)}, u32[]{:S(2)}) collective-permute-start(bf16[288,2304]{1,0:T(8,128)(2,1)} %get-tuple-element.93), channel_id=1, source_target_pairs={{0,4},{4,0},{8,12},{12,8},{16,20},{20,16},{24,28},{28,24},{1,5},{5... | collective-permute-start | bytes 3981320 | tf_op jit(solution)/shard_map/ppermute | solution.py:54
  692.7 79.8 %collective-permute-start.109 = (bf16[288,512]{1,0:T(8,128)(2,1)S(1)}, bf16[288,512]{1,0:T(8,128)(2,1)S(1)}, u32[]{:S(2)}, u32[]{:S(2)}) collective-permute-start(bf16[288,512]{1,0:T(8,128)(2,1)S(1)} %copy-done.63), channel_id=1, source_target_pairs={{0,4},{4,0},{8,12},{12,8},{16,20},{20,16},{24,28},{28,24},{1,5},{5... | collective-permute-start | bytes 884744 | tf_op jit(solution)/shard_map/ppermute | solution.py:54
  715.3 57.3 %collective-permute-start.115 = (bf16[288,512]{1,0:T(8,128)(2,1)S(1)}, bf16[288,512]{1,0:T(8,128)(2,1)S(1)}, u32[]{:S(2)}, u32[]{:S(2)}) collective-permute-start(bf16[288,512]{1,0:T(8,128)(2,1)S(1)} %copy-done.64), channel_id=1, source_target_pairs={{0,8},{4,20},{8,24},{12,4},{24,16},{28,12},{16,0},{20,28},{1,9},{5... | collective-permute-start | bytes 884744 | tf_op jit(solution)/shard_map/ppermute | solution.py:90
  805.0 98.8 %collective-permute-start.123 = (bf16[288,2304]{1,0:T(8,128)(2,1)S(1)}, bf16[288,2304]{1,0:T(8,128)(2,1)S(1)}, u32[]{:S(2)}, u32[]{:S(2)}) collective-permute-start(bf16[288,2304]{1,0:T(8,128)(2,1)S(1)} %copy-done.50), channel_id=1, source_target_pairs={{0,4},{4,0},{8,12},{12,8},{16,20},{20,16},{24,28},{28,24},{1,5},{5... | collective-permute-start | bytes 3981320 | tf_op jit(solution)/shard_map/ppermute | solution.py:54
  (222 other events, 3459.1 us)

commit v2 on v1

--- a/solution.py
+++ b/solution.py
@@ -54,25 +54,32 @@
         return lax.ppermute(value, self.axes, self.sibling)
 
 
+def after(value, *deps):
+    return lax.optimization_barrier((value,) + deps)[0]
+
+
 def put(buffer, piece, index):
     starts = (index * piece.shape[0],) + (0,) * (buffer.ndim - 1)
     return lax.dynamic_update_slice(buffer, piece, starts)
 
 
-def gather(ring, shard):
+def gather_steps(ring, shard):
     pos, core = ring.locate()
     whole = jnp.zeros((2 * ring.count * shard.shape[0],) + shard.shape[1:], shard.dtype)
     piece = shard
     for label in range(ring.count):
         if label:
+            waits = yield piece
             piece = lax.ppermute(piece, ring.axes, ring.pairs(-1))
+            if waits:
+                piece = after(piece, *waits)
         other = ring.swap(piece)
         whole = put(whole, piece, ring.owner(pos, core, label))
         whole = put(whole, other, ring.owner(pos, 1 - core, label))
-    return whole
-
-
-def scatter(ring, value, wire):
+    yield whole
+
+
+def scatter_steps(ring, value, wire):
     pos, core = ring.locate()
     rows = value.shape[0] // (2 * ring.count)
 
@@ -80,16 +87,25 @@
         start = ring.owner(pos, kind, label) * rows
         return lax.dynamic_slice_in_dim(value, start, rows).astype(wire)
 
+    labels = range(ring.count)
+    other = [ring.swap(block(1 - core, label)) for label in labels]
+
     def both(label):
-        count = ring.count
-        theirs = block(1 - core, label)
-        return block(core, label % count).astype(F32) + ring.swap(theirs).astype(F32)
-
-    total = both(ring.count - 1) if ring.count > 1 else both(0)
+        return block(core, label).astype(F32) + other[label].astype(F32)
+
+    total = both(ring.count - 1)
     for label in range(ring.count - 2, -1, -1):
-        got = lax.ppermute(total.astype(wire), ring.axes, ring.pairs(1))
+        total = total.astype(wire)
+        waits = yield total
+        got = lax.ppermute(total, ring.axes, ring.pairs(1))
+        if waits:
+            got = after(got, *waits)
         total = both(label) + got.astype(F32)
-    return total
+    yield total
+
+
+def scatter(ring, value, wire):
+    return finish(begun(scatter_steps(ring, value, wire)), ring.count - 1)
 
 
 def tp_pairs(count):
@@ -103,21 +119,51 @@
     def chunk(back):
         return lax.dynamic_slice_in_dim(part, ((here - back) % count) * rows, rows)
 
-    total = chunk(1).astype(F32)
+    total = chunk(1).astype(BF16)
     for step in range(1, count):
-        got = lax.ppermute(total.astype(BF16), "tp", tp_pairs(count))
+        waits = yield total
+        got = lax.ppermute(total, "tp", tp_pairs(count))
+        if waits:
+            got = after(got, *waits)
         total = chunk(step + 1).astype(F32) + got.astype(F32)
-    return total
-
-
-def tp_gather(own, count):
+        if step + 1 < count:
+            total = total.astype(BF16)
+    yield total
+
+
+def tp_gather(own, count, kind=BF16):
     here = lax.axis_index("tp")
-    whole = put(jnp.zeros((count * own.shape[0],) + own.shape[1:], own.dtype), own, here)
+    axis = own.ndim - 2
+    rows = own.shape[axis]
+    shape = own.shape[:axis] + (count * rows,) + own.shape[axis + 1 :]
+
+    def place(whole, piece, index):
+        return lax.dynamic_update_slice_in_dim(whole, piece.astype(kind), index * rows, axis)
+
+    whole = place(jnp.zeros(shape, kind), own, here)
     piece = own
     for step in range(1, count):
+        waits = yield piece
         piece = lax.ppermute(piece, "tp", tp_pairs(count))
-        whole = put(whole, piece, (here - step) % count)
-    return whole
+        if waits:
+            piece = after(piece, *waits)
+        whole = place(whole, piece, (here - step) % count)
+    yield whole
+
+
+def step(steps, *waits):
+    return steps.send(waits)
+
+
+def begun(steps):
+    next(steps)
+    return steps
+
+
+def finish(steps, count):
+    for _ in range(count):
+        last = step(steps)
+    return last
 
 
 def inverse_of(values):
@@ -166,6 +212,230 @@
     half = 0.5 * (1.0 + bent)
     slope = half + 0.5 * gate * (1.0 - bent * bent) * GELU_A * (1.0 + 3.0 * GELU_B * square)
     return gate * half, slope
+
+
+def spec(shape, where):
+    return pl.BlockSpec(shape, where)
+
+
+TILE = 768
+
+
+def call(body, grid, in_specs, out_specs, out_shape, flops, moved, name, limit=44):
+    return pl.pallas_call(
+        body,
+        grid=(grid,),
+        in_specs=in_specs,
+        out_specs=out_specs,
+        out_shape=out_shape,
+        compiler_params=pltpu.CompilerParams(
+            dimension_semantics=("arbitrary",), vmem_limit_bytes=limit << 20
+        ),
+        cost_estimate=pl.CostEstimate(flops=flops, bytes_accessed=moved, transcendentals=0),
+        name=name,
+    )
+
+
+def held_kernel(*refs):
+    pass
+
+
+def held(value, *deps):
+    return pl.pallas_call(
+        held_kernel,
+        in_specs=[pl.BlockSpec(memory_space=pl.ANY)] * (1 + len(deps)),
+        out_specs=pl.BlockSpec(memory_space=pl.ANY),
+        out_shape=jax.ShapeDtypeStruct(value.shape, value.dtype),
+        input_output_aliases={0: 0},
+        compiler_params=pltpu.CompilerParams(has_side_effects=True),
+        name="held",
+    )(value, *deps)
+
+
+def gate_up_kernel(x_ref, gate_ref, up_ref, gate_out, up_out, activ_out):
+    gate = dot(x_ref[...], gate_ref[...])
+    up = dot(x_ref[...], up_ref[...])
+    gate_out[...] = gate
+    up_out[...] = up
+    activ_out[...] = (gelu(gate) * up).astype(BF16)
+
+
+def gate_up(x, weights):
+    rows, depth = x.shape
+    units = weights.shape[1] // 2
+    tiles = units // TILE
+    tile = spec((rows, TILE), lambda j: (0, j))
+    return call(
+        gate_up_kernel,
+        tiles,
+        [
+            spec((rows, depth), lambda j: (0, 0)),
+            spec((depth, TILE), lambda j: (0, j)),
+            spec((depth, TILE), lambda j: (0, j + tiles)),
+        ],
+        (tile, tile, tile),
+        tuple(jax.ShapeDtypeStruct((rows, units), kind) for kind in (F32, F32, BF16)),
+        4 * rows * depth * units,
+        4 * depth * units + 12 * rows * units,
+        "gate_up",
+    )(x, weights, weights)
+
+
+def down_kernel(x_ref, w_ref, out_ref):
+    out_ref[...] = dot_nt(x_ref[...], w_ref[...]).astype(out_ref.dtype)
+
+
+def down(x, weights):
+    rows, units = x.shape
+    width = weights.shape[0]
+    return call(
+        down_kernel,
+        width // TILE,
+        [spec((rows, units), lambda j: (0, 0)), spec((TILE, units), lambda j: (j, 0))],
+        spec((rows, TILE), lambda j: (0, j)),
+        jax.ShapeDtypeStruct((rows, width), BF16),
+        2 * rows * width * units,
+        2 * width * units,
+        "down",
+    )(x, weights)
+
+
+def d_activ_kernel(x_ref, w_ref, gate_ref, up_ref, d_gate_ref, d_up_ref):
+    d_activ = dot(x_ref[...], w_ref[...])
+    bent, slope = gelu_and_slope(gate_ref[...])
+    d_gate_ref[...] = (d_activ * up_ref[...] * slope).astype(BF16)
+    d_up_ref[...] = (d_activ * bent).astype(BF16)
+
+
+def d_gate_up(x, weights, gate_lin, up_lin):
+    rows, width = x.shape
+    units = weights.shape[1]
+    tile = spec((rows, TILE), lambda j: (0, j))
+    return call(
+        d_activ_kernel,
+        units // TILE,
+        [
+            spec((rows, width), lambda j: (0, 0)),
+            spec((width, TILE), lambda j: (0, j)),
+            tile,
+            tile,
+        ],
+        (tile, tile),
+        tuple(jax.ShapeDtypeStruct((rows, units), BF16) for _ in range(2)),
+        2 * rows * width * units,
+        2 * width * units + 12 * rows * units,
+        "d_gate_up",
+    )(x, weights, gate_lin, up_lin)
+
+
+def d_normed_kernel(a_ref, b_ref, wa_ref, wb_ref, out_ref):
+    total = dot_nt(a_ref[...], wa_ref[...]) + dot_nt(b_ref[...], wb_ref[...])
+    out_ref[...] = total.astype(out_ref.dtype)
+
+
+def d_normed_of(d_gate, d_up, weights):
+    rows, units = d_gate.shape
+    width = weights.shape[0]
+    whole = spec((rows, units), lambda j: (0, 0))
+    return call(
+        d_normed_kernel,
+        width // TILE,
+        [
+            whole,
+            whole,
+            spec((TILE, units), lambda j: (j, 0)),
+            spec((TILE, units), lambda j: (j, 1)),
+        ],
+        spec((rows, TILE), lambda j: (0, j)),
+        jax.ShapeDtypeStruct((rows, width), BF16),
+        4 * rows * width * units,
+        4 * width * units,
+        "d_normed",
+    )(d_gate, d_up, weights, weights)
+
+
+def outer_kernel(a_ref, b_ref, out_ref):
+    out_ref[...] = dot_tn(a_ref[...], b_ref[...]).astype(out_ref.dtype)
+
+
+def outer(left, right, name):
+    rows, width = left.shape
+    units = right.shape[1]
+    return call(
+        outer_kernel,
+        width // TILE,
+        [spec((rows, TILE), lambda j: (0, j)), spec((rows, units), lambda j: (0, 0))],
+        spec((TILE, units), lambda j: (j, 0)),
+        jax.ShapeDtypeStruct((width, units), BF16),
+        2 * rows * width * units,
+        2 * width * units,
+        name,
+    )(left, right)
+
+
+def outer_pair_kernel(a_ref, b_ref, c_ref, *rest):
+    out_ref = rest[-1]
+    units = b_ref.shape[1]
+    out_ref[:, :units] = dot_tn(a_ref[...], b_ref[...]).astype(out_ref.dtype)
+    out_ref[:, units:] = dot_tn(a_ref[...], c_ref[...]).astype(out_ref.dtype)
+
+
+def outer_pair(left, right, other, begun, name):
+    rows, width = left.shape
+    units = right.shape[1]
+    whole = spec((rows, units), lambda j: (0, 0))
+    tiles = width // TILE
+    most = tiles - tiles // 2
+    start, grid = (0, most) if begun is None else (most, tiles - most)
+    more = [] if begun is None else [begun]
+    return pl.pallas_call(
+        outer_pair_kernel,
+        grid=(grid,),
+        in_specs=[spec((rows, TILE), lambda j: (0, j + start)), whole, whole]
+        + [pl.BlockSpec(memory_space=pl.ANY)] * len(more),
+        out_specs=spec((TILE, 2 * units), lambda j: (j + start, 0)),
+        out_shape=jax.ShapeDtypeStruct((width, 2 * units), BF16),
+        input_output_aliases={3: 0} if more else {},
+        compiler_params=pltpu.CompilerParams(
+            dimension_semantics=("arbitrary",), vmem_limit_bytes=44 << 20
+        ),
+        cost_estimate=pl.CostEstimate(
+            flops=4 * rows * grid * TILE * units,
+            bytes_accessed=4 * grid * TILE * units,
+            transcendentals=0,
+        ),
+        name=name,
+    )(left, right, other, *more)
+
+
+def outer_two_kernel(a_ref, b_ref, c_ref, d_ref, more_ref, out_ref):
+    units = b_ref.shape[1]
+    both = units + d_ref.shape[1]
+    out_ref[:, :units] = dot_tn(a_ref[...], b_ref[...]).astype(out_ref.dtype)
+    out_ref[:, units:both] = dot_tn(c_ref[...], d_ref[...]).astype(out_ref.dtype)
+    out_ref[:, both:] = more_ref[...].astype(out_ref.dtype)
+
+
+def outer_two(left, right, left_b, right_b, extra, name):
+    rows, width = left.shape
+    units, more = right.shape[1], right_b.shape[1]
+    side = spec((rows, TILE), lambda j: (0, j))
+    return call(
+        outer_two_kernel,
+        width // TILE,
+        [
+            side,
+            spec((rows, units), lambda j: (0, 0)),
+            side,
+            spec((rows, more), lambda j: (0, 0)),
+            spec((TILE, extra.shape[1]), lambda j: (j, 0)),
+        ],
+        spec((TILE, units + more + extra.shape[1]), lambda j: (j, 0)),
+        jax.ShapeDtypeStruct((width, units + more + extra.shape[1]), BF16),
+        2 * rows * width * (units + more),
+        2 * width * (units + more),
+        name,
+    )(left, right, left_b, right_b, extra)
 
 
 def stack_heads(ref, rows, first, count):
@@ -218,7 +488,7 @@
         in_specs=[pl.BlockSpec(memory_space=pltpu.SMEM)] + [vmem()] * 4,
         out_specs=(vmem(), vmem()),
         scratch_shapes=[pltpu.VMEM((blocks, heads * BLOCK, BLOCK), F32)],
-        compiler_params=pltpu.CompilerParams(vmem_limit_bytes=(24 if blocks <= 8 else 48) << 20),
+        compiler_params=pltpu.CompilerParams(vmem_limit_bytes=(16 if blocks <= 8 else 48) << 20),
         cost_estimate=pl.CostEstimate(
             flops=3 * heads * BLOCK * blocks * BLOCK * HEAD_DIM,
             bytes_accessed=4 << 20,
@@ -291,7 +561,7 @@
         in_specs=[pl.BlockSpec(memory_space=pltpu.SMEM)] + [vmem()] * 6,
         out_specs=(vmem(), vmem()),
         scratch_shapes=[pltpu.VMEM(tile, BF16), pltpu.VMEM(tile, F32), pltpu.VMEM(tile, F32)],
-        compiler_params=pltpu.CompilerParams(vmem_limit_bytes=(32 if blocks <= 8 else 56) << 20),
+        compiler_params=pltpu.CompilerParams(vmem_limit_bytes=(26 if blocks <= 8 else 56) << 20),
         cost_estimate=pl.CostEstimate(
             flops=11 * heads * BLOCK * blocks * BLOCK * HEAD_DIM,
             bytes_accessed=10 << 20,
@@ -331,15 +601,21 @@
     heads = q_weight.shape[1] // HEAD_DIM
     qcols = q_weight.shape[1]
 
-    qkv_w = gather(wide, jnp.concatenate([q_weight, key_weight, value_weight], axis=1))
-    out_w = gather(wide, out_weight.T)
+    split = ("fsdp", "ctx")
     gains_own = jnp.stack([gain_attn_in, gain_attn_out, gain_mlp_in, gain_mlp_out])
-    gains = gather(wide, gains_own[None]).astype(F32)
-    gains = gains.transpose(1, 0, 2).reshape(4, width)
+    gains_own = jnp.pad(gains_own, ((0, 124), (0, 0))).T
+    attn_own = jnp.concatenate(
+        [q_weight, key_weight, value_weight, out_weight.T, gains_own], axis=1
+    )
+    attn_w = lax.all_gather(attn_own, split, axis=0, tiled=True)
+    gu_own = jnp.concatenate([gate_weight, after(up_weight, attn_own)], axis=1)
+    gu_w = lax.all_gather(after(gu_own, attn_w), split, axis=0, tiled=True)
+    down_own = after(down_weight, gu_own).T
+    lin_cols = qcols + 2 * HEAD_DIM
+    out_cols = lin_cols + out_weight.shape[0]
+    qkv_w, out_w = attn_w[:, :lin_cols], attn_w[:, lin_cols:out_cols]
+    gains = attn_w[:, out_cols:].T.astype(F32)
     gain_one, gain_two, gain_three, gain_four = (gains[i] for i in range(4))
-    gate_w = gather(wide, gate_weight)
-    up_w = gather(wide, up_weight)
-    down_w = gather(wide, down_weight.T)
 
     order = block_order[0]
     blocks = order.shape[0]
@@ -370,7 +646,20 @@
     queries = queries.reshape(count, qcols)
     keys = rotate(lin[:, qcols : qcols + HEAD_DIM], cosine, sine).astype(BF16)
     values = lin[:, qcols + HEAD_DIM :].astype(BF16)
-    kv = gather(near, jnp.concatenate([keys, values], axis=1))
+    kv_own = jnp.concatenate([keys, values], axis=1)
+    kv_move = begun(gather_steps(near, kv_own))
+    for _ in range(near.count - 1):
+        kv = step(kv_move, queries, qseg, *infos)
+    down_move = gather_steps(wide, after(down_own, attn_w))
+    passing = next(down_move)
+    down_left = wide.count - 1
+
+    def pass_down(*waits):
+        nonlocal passing, down_left
+        if down_left:
+            passing, down_left = step(down_move, *waits), down_left - 1
+
+    pass_down(kv)
 
     def rows_of(array, i):
         return lax.slice_in_dim(array, i * BLOCK, (i + 1) * BLOCK)
@@ -378,92 +667,175 @@
     def share_of(array, i):
         return lax.dynamic_slice_in_dim(array, i * BLOCK + here * share, share).astype(F32)
 
-    attended, inverse_sum, branch_attn, inv_two, resid, inv_three, normed_mlp = ([] for _ in range(7))
-    for i in range(halves):
+    def joined(pieces):
+        return jnp.concatenate(pieces, axis=0)
+
+    hops = tp - 1
+    both = range(halves)
+
+    def all_steps(parts):
+        for _ in range(hops):
+            last = [step(part) for part in parts]
+        return last
+
+    attended, inverse_sum, sums = [], [], []
+    for i in both:
         out, inv = attend(infos[i], rows_of(queries, i), kv, rows_of(qseg, i), segs, heads)
         attended.append(out)
         inverse_sum.append(inv)
-        branch = tp_scatter(dot_nt(out, out_w), tp)
-        branch_attn.append(branch)
-        inv_two.append(inverse_of(branch))
-        resid.append(share_of(tok, i) + branch * inv_two[i] * gain_two)
-        inv_three.append(inverse_of(resid[i]))
-        normed_mlp.append(tp_gather((resid[i] * inv_three[i] * gain_three).astype(BF16), tp))
-
-    gate_lin, up_lin, activ, layer_out, d_mlp_low, grad_four = ([] for _ in range(6))
-    for i in range(halves):
-        gate_lin.append(dot(normed_mlp[i], gate_w))
-        up_lin.append(dot(normed_mlp[i], up_w))
-        activ.append((gelu(gate_lin[i]) * up_lin[i]).astype(BF16))
-        branch = tp_scatter(dot_nt(activ[i], down_w), tp)
+        sums.append(tp_scatter(dot_nt(out, out_w).astype(BF16), tp))
+        next(sums[i])
+    for n in range(hops):
+        branch_attn = [step(part) for part in sums]
+        if n == 1:
+            pass_down(*branch_attn)
+    inv_two = [inverse_of(branch) for branch in branch_attn]
+    resid = [share_of(tok, i) + branch_attn[i] * inv_two[i] * gain_two for i in both]
+    inv_three = [inverse_of(value) for value in resid]
+    moves = [tp_gather((resid[i] * inv_three[i] * gain_three).astype(BF16), tp) for i in both]
+    for move in moves:
+        next(move)
+    for n in range(hops - 1):
+        sent = [step(move) for move in moves]
+        if n == 0:
+            pass_down(*sent)
+    first = step(moves[0])
+    while down_left:
+        pass_down()
+    down_w = passing
+
+    gate_lin, up_lin, activ = [None] * halves, [None] * halves, [None] * halves
+    gate_lin[0], up_lin[0], activ[0] = gate_up(after(first, sent[-1]), gu_w)
+    normed_mlp = [first] + [step(move, activ[0]) for move in moves[1:]]
+    sums = [tp_scatter(down(activ[0], down_w), tp)]
+    sent = next(sums[0])
+    gate_lin[1], up_lin[1], activ[1] = gate_up(after(normed_mlp[1], sent), gu_w)
+    sent = step(sums[0], activ[1])
+    part = down(after(activ[1], sent), down_w)
+    sums.append(tp_scatter(part, tp))
+    next(sums[1])
+    sent = step(sums[0], part)
+
+    layer_own, grad_four, moves = [], [], []
+
+    def middle(i, branch):
         inv = inverse_of(branch)
-        layer_out.append(tp_gather((resid[i] + branch * inv * gain_four).astype(BF16), tp))
+        layer_own.append((resid[i] + branch * inv * gain_four).astype(BF16))
         d_branch, d_gain = norm_back(branch, inv, gain_four, share_of(cotangent[0], i))
         grad_four.append(d_gain)
-        d_mlp_low.append(tp_gather(d_branch.astype(BF16), tp))
-
-    d_gate, d_up, d_resid, d_attn_low, grad_three, grad_two, d_attended = ([] for _ in range(7))
-    for i in range(halves):
-        d_activ = dot(d_mlp_low[i], down_w)
-        bent, slope = gelu_and_slope(gate_lin[i])
-        d_gate.append((d_activ * up_lin[i] * slope).astype(BF16))
-        d_up.append((d_activ * bent).astype(BF16))
-        d_normed = tp_scatter(dot_nt(d_gate[i], gate_w) + dot_nt(d_up[i], up_w), tp)
-        d_in, d_gain = norm_back(resid[i], inv_three[i], gain_three, d_normed)
+        moves.append(tp_gather(d_branch.astype(BF16), tp))
+        return next(moves[i])
+
+    step(sums[1])
+    middle(0, step(sums[0]))
+    step(sums[1])
+    step(moves[0])
+    middle(1, step(sums[1]))
+    step(moves[0])
+    step(moves[1])
+    first = step(moves[0])
+    sent = step(moves[1])
+    layer_move = begun(tp_gather(after(jnp.stack(layer_own), first), tp))
+
+    d_gate, d_up = [None] * halves, [None] * halves
+    d_gate[0], d_up[0] = d_gate_up(after(first, sent), down_w, gate_lin[0], up_lin[0])
+    d_mlp_low = [first, step(moves[1], d_gate[0])]
+    grad_down = outer(joined(d_mlp_low), joined(activ), "grad_down")
+    sent_layer = step(layer_move, grad_down)
+    part = d_normed_of(after(d_gate[0], grad_down, sent_layer), d_up[0], gu_w)
+    sums = [tp_scatter(part, tp)]
+    sent = next(sums[0])
+    d_gate[1], d_up[1] = d_gate_up(after(d_mlp_low[1], sent), down_w, gate_lin[1], up_lin[1])
+    sent = step(sums[0], d_gate[1])
+    sent_layer = step(layer_move, sent)
+    part = d_normed_of(after(d_gate[1], sent, sent_layer), d_up[1], gu_w)
+    sums.append(tp_scatter(part, tp))
+    next(sums[1])
+    d_resid, grad_three, grad_two, moves = [], [], [], []
+
+    def middle_back(i, part):
+        d_in, d_gain = norm_back(resid[i], inv_three[i], gain_three, part)
         grad_three.append(d_gain)
         d_resid.append(share_of(cotangent[0], i) + d_in)
         d_branch, d_gain = norm_back(branch_attn[i], inv_two[i], gain_two, d_resid[i])
         grad_two.append(d_gain)
-        d_attn_low.append(tp_gather(d_branch.astype(BF16), tp))
-        d_attended.append(dot(d_attn_low[i], out_w).astype(BF16))
-
-    def joined(pieces):
-        return jnp.concatenate(pieces, axis=0)
-
+        moves.append(tp_gather(d_branch.astype(BF16), tp))
+        return next(moves[i])
+
+    step(sums[0], part)
+    sent = middle_back(0, step(sums[0]))
+    layer_out = step(layer_move, part)
     normed_all = joined(normed_mlp)
-    grad_down = scatter(wide, dot_tn(joined(d_mlp_low), joined(activ)).astype(BF16), BF16)
-    grad_gate = scatter(wide, dot_tn(normed_all, joined(d_gate)).astype(BF16), BF16)
-    grad_up = scatter(wide, dot_tn(normed_all, joined(d_up)).astype(BF16), BF16)
-    grad_out = scatter(wide, dot_tn(joined(d_attn_low), joined(attended)).astype(BF16), BF16)
-
+    d_pair = joined(d_gate), joined(d_up)
+    grad_gu = outer_pair(after(normed_all, sent, layer_out), *d_pair, None, "grad_gate_up")
+    mark = grad_gu[:8, :128]
+    sent = step(sums[1], mark), step(moves[0], mark)
+    grad_gu = outer_pair(after(normed_all, *sent), *d_pair, grad_gu, "grad_gate_up_more")
+    mark = grad_gu[-8:, :128]
+    step(sums[1], mark), step(moves[0], mark)
+    grad_down = lax.psum_scatter(grad_down, split, scatter_dimension=0, tiled=True)
+    sent = middle_back(1, step(sums[1]))
+    grad_gu = held(grad_gu, grad_down, sent)
+    grad_gu = lax.psum_scatter(grad_gu, split, scatter_dimension=0, tiled=True)
+    grad_down = grad_down.astype(F32)
+    first = step(moves[0])
+    d_attn_low = [first, finish(moves[1], hops)]
+
+    d_attn_all = joined(d_attn_low)
+    d_attended = dot(d_attn_all, out_w).astype(BF16)
     d_queries, d_kv = attend_back(
-        info_all, queries, joined(d_attended), kv, joined(inverse_sum), qseg, segs, heads
+        info_all, queries, d_attended, kv, joined(inverse_sum), qseg, segs, heads
     )
-    d_kv = scatter(near, d_kv, BF16)
     d_q_lin = rotate(
         d_queries.reshape(count, heads, HEAD_DIM) * scale, cosine[:, None], -sine[:, None]
     ).astype(BF16)
+    d_q_lin = d_q_lin.reshape(count, qcols)
+    from_q = dot_nt(d_q_lin, qkv_w[:, :qcols])
+    d_kv = scatter(near, d_kv, BF16)
     d_key_lin = rotate(d_kv[:, :HEAD_DIM], cosine, -sine).astype(BF16)
-    d_lin = jnp.concatenate(
-        [d_q_lin.reshape(count, qcols), d_key_lin, d_kv[:, HEAD_DIM:].astype(BF16)], axis=1
+    d_kv_lin = jnp.concatenate([d_key_lin, d_kv[:, HEAD_DIM:].astype(BF16)], axis=1)
+    d_normed_attn = from_q + dot_nt(d_kv_lin, qkv_w[:, qcols:])
+    d_normed_low = d_normed_attn.astype(BF16)
+    sums = [tp_scatter(rows_of(d_normed_low, i), tp) for i in both]
+    sent = [next(part) for part in sums]
+    grad_one = jnp.sum(after(d_normed_attn, *sent) * inputs * inv_one, axis=0)
+    grad_gains = jnp.stack([grad_one, sum(grad_two), sum(grad_three), sum(grad_four)])
+    grad_gains = jnp.pad(grad_gains, ((0, 124), (0, 0))).T
+    d_lin = jnp.concatenate([d_q_lin, d_kv_lin], axis=1)
+    grad_attn = outer_two(
+        normed_attn, d_lin, d_attn_all, joined(attended), grad_gains, "grad_attn"
     )
-    d_normed_attn = dot_nt(d_lin, qkv_w)
-    grad_qkv = scatter(wide, dot_tn(normed_attn, d_lin).astype(BF16), BF16)
-    grad_one = jnp.sum(d_normed_attn * inputs * inv_one, axis=0)
-    grad_tokens = []
-    for i in range(halves):
-        d_normed = tp_scatter(rows_of(d_normed_attn, i), tp)
+    for _ in range(hops):
+        sent = [step(part) for part in sums]
+    moves = []
+    for i in both:
         own = share_of(tok, i)
-        d_in, unused = norm_back(own, inverse_of(own), gain_one, d_normed)
-        grad_tokens.append(tp_gather((d_resid[i] + d_in).astype(BF16), tp))
-
-    grad_gains = jnp.stack([grad_one, sum(grad_two), sum(grad_three), sum(grad_four)])
-    grad_gains = grad_gains.reshape(4, group, width // group).transpose(1, 0, 2)
-    grad_gains = scatter(wide, grad_gains, F32)[0]
-    travelling = grad_gains
-    for step in range(1, tp):
-        travelling = lax.ppermute(travelling, "tp", tp_pairs(tp))
-        grad_gains = grad_gains + travelling
+        d_in, unused = norm_back(own, inverse_of(own), gain_one, sent[i])
+        moves.append(begun(tp_gather((d_resid[i] + d_in).astype(BF16), tp, F32)))
+        sent[i] = step(moves[i])
+    grad_attn = held(grad_attn, grad_gu, *sent)
+    grad_gu = grad_gu.astype(F32)
+    grad_attn = lax.psum_scatter(grad_attn, split, scatter_dimension=0, tiled=True).astype(F32)
+    for _ in range(hops - 1):
+        grad_tokens = [step(move) for move in moves]
+    grad_gains = grad_attn[:, out_cols:]
+    bit = 1
+    while bit < tp:
+        swap = [(i, i ^ bit) for i in range(tp)]
+        grad_gains = grad_gains + lax.ppermute(grad_gains, "tp", swap)
+        bit *= 2
+    grad_qkv, grad_out = grad_attn[:, :lin_cols], grad_attn[:, lin_cols:out_cols]
+    grad_gains = grad_gains.T
 
     return (
-        joined(layer_out)[None],
-        joined(grad_tokens).astype(F32)[None],
+        layer_out.reshape(1, count, width),
+        joined(grad_tokens)[None],
         grad_qkv[:, :qcols],
         grad_qkv[:, qcols : qcols + HEAD_DIM],
         grad_qkv[:, qcols + HEAD_DIM :],
         grad_out.T,
-        grad_gate,
-        grad_up,
+        grad_gu[:, : gate_weight.shape[1]],
+        grad_gu[:, gate_weight.shape[1] :],
         grad_down.T,
         grad_gains[0],
         grad_gains[1],

time: 941 us -> 731 us (0.78)
  matrix products: 132 us -> 17.3 us
  Pallas kernels: 17.1 us -> 120 us
  waiting for transfers between devices: 491 us -> 409 us
  local copies, waits for them, and re-layouts: 129 us -> 85.1 us
  starting transfers between devices: 66 us -> 23 us
  other arithmetic: 82.1 us -> 41.6 us
  between operations: 14 us -> 27.3 us
    ppermute x65 -> x31, waiting for transfers between devices: 326 us -> 174 us  [the longest x24 120 us: tp_scatter(): got = lax.ppermute(total, 'tp', tp_pairs(count))]
    pallas_call x0 -> x14, Pallas kernels: none -> 102 us  [the longest x2 21.4 us: d_normed_of(): call(d_normed_kernel, width // TILE, [whole, whole, spec((TILE, units), l...]
    all_gather x0 -> x2, waiting for transfers between devices: none -> 51.2 us  [the longest x1 51.2 us: per_device(): attn_w = lax.all_gather(attn_own, split, axis=0, tiled=True)]
    dynamic_update_slice x80 -> x11, local copies, waits for them, and re-layouts: 61 us -> 16 us  [put(): return lax.dynamic_update_slice(buffer, piece, starts)]
    dot_general x9 -> x4, matrix products: 52.5 us -> 8 us  [dot_nt(): lax.dot_general(left, right, (((1,), (1,)), ((), ())), preferred_element_...]
    dot_general x9 -> x2, matrix products: 46.3 us -> 9.25 us  [dot(): return jnp.dot(left, right, preferred_element_type=F32)]
    dot_general x5 -> x0, matrix products: 33.3 us -> none  [dot_tn(): lax.dot_general(left, right, (((0,), (0,)), ((), ())), preferred_element_...]
    convert_element_type x33 -> x20, other arithmetic: 38.3 us -> 7.16 us  [the longest x16 3.1 us: tp_scatter(): total = total.astype(BF16)]
  transfers between devices with their start and end apart: 147 -> 71, of which waited for: 77 -> 51; matrix products, arithmetic and copies ran while one was open for 33% -> 16% of each run, Pallas kernels for 2% -> 14%
where the time goes in v2:
time: 731 us; the launch traced here: 723 us
  waiting for transfers between devices  409 us (56%)
  Pallas kernels  120 us (16%)
  local copies, waits for them, and re-layouts  85.1 us (12%)
  other arithmetic  41.6 us (6%)
  between operations  27.3 us (4%)
  starting transfers between devices  23 us (3%)
  matrix products  17.3 us (2%)
    ppermute x27, waiting for transfers between devices, tp_gather(): piece = lax.ppermute(piece, 'tp', tp_pairs(count))  154 us
    ppermute x24, waiting for transfers between devices, tp_scatter(): got = lax.ppermute(total, 'tp', tp_pairs(count))  120 us
    all_gather x1, waiting for transfers between devices, per_device(): attn_w = lax.all_gather(attn_own, split, axis=0, tiled=True)  51.2 us
    reduce_scatter x1, waiting for transfers between devices, per_device(): lax.psum_scatter(grad_attn, split, scatter_dimension=0, tiled=True)  28.9 us
    ppermute x4, waiting for transfers between devices, gather_steps(): piece = lax.ppermute(piece, ring.axes, ring.pairs(-1))  25.4 us
    unnamed x232, local copies, waits for them, and re-layouts  24.9 us
    ppermute x1, waiting for transfers between devices, scatter_steps(): got = lax.ppermute(total, ring.axes, ring.pairs(1))  22.5 us
    pallas_call x2, Pallas kernels, d_normed_of(): call(d_normed_kernel, width // TILE, [whole, whole, spec((TILE, units), l...  21.4 us
  transfers between devices with their start and end apart: 71, of which 51 were waited for; matrix products, arithmetic and copies ran while one was open for 16% of the time, Pallas kernels for 14%

profile of v2, /device:TPU:0, one launch (start us, length us, event | category | flops | bytes accessed | tf_op | source)
XLA Modules:
  0.0 723.0 jit_solution(5160159382516661704)
XLA Ops:
  18.0 51.2 %all-gather.3.cloned.1.call-done = bf16[2304,1664]{1,0:T(8,128)(2,1)} async-done(((bf16[288,1664]{1,0:T(8,128)(2,1)}), bf16[2304,1664]{1,0:T(8,128)(2,1)}) %all-gather.3.cloned.1.call-update) | async-done | bytes 7667728 | tf_op jit(solution)/shard_map/all_gather | solution.py:610
  108.6 15.8 %collective-permute-done.1 = bf16[512,512]{1,0:T(8,128)(2,1)} collective-permute-done((bf16[512,512]{1,0:T(8,128)(2,1)S(1)}, bf16[512,512]{1,0:T(8,128)(2,1)}, u32[]{:S(2)}, u32[]{:S(2)}) %collective-permute-start.1) | collective-permute-done | bytes 524320 | tf_op jit(solution)/shard_map/ppermute | solution.py:73
  157.0 8.3 %collective-permute-done.10 = bf16[64,2304]{1,0:T(8,128)(2,1)S(1)} collective-permute-done((bf16[64,2304]{1,0:T(8,128)(2,1)S(1)}, bf16[64,2304]{1,0:T(8,128)(2,1)S(1)}, u32[]{:S(2)}, u32[]{:S(2)}) %collective-permute-start.10) | collective-permute-done | bytes 294944 | tf_op jit(solution)/shard_map/ppermute | solution.py:125
  228.5 10.5 %gate_up.2 = (f32[256,2304]{1,0:T(8,128)S(1)}, f32[256,2304]{1,0:T(8,128)S(1)}, bf16[256,2304]{1,0:T(8,128)(2,1)S(1)}) custom-call(bf16[256,2304]{1,0:T(8,128)(2,1)S(1)} %constant_dynamic-update-slice_fusion.32.x_ref, bf16[2304,4608]{1,0:T(8,128)(2,1)} %all-gather.5.cloned.1.call-done.gate_ref.up_ref.wa_ref.wb_ref, ...), custom_call_target="tpu_custom_call" | custom-call | flops 5435817984 | bytes 28311552 | tf_op jit(solution)/shard_map/gate_up/pallas_call | solution.py:268
  248.8 10.5 %gate_up.3 = (f32[256,2304]{1,0:T(8,128)S(1)}, f32[256,2304]{1,0:T(8,128)S(1)}, bf16[256,2304]{1,0:T(8,128)(2,1)S(1)}) custom-call(bf16[256,2304]{1,0:T(8,128)(2,1)S(1)} %get-tuple-element.207, bf16[2304,4608]{1,0:T(8,128)(2,1)} %all-gather.5.cloned.1.call-done.gate_ref.up_ref.wa_ref.wb_ref, ...), custom_call_target="tpu_custom_call" | custom-call | flops 5435817984 | bytes 28311552 | tf_op jit(solution)/shard_map/gate_up/pallas_call | solution.py:268
  271.0 8.7 %collective-permute-done.25 = bf16[64,2304]{1,0:T(8,128)(2,1)S(1)} collective-permute-done((bf16[64,2304]{1,0:T(8,128)(2,1)S(1)}, bf16[64,2304]{1,0:T(8,128)(2,1)S(1)}, u32[]{:S(2)}, u32[]{:S(2)}) %collective-permute-start.25) | collective-permute-done | bytes 294944 | tf_op jit(solution)/shard_map/ppermute | solution.py:125
  308.5 10.1 %collective-permute-done.32 = bf16[64,2304]{1,0:T(8,128)(2,1)S(1)} collective-permute-done((bf16[64,2304]{1,0:T(8,128)(2,1)S(1)}, bf16[64,2304]{1,0:T(8,128)(2,1)S(1)}, u32[]{:S(2)}, u32[]{:S(2)}) %collective-permute-start.32) | collective-permute-done | bytes 294944 | tf_op jit(solution)/shard_map/ppermute | solution.py:147
  324.9 11.0 %collective-permute-done.29 = bf16[64,2304]{1,0:T(8,128)(2,1)S(1)} collective-permute-done((bf16[64,2304]{1,0:T(8,128)(2,1)S(1)}, bf16[64,2304]{1,0:T(8,128)(2,1)S(1)}, u32[]{:S(2)}, u32[]{:S(2)}) %collective-permute-start.29) | collective-permute-done | bytes 294944 | tf_op jit(solution)/shard_map/ppermute | solution.py:147
  336.0 11.6 %collective-permute-done.30 = bf16[64,2304]{1,0:T(8,128)(2,1)S(1)} collective-permute-done((bf16[64,2304]{1,0:T(8,128)(2,1)S(1)}, bf16[64,2304]{1,0:T(8,128)(2,1)S(1)}, u32[]{:S(2)}, u32[]{:S(2)}) %collective-permute-start.30) | collective-permute-done | bytes 294944 | tf_op jit(solution)/shard_map/ppermute | solution.py:147
  355.8 8.1 %grad_down.1 = bf16[2304,2304]{1,0:T(8,128)(2,1)} custom-call(bf16[512,2304]{1,0:T(8,128)(2,1)S(1)} %pad_maximum_fusion.a_ref, bf16[512,2304]{1,0:T(8,128)(2,1)S(1)} %pad_maximum_fusion.1.b_ref), custom_call_target="tpu_custom_call" | custom-call | flops 5435817984 | bytes 10616832 | tf_op jit(solution)/shard_map/grad_down/pallas_call | solution.py:364
  367.2 10.1 %collective-permute-done.31 = bf16[2,64,2304]{2,1,0:T(8,128)(2,1)S(1)} collective-permute-done((bf16[2,64,2304]{2,1,0:T(8,128)(2,1)S(1)}, bf16[2,64,2304]{2,1,0:T(8,128)(2,1)S(1)}, u32[]{:S(2)}, u32[]{:S(2)}) %collective-permute-start.31) | collective-permute-done | bytes 589856 | tf_op jit(solution)/shard_map/ppermute | solution.py:147
  377.2 11.0 %d_normed.2 = bf16[256,2304]{1,0:T(8,128)(2,1)S(1)} custom-call(bf16[256,2304]{1,0:T(8,128)(2,1)S(1)} %copy-done.3, bf16[256,2304]{1,0:T(8,128)(2,1)S(1)} %copy-done.5, bf16[2304,4608]{1,0:T(8,128)(2,1)} %all-gather.5.cloned.1.call-done.gate_ref.up_ref.wa_ref.wb_ref, bf16[2304,4608]{1,0:T(8,128)(2,1)} %all-gather.5.cloned.1.call-done.gate_ref.up_ref.wa_ref.wb_ref), custom_call_target="tpu_custom_call" | custom-call | flops 5435817984 | bytes 21233664 | tf_op jit(solution)/shard_map/d_normed/pallas_call | solution.py:340
  400.2 12.6 %collective-permute-done.35 = bf16[2,64,2304]{2,1,0:T(8,128)(2,1)} collective-permute-done((bf16[2,64,2304]{2,1,0:T(8,128)(2,1)S(1)}, bf16[2,64,2304]{2,1,0:T(8,128)(2,1)}, u32[]{:S(2)}, u32[]{:S(2)}) %collective-permute-start.35) | collective-permute-done | bytes 589856 | tf_op jit(solution)/shard_map/ppermute | solution.py:147
  412.8 10.3 %d_normed.3 = bf16[256,2304]{1,0:T(8,128)(2,1)S(1)} custom-call(bf16[256,2304]{1,0:T(8,128)(2,1)S(1)} %get-tuple-element.96.a_ref, bf16[256,2304]{1,0:T(8,128)(2,1)S(1)} %get-tuple-element.97.b_ref, bf16[2304,4608]{1,0:T(8,128)(2,1)} %all-gather.5.cloned.1.call-done.gate_ref.up_ref.wa_ref.wb_ref, ...), custom_call_target="tpu_custom_call" | custom-call | flops 5435817984 | bytes 21233664 | tf_op jit(solution)/shard_map/d_normed/pallas_call | solution.py:340
  425.6 12.0 %collective-permute-done.39 = bf16[64,2304]{1,0:T(8,128)(2,1)S(1)} collective-permute-done((bf16[64,2304]{1,0:T(8,128)(2,1)S(1)}, bf16[64,2304]{1,0:T(8,128)(2,1)S(1)}, u32[]{:S(2)}, u32[]{:S(2)}) %collective-permute-start.39) | collective-permute-done | bytes 294944 | tf_op jit(solution)/shard_map/ppermute | solution.py:125
  440.8 10.8 %grad_gate_up.1.rest_0_ = bf16[2304,4608]{1,0:T(8,128)(2,1)} custom-call(bf16[512,2304]{1,0:T(8,128)(2,1)S(1)} %pad_maximum_fusion.2.a_ref, bf16[512,2304]{1,0:T(8,128)(2,1)S(1)} %constant_dynamic-update-slice_fusion.46.b_ref, bf16[512,2304]{1,0:T(8,128)(2,1)S(1)} %constant_dynamic-update-slice_fusion.48.c_ref), custom_call_target="tpu_custom_call" | custom-call | flops 7247757312 | bytes 14155776 | tf_op jit(solution)/shard_map/grad_gate_up/pallas_call | solution.py:391
  462.3 8.5 %collective-permute-done.45 = bf16[64,2304]{1,0:T(8,128)(2,1)S(1)} collective-permute-done((bf16[64,2304]{1,0:T(8,128)(2,1)S(1)}, bf16[64,2304]{1,0:T(8,128)(2,1)S(1)}, u32[]{:S(2)}, u32[]{:S(2)}) %collective-permute-start.45) | collective-permute-done | bytes 294944 | tf_op jit(solution)/shard_map/ppermute | solution.py:125
  477.2 10.6 %collective-permute-done.41 = bf16[64,2304]{1,0:T(8,128)(2,1)S(1)} collective-permute-done((bf16[64,2304]{1,0:T(8,128)(2,1)S(1)}, bf16[64,2304]{1,0:T(8,128)(2,1)S(1)}, u32[]{:S(2)}, u32[]{:S(2)}) %collective-permute-start.41) | collective-permute-done | bytes 294944 | tf_op jit(solution)/shard_map/ppermute | solution.py:147
  488.5 9.7 %collective-permute-done.43 = bf16[64,2304]{1,0:T(8,128)(2,1)S(1)} collective-permute-done((bf16[64,2304]{1,0:T(8,128)(2,1)S(1)}, bf16[64,2304]{1,0:T(8,128)(2,1)S(1)}, u32[]{:S(2)}, u32[]{:S(2)}) %collective-permute-start.43) | collective-permute-done | bytes 294944 | tf_op jit(solution)/shard_map/ppermute | solution.py:147
  502.0 7.8 %collective-permute-done.47 = bf16[64,2304]{1,0:T(8,128)(2,1)S(1)} collective-permute-done((bf16[64,2304]{1,0:T(8,128)(2,1)S(1)}, bf16[64,2304]{1,0:T(8,128)(2,1)S(1)}, u32[]{:S(2)}, u32[]{:S(2)}) %collective-permute-start.47) | collective-permute-done | bytes 294944 | tf_op jit(solution)/shard_map/ppermute | solution.py:147
  523.0 9.9 %attend_back.1 = (f32[512,512]{1,0:T(8,128)S(1)}, f32[2048,512]{1,0:T(8,128)S(1)}) custom-call(s32[12]{0:T(128)S(1)} %pad_add_fusion.3.info, bf16[512,512]{1,0:T(8,128)(2,1)S(1)} %bitcast.99, bf16[512,512]{1,0:T(8,128)(2,1)S(1)} %fusion.14.do_ref, bf16[2048,512]{1,0:T(8,128)(2,1)S(1)} %copy-done.13, f32[1024,1]{1,0:T(8,128)S(1)} %copy.60.inv_ref, ...), custom_call_target="tpu_custom_call" | custom-call | flops 2952790016 | bytes 10485760 | tf_op jit(solution)/shard_map/attend_back/pallas_call | solution.py:555
  540.4 22.5 %collective-permute-done.51 = bf16[512,512]{1,0:T(8,128)(2,1)} collective-permute-done((bf16[512,512]{1,0:T(8,128)(2,1)}, bf16[512,512]{1,0:T(8,128)(2,1)}, u32[]{:S(2)}, u32[]{:S(2)}) %collective-permute-start.51) | collective-permute-done | bytes 524320 | tf_op jit(solution)/shard_map/ppermute | solution.py:100
  635.1 10.7 %collective-permute-done.56 = bf16[64,2304]{1,0:T(8,128)(2,1)S(1)} collective-permute-done((bf16[64,2304]{1,0:T(8,128)(2,1)S(1)}, bf16[64,2304]{1,0:T(8,128)(2,1)S(1)}, u32[]{:S(2)}, u32[]{:S(2)}) %collective-permute-start.56) | collective-permute-done | bytes 294944 | tf_op jit(solution)/shard_map/ppermute | solution.py:147
  670.7 28.9 %reduce-scatter.8.cloned.1.call-done = bf16[288,1664]{1,0:T(8,128)(2,1)} async-done(((bf16[2304,1664]{1,0:T(8,128)(2,1)}), bf16[288,1664]{1,0:T(8,128)(2,1)}) %reduce-scatter.8.cloned.1.call-update) | async-done | bytes 958480 | tf_op jit(solution)/shard_map/reduce_scatter | solution.py:818
  (576 shorter events, 374.7 us)
Async XLA Ops:
  7.2 62.0 %all-gather.3.cloned.1.call-start = ((), (), s32[]{:S(2)}) async-start(), calls=%async_computation.3 | async-start | bytes 8626176 | tf_op jit(solution)/shard_map/all_gather | solution.py:610
  15.0 213.5 %all-gather.5.cloned.1.call-start = ((), (), s32[]{:S(2)}) async-start(), calls=%async_computation.4 | async-start | bytes 23887872 | tf_op jit(solution)/shard_map/all_gather | solution.py:612
  69.2 405.5 %reduce-scatter.4.cloned.1.call-start = ((), (), s32[]{:S(2)}) async-start(), calls=%async_computation.5 | async-start | bytes 11943936 | tf_op jit(solution)/shard_map/reduce_scatter | solution.py:776
  99.7 24.6 %collective-permute-start.1 = (bf16[512,512]{1,0:T(8,128)(2,1)S(1)}, bf16[512,512]{1,0:T(8,128)(2,1)}, u32[]{:S(2)}, u32[]{:S(2)}) collective-permute-start(bf16[512,512]{1,0:T(8,128)(2,1)S(1)} %get-tuple-element.185), channel_id=1, source_target_pairs={{0,8},{4,12},{8,0},{12,4},{1,9},{5,13},{9,1},{13,5},{2,10},{6,14},... | collective-permute-start | bytes 1572872 | tf_op jit(solution)/shard_map/ppermute | solution.py:73
  100.9 31.7 %collective-permute-start = (bf16[512,512]{1,0:T(8,128)(2,1)S(1)}, bf16[512,512]{1,0:T(8,128)(2,1)}, u32[]{:S(2)}, u32[]{:S(2)}) collective-permute-start(bf16[512,512]{1,0:T(8,128)(2,1)S(1)} %get-tuple-element.185), channel_id=1, source_target_pairs={{0,4},{4,0},{8,12},{12,8},{1,5},{5,1},{9,13},{13,9},{2,6},{6,2},{1... | collective-permute-start | bytes 1572872 | tf_op jit(solution)/shard_map/ppermute | solution.py:54
  100.9 52.3 %collective-permute-start.15 = (bf16[288,2304]{1,0:T(8,128)(2,1)}, bf16[288,2304]{1,0:T(8,128)(2,1)}, u32[]{:S(2)}, u32[]{:S(2)}) collective-permute-start(bf16[288,2304]{1,0:T(8,128)(2,1)} %bitcast.14), channel_id=1, source_target_pairs={{0,16},{4,12},{8,0},{12,28},{24,8},{28,20},{16,24},{20,4},{1,17},{... | collective-permute-start | bytes 3981320 | tf_op jit(solution)/shard_map/ppermute | solution.py:73
  101.8 69.9 %collective-permute-start.14 = (bf16[288,2304]{1,0:T(8,128)(2,1)}, bf16[288,2304]{1,0:T(8,128)(2,1)}, u32[]{:S(2)}, u32[]{:S(2)}) collective-permute-start(bf16[288,2304]{1,0:T(8,128)(2,1)} %bitcast.14), channel_id=1, source_target_pairs={{0,4},{4,0},{8,12},{12,8},{16,20},{20,16},{24,28},{28,24},{1,5},{5... | collective-permute-start | bytes 3981320 | tf_op jit(solution)/shard_map/ppermute | solution.py:54
  153.3 50.7 %collective-permute-start.17 = (bf16[288,2304]{1,0:T(8,128)(2,1)}, bf16[288,2304]{1,0:T(8,128)(2,1)S(1)}, u32[]{:S(2)}, u32[]{:S(2)}) collective-permute-start(bf16[288,2304]{1,0:T(8,128)(2,1)} %collective-permute-done.15), channel_id=1, source_target_pairs={{0,16},{4,12},{8,0},{12,28},{24,8},{28,20},{16,24},{20,4},{1,17},{... | collective-permute-start | bytes 3981320 | tf_op jit(solution)/shard_map/ppermute | solution.py:73
  153.3 64.5 %collective-permute-start.16 = (bf16[288,2304]{1,0:T(8,128)(2,1)}, bf16[288,2304]{1,0:T(8,128)(2,1)S(1)}, u32[]{:S(2)}, u32[]{:S(2)}) collective-permute-start(bf16[288,2304]{1,0:T(8,128)(2,1)} %collective-permute-done.15), channel_id=1, source_target_pairs={{0,4},{4,0},{8,12},{12,8},{16,20},{20,16},{24,28},{28,24},{1,5},{5... | collective-permute-start | bytes 3981320 | tf_op jit(solution)/shard_map/ppermute | solution.py:54
  186.3 17.6 %collective-permute-start.12 = (bf16[64,2304]{1,0:T(8,128)(2,1)S(1)}, bf16[64,2304]{1,0:T(8,128)(2,1)S(1)}, u32[]{:S(2)}, u32[]{:S(2)}) collective-permute-start(bf16[64,2304]{1,0:T(8,128)(2,1)S(1)} %get-tuple-element.158), channel_id=1, source_target_pairs={{0,1},{1,2},{2,3},{3,0},{4,5},{5,6},{6,7},{7,4},{8,9},{9,10},{10,1... | collective-permute-start | bytes 884744 | tf_op jit(solution)/shard_map/ppermute | solution.py:147
  203.9 19.8 %collective-permute-start.19 = (bf16[288,2304]{1,0:T(8,128)(2,1)S(1)}, bf16[288,2304]{1,0:T(8,128)(2,1)S(1)}, u32[]{:S(2)}, u32[]{:S(2)}) collective-permute-start(bf16[288,2304]{1,0:T(8,128)(2,1)S(1)} %collective-permute-done.17), channel_id=1, source_target_pairs={{0,16},{4,12},{8,0},{12,28},{24,8},{28,20},{16,24},{20,4},{1,17},{... | collective-permute-start | bytes 3981320 | tf_op jit(solution)/shard_map/ppermute | solution.py:73
  216.7 29.6 %collective-permute-start.22 = (bf16[64,2304]{1,0:T(8,128)(2,1)}, bf16[64,2304]{1,0:T(8,128)(2,1)}, u32[]{:S(2)}, u32[]{:S(2)}) collective-permute-start(bf16[64,2304]{1,0:T(8,128)(2,1)} %collective-permute-done.13), channel_id=1, source_target_pairs={{0,1},{1,2},{2,3},{3,0},{4,5},{5,6},{6,7},{7,4},{8,9},{9,10},{10,1... | collective-permute-start | bytes 884744 | tf_op jit(solution)/shard_map/ppermute | solution.py:147
  307.1 17.7 %collective-permute-start.28 = (bf16[64,2304]{1,0:T(8,128)(2,1)S(1)}, bf16[64,2304]{1,0:T(8,128)(2,1)S(1)}, u32[]{:S(2)}, u32[]{:S(2)}) collective-permute-start(bf16[64,2304]{1,0:T(8,128)(2,1)S(1)} %get-tuple-element.152), channel_id=1, source_target_pairs={{0,1},{1,2},{2,3},{3,0},{4,5},{5,6},{6,7},{7,4},{8,9},{9,10},{10,1... | collective-permute-start | bytes 884744 | tf_op jit(solution)/shard_map/ppermute | solution.py:147
  318.5 17.4 %collective-permute-start.33 = (bf16[64,2304]{1,0:T(8,128)(2,1)S(1)}, bf16[64,2304]{1,0:T(8,128)(2,1)S(1)}, u32[]{:S(2)}, u32[]{:S(2)}) collective-permute-start(bf16[64,2304]{1,0:T(8,128)(2,1)S(1)} %collective-permute-done.32), channel_id=1, source_target_pairs={{0,1},{1,2},{2,3},{3,0},{4,5},{5,6},{6,7},{7,4},{8,9},{9,10},{10,1... | collective-permute-start | bytes 884744 | tf_op jit(solution)/shard_map/ppermute | solution.py:147
  335.9 18.6 %collective-permute-start.34 = (bf16[64,2304]{1,0:T(8,128)(2,1)S(1)}, bf16[64,2304]{1,0:T(8,128)(2,1)S(1)}, u32[]{:S(2)}, u32[]{:S(2)}) collective-permute-start(bf16[64,2304]{1,0:T(8,128)(2,1)S(1)} %collective-permute-done.33), channel_id=1, source_target_pairs={{0,1},{1,2},{2,3},{3,0},{4,5},{5,6},{6,7},{7,4},{8,9},{9,10},{10,1... | collective-permute-start | bytes 884744 | tf_op jit(solution)/shard_map/ppermute | solution.py:147
  364.0 268.5 %reduce-scatter.6.cloned.1.call-start = ((), (), s32[]{:S(2)}) async-start(), calls=%async_computation.6 | async-start | bytes 23887872 | tf_op jit(solution)/shard_map/reduce_scatter | solution.py:779
  388.4 24.5 %collective-permute-start.35 = (bf16[2,64,2304]{2,1,0:T(8,128)(2,1)S(1)}, bf16[2,64,2304]{2,1,0:T(8,128)(2,1)}, u32[]{:S(2)}, u32[]{:S(2)}) collective-permute-start(bf16[2,64,2304]{2,1,0:T(8,128)(2,1)S(1)} %collective-permute-done.31), channel_id=1, source_target_pairs={{0,1},{1,2},{2,3},{3,0},{4,5},{5,6},{6,7},{7,4},{8,9},{9,10},{10,1... | collective-permute-start | bytes 1769480 | tf_op jit(solution)/shard_map/ppermute | solution.py:147
  400.2 23.1 %collective-permute-start.38 = (bf16[64,2304]{1,0:T(8,128)(2,1)S(1)}, bf16[64,2304]{1,0:T(8,128)(2,1)S(1)}, u32[]{:S(2)}, u32[]{:S(2)}) collective-permute-start(bf16[64,2304]{1,0:T(8,128)(2,1)S(1)} %add_convert_fusion.8), channel_id=1, source_target_pairs={{0,1},{1,2},{2,3},{3,0},{4,5},{5,6},{6,7},{7,4},{8,9},{9,10},{10,1... | collective-permute-start | bytes 884744 | tf_op jit(solution)/shard_map/ppermute | solution.py:125
  412.8 26.9 %collective-permute-start.37 = (bf16[2,64,2304]{2,1,0:T(8,128)(2,1)}, bf16[2,64,2304]{2,1,0:T(8,128)(2,1)S(1)}, u32[]{:S(2)}, u32[]{:S(2)}) collective-permute-start(bf16[2,64,2304]{2,1,0:T(8,128)(2,1)} %collective-permute-done.35), channel_id=1, source_target_pairs={{0,1},{1,2},{2,3},{3,0},{4,5},{5,6},{6,7},{7,4},{8,9},{9,10},{10,1... | collective-permute-start | bytes 1769480 | tf_op jit(solution)/shard_map/ppermute | solution.py:147
  423.5 28.1 %collective-permute-start.42 = (bf16[64,2304]{1,0:T(8,128)(2,1)S(1)}, bf16[64,2304]{1,0:T(8,128)(2,1)S(1)}, u32[]{:S(2)}, u32[]{:S(2)}) collective-permute-start(bf16[64,2304]{1,0:T(8,128)(2,1)S(1)} %constant_dynamic-slice_fusion.2), channel_id=1, source_target_pairs={{0,1},{1,2},{2,3},{3,0},{4,5},{5,6},{6,7},{7,4},{8,9},{9,10},{10,1... | collective-permute-start | bytes 884744 | tf_op jit(solution)/shard_map/ppermute | solution.py:125
  474.8 224.7 %reduce-scatter.8.cloned.1.call-start = ((), (), s32[]{:S(2)}) async-start(), calls=%async_computation.7 | async-start | bytes 8626176 | tf_op jit(solution)/shard_map/reduce_scatter | solution.py:818
  536.8 26.0 %collective-permute-start.51 = (bf16[512,512]{1,0:T(8,128)(2,1)}, bf16[512,512]{1,0:T(8,128)(2,1)}, u32[]{:S(2)}, u32[]{:S(2)}) collective-permute-start(bf16[512,512]{1,0:T(8,128)(2,1)} %add_convert_fusion), channel_id=1, source_target_pairs={{0,8},{4,12},{8,0},{12,4},{1,9},{5,13},{9,1},{13,5},{2,10},{6,14},... | collective-permute-start | bytes 1572872 | tf_op jit(solution)/shard_map/ppermute | solution.py:100
  575.3 17.6 %collective-permute-start.52 = (bf16[64,2304]{1,0:T(8,128)(2,1)}, bf16[64,2304]{1,0:T(8,128)(2,1)}, u32[]{:S(2)}, u32[]{:S(2)}) collective-permute-start(bf16[64,2304]{1,0:T(8,128)(2,1)} %constant_dynamic-slice_fusion.1), channel_id=1, source_target_pairs={{0,1},{1,2},{2,3},{3,0},{4,5},{5,6},{6,7},{7,4},{8,9},{9,10},{10,1... | collective-permute-start | bytes 884744 | tf_op jit(solution)/shard_map/ppermute | solution.py:125
  634.2 18.0 %collective-permute-start.62 = (bf16[64,2304]{1,0:T(8,128)(2,1)S(1)}, bf16[64,2304]{1,0:T(8,128)(2,1)S(1)}, u32[]{:S(2)}, u32[]{:S(2)}) collective-permute-start(bf16[64,2304]{1,0:T(8,128)(2,1)S(1)} %copy-done.70), channel_id=1, source_target_pairs={{0,1},{1,2},{2,3},{3,0},{4,5},{5,6},{6,7},{7,4},{8,9},{9,10},{10,1... | collective-permute-start | bytes 884744 | tf_op jit(solution)/shard_map/ppermute | solution.py:147
  (156 other events, 1928.5 us)
Sparse Core Ops, SparseCore 0:
  15.1 54.0 all-gather.2
  71.7 141.7 all-gather.4
  364.1 79.3 reduce-scatter.3
  475.0 146.0 reduce-scatter.5
  633.3 66.2 reduce-scatter.7

commit v3 on v2

--- a/solution.py
+++ b/solution.py
@@ -63,19 +63,66 @@
     return lax.dynamic_update_slice(buffer, piece, starts)
 
 
-def gather_steps(ring, shard):
+def blank_kernel(ref):
+    pass
+
+
+def blank(shape, kind):
+    return pl.pallas_call(
+        blank_kernel,
+        out_specs=pl.BlockSpec(memory_space=pl.ANY),
+        out_shape=jax.ShapeDtypeStruct(shape, kind),
+        compiler_params=pltpu.CompilerParams(has_side_effects=True),
+        name="blank",
+    )()
+
+
+def put_two_kernel(spots, whole_ref, one_ref, two_ref, out_ref, sems):
+    rows = one_ref.shape[0]
+    copies = []
+    for n, ref in enumerate((one_ref, two_ref)):
+        start = pl.multiple_of(spots[n] * rows, 16)
+        copies.append(pltpu.make_async_copy(ref, out_ref.at[pl.ds(start, rows)], sems.at[n]))
+    for copy in copies:
+        copy.start()
+    for copy in copies:
+        copy.wait()
+
+
+def put_two(whole, one, spot, two, other_spot):
+    if one.shape[0] % 16:
+        return put(put(whole, one, spot), two, other_spot)
+    anywhere = pl.BlockSpec(memory_space=pl.ANY)
+    return pl.pallas_call(
+        put_two_kernel,
+        in_specs=[pl.BlockSpec(memory_space=pltpu.SMEM), anywhere, vmem(), vmem()],
+        out_specs=anywhere,
+        out_shape=jax.ShapeDtypeStruct(whole.shape, whole.dtype),
+        scratch_shapes=[pltpu.SemaphoreType.DMA((2,))],
+        input_output_aliases={1: 0},
+        cost_estimate=pl.CostEstimate(flops=0, bytes_accessed=8 * one.size, transcendentals=0),
+        name="put_two",
+    )(jnp.stack([spot, other_spot]).astype(jnp.int32), whole, one, two)
+
+
+def gather_steps(ring, shard, first=None):
     pos, core = ring.locate()
-    whole = jnp.zeros((2 * ring.count * shard.shape[0],) + shard.shape[1:], shard.dtype)
+    whole = blank((2 * ring.count * shard.shape[0],) + shard.shape[1:], shard.dtype)
     piece = shard
     for label in range(ring.count):
         if label:
+            if label == 1 and first is not None:
+                piece = after(piece, first)
             waits = yield piece
             piece = lax.ppermute(piece, ring.axes, ring.pairs(-1))
             if waits:
                 piece = after(piece, *waits)
         other = ring.swap(piece)
-        whole = put(whole, piece, ring.owner(pos, core, label))
-        whole = put(whole, other, ring.owner(pos, 1 - core, label))
+        spots = ring.owner(pos, core, label), ring.owner(pos, 1 - core, label)
+        if first is None:
+            whole = put_two(whole, piece, spots[0], other, spots[1])
+        else:
+            whole = put(put(whole, piece, spots[0]), other, spots[1])
     yield whole
 
 
@@ -374,7 +421,8 @@
 
 
 def outer_pair_kernel(a_ref, b_ref, c_ref, *rest):
-    out_ref = rest[-1]
+    out_ref, mark_ref = rest[-2:]
+    mark_ref[...] = jnp.zeros(mark_ref.shape, mark_ref.dtype)
     units = b_ref.shape[1]
     out_ref[:, :units] = dot_tn(a_ref[...], b_ref[...]).astype(out_ref.dtype)
     out_ref[:, units:] = dot_tn(a_ref[...], c_ref[...]).astype(out_ref.dtype)
@@ -393,8 +441,14 @@
         grid=(grid,),
         in_specs=[spec((rows, TILE), lambda j: (0, j + start)), whole, whole]
         + [pl.BlockSpec(memory_space=pl.ANY)] * len(more),
-        out_specs=spec((TILE, 2 * units), lambda j: (j + start, 0)),
-        out_shape=jax.ShapeDtypeStruct((width, 2 * units), BF16),
+        out_specs=(
+            spec((TILE, 2 * units), lambda j: (j + start, 0)),
+            spec((8, 128), lambda j: (0, 0)),
+        ),
+        out_shape=(
+            jax.ShapeDtypeStruct((width, 2 * units), BF16),
+            jax.ShapeDtypeStruct((8, 128), F32),
+        ),
         input_output_aliases={3: 0} if more else {},
         compiler_params=pltpu.CompilerParams(
             dimension_semantics=("arbitrary",), vmem_limit_bytes=44 << 20
@@ -614,7 +668,7 @@
     lin_cols = qcols + 2 * HEAD_DIM
     out_cols = lin_cols + out_weight.shape[0]
     qkv_w, out_w = attn_w[:, :lin_cols], attn_w[:, lin_cols:out_cols]
-    gains = attn_w[:, out_cols:].T.astype(F32)
+    gains = attn_w[:, out_cols : out_cols + 4].T.astype(F32)
     gain_one, gain_two, gain_three, gain_four = (gains[i] for i in range(4))
 
     order = block_order[0]
@@ -650,7 +704,7 @@
     kv_move = begun(gather_steps(near, kv_own))
     for _ in range(near.count - 1):
         kv = step(kv_move, queries, qseg, *infos)
-    down_move = gather_steps(wide, after(down_own, attn_w))
+    down_move = gather_steps(wide, down_own, attn_w)
     passing = next(down_move)
     down_left = wide.count - 1
 
@@ -697,16 +751,14 @@
         next(move)
     for n in range(hops - 1):
         sent = [step(move) for move in moves]
-        if n == 0:
-            pass_down(*sent)
     first = step(moves[0])
-    while down_left:
-        pass_down()
-    down_w = passing
 
     gate_lin, up_lin, activ = [None] * halves, [None] * halves, [None] * halves
     gate_lin[0], up_lin[0], activ[0] = gate_up(after(first, sent[-1]), gu_w)
     normed_mlp = [first] + [step(move, activ[0]) for move in moves[1:]]
+    while down_left:
+        pass_down(activ[0])
+    down_w = passing
     sums = [tp_scatter(down(activ[0], down_w), tp)]
     sent = next(sums[0])
     gate_lin[1], up_lin[1], activ[1] = gate_up(after(normed_mlp[1], sent), gu_w)
@@ -735,22 +787,18 @@
     step(moves[1])
     first = step(moves[0])
     sent = step(moves[1])
-    layer_move = begun(tp_gather(after(jnp.stack(layer_own), first), tp))
-
     d_gate, d_up = [None] * halves, [None] * halves
-    d_gate[0], d_up[0] = d_gate_up(after(first, sent), down_w, gate_lin[0], up_lin[0])
-    d_mlp_low = [first, step(moves[1], d_gate[0])]
+    d_mlp_low = [first, step(moves[1])]
     grad_down = outer(joined(d_mlp_low), joined(activ), "grad_down")
-    sent_layer = step(layer_move, grad_down)
-    part = d_normed_of(after(d_gate[0], grad_down, sent_layer), d_up[0], gu_w)
+    d_gate[0], d_up[0] = d_gate_up(after(first, grad_down), down_w, gate_lin[0], up_lin[0])
+    part = d_normed_of(after(d_gate[0], grad_down), d_up[0], gu_w)
     sums = [tp_scatter(part, tp)]
     sent = next(sums[0])
     d_gate[1], d_up[1] = d_gate_up(after(d_mlp_low[1], sent), down_w, gate_lin[1], up_lin[1])
     sent = step(sums[0], d_gate[1])
-    sent_layer = step(layer_move, sent)
-    part = d_normed_of(after(d_gate[1], sent, sent_layer), d_up[1], gu_w)
+    part = d_normed_of(after(d_gate[1], sent), d_up[1], gu_w)
     sums.append(tp_scatter(part, tp))
-    next(sums[1])
+    sent = next(sums[1]), step(sums[0], part)
     d_resid, grad_three, grad_two, moves = [], [], [], []
 
     def middle_back(i, part):
@@ -762,36 +810,39 @@
         moves.append(tp_gather(d_branch.astype(BF16), tp))
         return next(moves[i])
 
-    step(sums[0], part)
-    sent = middle_back(0, step(sums[0]))
-    layer_out = step(layer_move, part)
     normed_all = joined(normed_mlp)
     d_pair = joined(d_gate), joined(d_up)
-    grad_gu = outer_pair(after(normed_all, sent, layer_out), *d_pair, None, "grad_gate_up")
-    mark = grad_gu[:8, :128]
+    grad_gu, mark = outer_pair(after(normed_all, *sent), *d_pair, None, "grad_gate_up")
+    sent = middle_back(0, step(sums[0], mark)), step(sums[1], mark)
+    grad_gu, mark = outer_pair(after(normed_all, *sent), *d_pair, grad_gu, "grad_gate_up_more")
     sent = step(sums[1], mark), step(moves[0], mark)
-    grad_gu = outer_pair(after(normed_all, *sent), *d_pair, grad_gu, "grad_gate_up_more")
-    mark = grad_gu[-8:, :128]
-    step(sums[1], mark), step(moves[0], mark)
     grad_down = lax.psum_scatter(grad_down, split, scatter_dimension=0, tiled=True)
-    sent = middle_back(1, step(sums[1]))
-    grad_gu = held(grad_gu, grad_down, sent)
+    middle_back(1, step(sums[1]))
+    grad_gu = held(grad_gu, grad_down, *sent)
     grad_gu = lax.psum_scatter(grad_gu, split, scatter_dimension=0, tiled=True)
     grad_down = grad_down.astype(F32)
+    step(moves[0])
+    step(moves[1])
     first = step(moves[0])
-    d_attn_low = [first, finish(moves[1], hops)]
+    d_attn_low = [first, finish(moves[1], hops - 1)]
 
     d_attn_all = joined(d_attn_low)
     d_attended = dot(d_attn_all, out_w).astype(BF16)
     d_queries, d_kv = attend_back(
         info_all, queries, d_attended, kv, joined(inverse_sum), qseg, segs, heads
     )
+    kv_move = scatter_steps(near, d_kv, BF16)
+    d_queries = after(d_queries, next(kv_move))
     d_q_lin = rotate(
         d_queries.reshape(count, heads, HEAD_DIM) * scale, cosine[:, None], -sine[:, None]
     ).astype(BF16)
     d_q_lin = d_q_lin.reshape(count, qcols)
-    from_q = dot_nt(d_q_lin, qkv_w[:, :qcols])
-    d_kv = scatter(near, d_kv, BF16)
+    layer_move = begun(tp_gather(after(jnp.stack(layer_own), d_attn_all), tp))
+    passing = step(layer_move, d_kv)
+    from_q = dot_nt(after(d_q_lin, passing), qkv_w[:, :qcols])
+    passing = step(layer_move, from_q)
+    for _ in range(near.count - 1):
+        d_kv = step(kv_move, passing)
     d_key_lin = rotate(d_kv[:, :HEAD_DIM], cosine, -sine).astype(BF16)
     d_kv_lin = jnp.concatenate([d_key_lin, d_kv[:, HEAD_DIM:].astype(BF16)], axis=1)
     d_normed_attn = from_q + dot_nt(d_kv_lin, qkv_w[:, qcols:])
@@ -799,33 +850,36 @@
     sums = [tp_scatter(rows_of(d_normed_low, i), tp) for i in both]
     sent = [next(part) for part in sums]
     grad_one = jnp.sum(after(d_normed_attn, *sent) * inputs * inv_one, axis=0)
-    grad_gains = jnp.stack([grad_one, sum(grad_two), sum(grad_three), sum(grad_four)])
-    grad_gains = jnp.pad(grad_gains, ((0, 124), (0, 0))).T
+    grad_gains = [grad_one, sum(grad_two), sum(grad_three), sum(grad_four)]
+    grad_gains = jnp.stack(grad_gains + [jnp.zeros_like(grad_one)] * 4)
+    left, bit = hops, 1
+    while bit < tp:
+        got = lax.ppermute(grad_gains, "tp", [(i, i ^ bit) for i in range(tp)])
+        if left > 1:
+            sent, left = [step(part) for part in sums], left - 1
+        grad_gains = grad_gains + after(got, *sent)
+        bit *= 2
+    grad_gains = jnp.pad(grad_gains, ((0, 120), (0, 0))).T
     d_lin = jnp.concatenate([d_q_lin, d_kv_lin], axis=1)
     grad_attn = outer_two(
         normed_attn, d_lin, d_attn_all, joined(attended), grad_gains, "grad_attn"
     )
-    for _ in range(hops):
+    grad_attn = held(grad_attn, grad_gu, *sent)
+    for _ in range(left):
         sent = [step(part) for part in sums]
+    grad_attn = lax.psum_scatter(grad_attn, split, scatter_dimension=0, tiled=True).astype(F32)
+    grad_gu = grad_gu.astype(F32)
     moves = []
     for i in both:
         own = share_of(tok, i)
         d_in, unused = norm_back(own, inverse_of(own), gain_one, sent[i])
         moves.append(begun(tp_gather((d_resid[i] + d_in).astype(BF16), tp, F32)))
-        sent[i] = step(moves[i])
-    grad_attn = held(grad_attn, grad_gu, *sent)
-    grad_gu = grad_gu.astype(F32)
-    grad_attn = lax.psum_scatter(grad_attn, split, scatter_dimension=0, tiled=True).astype(F32)
-    for _ in range(hops - 1):
+    for n in range(hops):
         grad_tokens = [step(move) for move in moves]
-    grad_gains = grad_attn[:, out_cols:]
-    bit = 1
-    while bit < tp:
-        swap = [(i, i ^ bit) for i in range(tp)]
-        grad_gains = grad_gains + lax.ppermute(grad_gains, "tp", swap)
-        bit *= 2
+        if n == hops - 2:
+            layer_out = step(layer_move, *grad_tokens)
+    grad_gains = grad_attn[:, out_cols : out_cols + 4].T
     grad_qkv, grad_out = grad_attn[:, :lin_cols], grad_attn[:, lin_cols:out_cols]
-    grad_gains = grad_gains.T
 
     return (
         layer_out.reshape(1, count, width),

time: 731 us -> 699 us (0.956)
  waiting for transfers between devices: 409 us -> 345 us
  other arithmetic: 41.6 us -> 56.2 us
  starting transfers between devices: 23 us -> 33.3 us
  Pallas kernels: 120 us -> 128 us
    reduce_scatter x1, waiting for transfers between devices: 28.9 us -> 0.01 us  [per_device(): lax.psum_scatter(grad_attn, split, scatter_dimension=0, tiled=True)]
    ppermute x1, waiting for transfers between devices: 22.5 us -> 0.01 us  [scatter_steps(): got = lax.ppermute(total, ring.axes, ring.pairs(1))]
    ppermute x24, waiting for transfers between devices: 120 us -> 98.9 us  [tp_scatter(): got = lax.ppermute(total, 'tp', tp_pairs(count))]
    ppermute x27, waiting for transfers between devices: 154 us -> 162 us  [tp_gather(): piece = lax.ppermute(piece, 'tp', tp_pairs(count))]
    ppermute x24, starting transfers between devices: 11.2 us -> 18.9 us  [tp_scatter(): got = lax.ppermute(total, 'tp', tp_pairs(count))]
    dynamic_update_slice x11 -> x8, local copies, waits for them, and re-layouts: 16 us -> 18.9 us  [put(): return lax.dynamic_update_slice(buffer, piece, starts)]
    unnamed x232 -> x244, local copies, waits for them, and re-layouts: 24.9 us -> 24.7 us
  transfers between devices with their start and end apart: 71 -> 71, of which waited for: 51 -> 45; matrix products, arithmetic and copies ran while one was open for 16% -> 18% of each run, Pallas kernels for 14% -> 15%
where the time goes in v3:
time: 699 us; the launch traced here: 690 us
  waiting for transfers between devices  345 us (49%)
  Pallas kernels  128 us (18%)
  local copies, waits for them, and re-layouts  82.8 us (12%)
  other arithmetic  56.2 us (8%)
  starting transfers between devices  33.3 us (5%)
  between operations  27.5 us (4%)
  matrix products  17.4 us (2%)
    ppermute x27, waiting for transfers between devices, tp_gather(): piece = lax.ppermute(piece, 'tp', tp_pairs(count))  162 us
    ppermute x24, waiting for transfers between devices, tp_scatter(): got = lax.ppermute(total, 'tp', tp_pairs(count))  98.9 us
    all_gather x1, waiting for transfers between devices, per_device(): attn_w = lax.all_gather(attn_own, split, axis=0, tiled=True)  51.3 us
    ppermute x4, waiting for transfers between devices, gather_steps(): piece = lax.ppermute(piece, ring.axes, ring.pairs(-1))  27 us
    unnamed x244, local copies, waits for them, and re-layouts  24.7 us
    pallas_call x2, Pallas kernels, d_normed_of(): call(d_normed_kernel, width // TILE, [whole, whole, spec((TILE, units), l...  22.5 us
    pallas_call x2, Pallas kernels, gate_up(): call(gate_up_kernel, tiles, [spec((rows, depth), lambda j: (0, 0)), spec(...  21.5 us
    ppermute x24, starting transfers between devices, tp_scatter(): got = lax.ppermute(total, 'tp', tp_pairs(count))  18.9 us
  transfers between devices with their start and end apart: 71, of which 45 were waited for; matrix products, arithmetic and copies ran while one was open for 18% of the time, Pallas kernels for 15%

profile of v3, /device:TPU:0, one launch (start us, length us, event | category | flops | bytes accessed | tf_op | source)
XLA Modules:
  0.0 689.9 jit_solution(7427544825265233013)
XLA Ops:
  17.8 51.3 %all-gather.3.cloned.1.call-done = bf16[2304,1664]{1,0:T(8,128)(2,1)} async-done(((bf16[288,1664]{1,0:T(8,128)(2,1)}), bf16[2304,1664]{1,0:T(8,128)(2,1)}) %all-gather.3.cloned.1.call-update) | async-done | bytes 7667728 | tf_op jit(solution)/shard_map/all_gather | solution.py:664
  100.6 20.3 %collective-permute-done.1.one_ref = bf16[512,512]{1,0:T(8,128)(2,1)} collective-permute-done((bf16[512,512]{1,0:T(8,128)(2,1)}, bf16[512,512]{1,0:T(8,128)(2,1)}, u32[]{:S(2)}, u32[]{:S(2)}) %collective-permute-start.1) | collective-permute-done | bytes 524320 | tf_op jit(solution)/shard_map/ppermute | solution.py:117
  154.0 8.7 %collective-permute-done.3 = bf16[64,2304]{1,0:T(8,128)(2,1)S(1)} collective-permute-done((bf16[64,2304]{1,0:T(8,128)(2,1)S(1)}, bf16[64,2304]{1,0:T(8,128)(2,1)S(1)}, u32[]{:S(2)}, u32[]{:S(2)}) %collective-permute-start.3) | collective-permute-done | bytes 294944 | tf_op jit(solution)/shard_map/ppermute | solution.py:172
  190.3 8.2 %collective-permute-done.6 = bf16[64,2304]{1,0:T(8,128)(2,1)S(1)} collective-permute-done((bf16[64,2304]{1,0:T(8,128)(2,1)S(1)}, bf16[64,2304]{1,0:T(8,128)(2,1)S(1)}, u32[]{:S(2)}, u32[]{:S(2)}) %collective-permute-start.6) | collective-permute-done | bytes 294944 | tf_op jit(solution)/shard_map/ppermute | solution.py:194
  221.0 10.9 %gate_up.2 = (f32[256,2304]{1,0:T(8,128)S(1)}, f32[256,2304]{1,0:T(8,128)S(1)}, bf16[256,2304]{1,0:T(8,128)(2,1)S(1)}) custom-call(bf16[256,2304]{1,0:T(8,128)(2,1)S(1)} %constant_dynamic-update-slice_fusion.42.x_ref, bf16[2304,4608]{1,0:T(8,128)(2,1)} %all-gather.5.cloned.1.call-done.gate_ref.up_ref.wa_ref.wb_ref, ...), custom_call_target="tpu_custom_call" | custom-call | flops 5435817984 | bytes 28311552 | tf_op jit(solution)/shard_map/gate_up/pallas_call | solution.py:315
  254.1 10.6 %gate_up.3 = (f32[256,2304]{1,0:T(8,128)S(1)}, f32[256,2304]{1,0:T(8,128)S(1)}, bf16[256,2304]{1,0:T(8,128)(2,1)S(1)}) custom-call(bf16[256,2304]{1,0:T(8,128)(2,1)S(1)} %get-tuple-element.225, bf16[2304,4608]{1,0:T(8,128)(2,1)} %all-gather.5.cloned.1.call-done.gate_ref.up_ref.wa_ref.wb_ref, ...), custom_call_target="tpu_custom_call" | custom-call | flops 5435817984 | bytes 28311552 | tf_op jit(solution)/shard_map/gate_up/pallas_call | solution.py:315
  266.1 7.1 %down.3 = bf16[256,2304]{1,0:T(8,128)(2,1)S(1)} custom-call(bf16[256,2304]{1,0:T(8,128)(2,1)S(1)} %get-tuple-element.87.x_ref, bf16[2304,2304]{1,0:T(8,128)(2,1)} %constant_dynamic-update-slice_fusion.34.w_ref), custom_call_target="tpu_custom_call" | custom-call | flops 2717908992 | bytes 10616832 | tf_op jit(solution)/shard_map/down/pallas_call | solution.py:338
  276.6 8.4 %collective-permute-done.25 = bf16[64,2304]{1,0:T(8,128)(2,1)S(1)} collective-permute-done((bf16[64,2304]{1,0:T(8,128)(2,1)S(1)}, bf16[64,2304]{1,0:T(8,128)(2,1)S(1)}, u32[]{:S(2)}, u32[]{:S(2)}) %collective-permute-start.25) | collective-permute-done | bytes 294944 | tf_op jit(solution)/shard_map/ppermute | solution.py:172
  313.7 10.2 %collective-permute-done.28 = bf16[64,2304]{1,0:T(8,128)(2,1)S(1)} collective-permute-done((bf16[64,2304]{1,0:T(8,128)(2,1)S(1)}, bf16[64,2304]{1,0:T(8,128)(2,1)S(1)}, u32[]{:S(2)}, u32[]{:S(2)}) %collective-permute-start.28) | collective-permute-done | bytes 294944 | tf_op jit(solution)/shard_map/ppermute | solution.py:194
  355.2 8.1 %grad_down.1 = bf16[2304,2304]{1,0:T(8,128)(2,1)} custom-call(bf16[512,2304]{1,0:T(8,128)(2,1)S(1)} %pad_maximum_fusion.a_ref, bf16[512,2304]{1,0:T(8,128)(2,1)S(1)} %pad_maximum_fusion.1.b_ref), custom_call_target="tpu_custom_call" | custom-call | flops 5435817984 | bytes 10616832 | tf_op jit(solution)/shard_map/grad_down/pallas_call | solution.py:411
  368.1 8.0 %d_gate_up.2 = (bf16[256,2304]{1,0:T(8,128)(2,1)S(1)}, bf16[256,2304]{1,0:T(8,128)(2,1)S(1)}) custom-call(bf16[256,2304]{1,0:T(8,128)(2,1)S(1)} %copy-done.3, bf16[2304,2304]{1,0:T(8,128)(2,1)} %constant_dynamic-update-slice_fusion.34.w_ref, f32[256,2304]{1,0:T(8,128)S(1)} %copy-done.11, f32[256,2304]{1,0:T(8,128)S(1)} %copy-done.13), custom_call_target="tpu_custom_call" | custom-call | flops 2717908992 | bytes 17694720 | tf_op jit(solution)/shard_map/d_gate_up/pallas_call | solution.py:361
  376.1 12.0 %d_normed.2 = bf16[256,2304]{1,0:T(8,128)(2,1)S(1)} custom-call(bf16[256,2304]{1,0:T(8,128)(2,1)S(1)} %get-tuple-element.93.a_ref, bf16[256,2304]{1,0:T(8,128)(2,1)S(1)} %get-tuple-element.94.b_ref, bf16[2304,4608]{1,0:T(8,128)(2,1)} %all-gather.5.cloned.1.call-done.gate_ref.up_ref.wa_ref.wb_ref, ...), custom_call_target="tpu_custom_call" | custom-call | flops 5435817984 | bytes 21233664 | tf_op jit(solution)/shard_map/d_normed/pallas_call | solution.py:387
  388.2 7.5 %d_gate_up.3 = (bf16[256,2304]{1,0:T(8,128)(2,1)S(1)}, bf16[256,2304]{1,0:T(8,128)(2,1)S(1)}) custom-call(bf16[256,2304]{1,0:T(8,128)(2,1)S(1)} %constant_dynamic-update-slice_fusion.22.x_ref, bf16[2304,2304]{1,0:T(8,128)(2,1)} %constant_dynamic-update-slice_fusion.34.w_ref, f32[256,2304]{1,0:T(8,128)S(1)} %copy-done.15, f32[256,2304]{1,0:T(8,128)S(1)} %copy-done.17), custom_call_target="tpu_custom_call" | custom-call | flops 2717908992 | bytes 17694720 | tf_op jit(solution)/shard_map/d_gate_up/pallas_call | solution.py:361
  398.3 10.6 %d_normed.3 = bf16[256,2304]{1,0:T(8,128)(2,1)S(1)} custom-call(bf16[256,2304]{1,0:T(8,128)(2,1)S(1)} %get-tuple-element.100.a_ref, bf16[256,2304]{1,0:T(8,128)(2,1)S(1)} %get-tuple-element.101.b_ref, bf16[2304,4608]{1,0:T(8,128)(2,1)} %all-gather.5.cloned.1.call-done.gate_ref.up_ref.wa_ref.wb_ref, ...), custom_call_target="tpu_custom_call" | custom-call | flops 5435817984 | bytes 21233664 | tf_op jit(solution)/shard_map/d_normed/pallas_call | solution.py:387
  412.1 10.8 %grad_gate_up.1 = (bf16[2304,4608]{1,0:T(8,128)(2,1)}, f32[8,128]{1,0:T(8,128)}) custom-call(bf16[512,2304]{1,0:T(8,128)(2,1)S(1)} %pad_maximum_fusion.2.a_ref, bf16[512,2304]{1,0:T(8,128)(2,1)S(1)} %constant_dynamic-update-slice_fusion.6.b_ref, bf16[512,2304]{1,0:T(8,128)(2,1)S(1)} %constant_dynamic-update-slice_fusion.8.c_ref), custom_call_target="tpu_custom_call" | custom-call | flops 7247757312 | bytes 14155776 | tf_op jit(solution)/shard_map/grad_gate_up/pallas_call | solution.py:439
  468.0 9.4 %collective-permute-done.43 = bf16[64,2304]{1,0:T(8,128)(2,1)S(1)} collective-permute-done((bf16[64,2304]{1,0:T(8,128)(2,1)S(1)}, bf16[64,2304]{1,0:T(8,128)(2,1)S(1)}, u32[]{:S(2)}, u32[]{:S(2)}) %collective-permute-start.43) | collective-permute-done | bytes 294944 | tf_op jit(solution)/shard_map/ppermute | solution.py:194
  477.5 9.4 %collective-permute-done.44 = bf16[64,2304]{1,0:T(8,128)(2,1)S(1)} collective-permute-done((bf16[64,2304]{1,0:T(8,128)(2,1)S(1)}, bf16[64,2304]{1,0:T(8,128)(2,1)S(1)}, u32[]{:S(2)}, u32[]{:S(2)}) %collective-permute-start.44) | collective-permute-done | bytes 294944 | tf_op jit(solution)/shard_map/ppermute | solution.py:194
  487.0 8.4 %collective-permute-done.45 = bf16[64,2304]{1,0:T(8,128)(2,1)S(1)} collective-permute-done((bf16[64,2304]{1,0:T(8,128)(2,1)S(1)}, bf16[64,2304]{1,0:T(8,128)(2,1)S(1)}, u32[]{:S(2)}, u32[]{:S(2)}) %collective-permute-start.45) | collective-permute-done | bytes 294944 | tf_op jit(solution)/shard_map/ppermute | solution.py:194
  498.7 10.3 %attend_back.1 = (f32[512,512]{1,0:T(8,128)S(1)}, f32[2048,512]{1,0:T(8,128)S(1)}) custom-call(s32[12]{0:T(128)S(1)} %pad_add_fusion.5.info, bf16[512,512]{1,0:T(8,128)(2,1)S(1)} %bitcast.104, bf16[512,512]{1,0:T(8,128)(2,1)S(1)} %fusion.14.do_ref, bf16[2048,512]{1,0:T(8,128)(2,1)S(1)} %copy-done.1, f32[1024,1]{1,0:T(8,128)S(1)} %copy-done.21, ...), custom_call_target="tpu_custom_call" | custom-call | flops 2952790016 | bytes 10485760 | tf_op jit(solution)/shard_map/attend_back/pallas_call | solution.py:609
  518.1 10.1 %collective-permute-done.46 = bf16[2,64,2304]{2,1,0:T(8,128)(2,1)} collective-permute-done((bf16[2,64,2304]{2,1,0:T(8,128)(2,1)}, bf16[2,64,2304]{2,1,0:T(8,128)(2,1)}, u32[]{:S(2)}, u32[]{:S(2)}) %collective-permute-start.46) | collective-permute-done | bytes 589856 | tf_op jit(solution)/shard_map/ppermute | solution.py:194
  533.8 11.3 %collective-permute-done.47 = bf16[2,64,2304]{2,1,0:T(8,128)(2,1)S(1)} collective-permute-done((bf16[2,64,2304]{2,1,0:T(8,128)(2,1)}, bf16[2,64,2304]{2,1,0:T(8,128)(2,1)S(1)}, u32[]{:S(2)}, u32[]{:S(2)}) %collective-permute-start.47) | collective-permute-done | bytes 589856 | tf_op jit(solution)/shard_map/ppermute | solution.py:194
  557.2 7.5 %collective-permute-done.57 = bf16[64,2304]{1,0:T(8,128)(2,1)} collective-permute-done((bf16[64,2304]{1,0:T(8,128)(2,1)}, bf16[64,2304]{1,0:T(8,128)(2,1)}, u32[]{:S(2)}, u32[]{:S(2)}) %collective-permute-start.57) | collective-permute-done | bytes 294944 | tf_op jit(solution)/shard_map/ppermute | solution.py:172
  619.6 16.1 %collective-permute-done.55 = bf16[64,2304]{1,0:T(8,128)(2,1)S(1)} collective-permute-done((bf16[64,2304]{1,0:T(8,128)(2,1)S(1)}, bf16[64,2304]{1,0:T(8,128)(2,1)S(1)}, u32[]{:S(2)}, u32[]{:S(2)}) %collective-permute-start.55) | collective-permute-done | bytes 294944 | tf_op jit(solution)/shard_map/ppermute | solution.py:194
  653.9 11.6 %collective-permute-done.62 = bf16[64,2304]{1,0:T(8,128)(2,1)S(1)} collective-permute-done((bf16[64,2304]{1,0:T(8,128)(2,1)S(1)}, bf16[64,2304]{1,0:T(8,128)(2,1)S(1)}, u32[]{:S(2)}, u32[]{:S(2)}) %collective-permute-start.62) | collective-permute-done | bytes 294944 | tf_op jit(solution)/shard_map/ppermute | solution.py:194
  (592 shorter events, 375.5 us)
Async XLA Ops:
  7.2 61.9 %all-gather.3.cloned.1.call-start = ((), (), s32[]{:S(2)}) async-start(), calls=%async_computation.3 | async-start | bytes 8626176 | tf_op jit(solution)/shard_map/all_gather | solution.py:664
  14.9 206.0 %all-gather.5.cloned.1.call-start = ((), (), s32[]{:S(2)}) async-start(), calls=%async_computation.4 | async-start | bytes 23887872 | tf_op jit(solution)/shard_map/all_gather | solution.py:666
  69.1 375.1 %reduce-scatter.4.cloned.1.call-start = ((), (), s32[]{:S(2)}) async-start(), calls=%async_computation.5 | async-start | bytes 11943936 | tf_op jit(solution)/shard_map/reduce_scatter | solution.py:819
  69.2 106.2 %collective-permute-start.14 = (bf16[288,2304]{1,0:T(8,128)(2,1)}, bf16[288,2304]{1,0:T(8,128)(2,1)}, u32[]{:S(2)}, u32[]{:S(2)}) collective-permute-start(bf16[288,2304]{1,0:T(8,128)(2,1)} %bitcast.18), channel_id=1, source_target_pairs={{0,4},{4,0},{8,12},{12,8},{16,20},{20,16},{24,28},{28,24},{1,5},{5... | collective-permute-start | bytes 3981320 | tf_op jit(solution)/shard_map/ppermute | solution.py:54
  94.8 26.1 %collective-permute-start.1 = (bf16[512,512]{1,0:T(8,128)(2,1)}, bf16[512,512]{1,0:T(8,128)(2,1)}, u32[]{:S(2)}, u32[]{:S(2)}) collective-permute-start(bf16[512,512]{1,0:T(8,128)(2,1)} %pad_maximum_fusion.6.one_ref), channel_id=1, source_target_pairs={{0,8},{4,12},{8,0},{12,4},{1,9},{5,13},{9,1},{13,5},{2,10},{6,14},... | collective-permute-start | bytes 1572872 | tf_op jit(solution)/shard_map/ppermute | solution.py:117
  97.8 30.7 %collective-permute-start = (bf16[512,512]{1,0:T(8,128)(2,1)}, bf16[512,512]{1,0:T(8,128)(2,1)}, u32[]{:S(2)}, u32[]{:S(2)}) collective-permute-start(bf16[512,512]{1,0:T(8,128)(2,1)} %pad_maximum_fusion.6.one_ref), channel_id=1, source_target_pairs={{0,4},{4,0},{8,12},{12,8},{1,5},{5,1},{9,13},{13,9},{2,6},{6,2},{1... | collective-permute-start | bytes 1572872 | tf_op jit(solution)/shard_map/ppermute | solution.py:54
  126.6 51.3 %collective-permute-start.15 = (bf16[288,2304]{1,0:T(8,128)(2,1)}, bf16[288,2304]{1,0:T(8,128)(2,1)}, u32[]{:S(2)}, u32[]{:S(2)}) collective-permute-start(bf16[288,2304]{1,0:T(8,128)(2,1)} %bitcast.18), channel_id=1, source_target_pairs={{0,16},{4,12},{8,0},{12,28},{24,8},{28,20},{16,24},{20,4},{1,17},{... | collective-permute-start | bytes 3981320 | tf_op jit(solution)/shard_map/ppermute | solution.py:117
  177.9 37.9 %collective-permute-start.17 = (bf16[288,2304]{1,0:T(8,128)(2,1)}, bf16[288,2304]{1,0:T(8,128)(2,1)}, u32[]{:S(2)}, u32[]{:S(2)}) collective-permute-start(bf16[288,2304]{1,0:T(8,128)(2,1)} %collective-permute-done.15), channel_id=1, source_target_pairs={{0,16},{4,12},{8,0},{12,28},{24,8},{28,20},{16,24},{20,4},{1,17},{... | collective-permute-start | bytes 3981320 | tf_op jit(solution)/shard_map/ppermute | solution.py:117
  178.9 55.0 %collective-permute-start.16 = (bf16[288,2304]{1,0:T(8,128)(2,1)}, bf16[288,2304]{1,0:T(8,128)(2,1)}, u32[]{:S(2)}, u32[]{:S(2)}) collective-permute-start(bf16[288,2304]{1,0:T(8,128)(2,1)} %collective-permute-done.15), channel_id=1, source_target_pairs={{0,4},{4,0},{8,12},{12,8},{16,20},{20,16},{24,28},{28,24},{1,5},{5... | collective-permute-start | bytes 3981320 | tf_op jit(solution)/shard_map/ppermute | solution.py:54
  187.0 17.8 %collective-permute-start.12 = (bf16[64,2304]{1,0:T(8,128)(2,1)S(1)}, bf16[64,2304]{1,0:T(8,128)(2,1)S(1)}, u32[]{:S(2)}, u32[]{:S(2)}) collective-permute-start(bf16[64,2304]{1,0:T(8,128)(2,1)S(1)} %get-tuple-element.176), channel_id=1, source_target_pairs={{0,1},{1,2},{2,3},{3,0},{4,5},{5,6},{6,7},{7,4},{8,9},{9,10},{10,1... | collective-permute-start | bytes 884744 | tf_op jit(solution)/shard_map/ppermute | solution.py:194
  215.8 18.1 %collective-permute-start.19 = (bf16[288,2304]{1,0:T(8,128)(2,1)}, bf16[288,2304]{1,0:T(8,128)(2,1)}, u32[]{:S(2)}, u32[]{:S(2)}) collective-permute-start(bf16[288,2304]{1,0:T(8,128)(2,1)} %collective-permute-done.17), channel_id=1, source_target_pairs={{0,16},{4,12},{8,0},{12,28},{24,8},{28,20},{16,24},{20,4},{1,17},{... | collective-permute-start | bytes 3981320 | tf_op jit(solution)/shard_map/ppermute | solution.py:117
  217.3 24.1 %collective-permute-start.22 = (bf16[64,2304]{1,0:T(8,128)(2,1)}, bf16[64,2304]{1,0:T(8,128)(2,1)}, u32[]{:S(2)}, u32[]{:S(2)}) collective-permute-start(bf16[64,2304]{1,0:T(8,128)(2,1)} %collective-permute-done.13), channel_id=1, source_target_pairs={{0,1},{1,2},{2,3},{3,0},{4,5},{5,6},{6,7},{7,4},{8,9},{9,10},{10,1... | collective-permute-start | bytes 884744 | tf_op jit(solution)/shard_map/ppermute | solution.py:194
  219.9 19.0 %collective-permute-start.18 = (bf16[288,2304]{1,0:T(8,128)(2,1)}, bf16[288,2304]{1,0:T(8,128)(2,1)}, u32[]{:S(2)}, u32[]{:S(2)}) collective-permute-start(bf16[288,2304]{1,0:T(8,128)(2,1)} %collective-permute-done.17), channel_id=1, source_target_pairs={{0,4},{4,0},{8,12},{12,8},{16,20},{20,16},{24,28},{28,24},{1,5},{5... | collective-permute-start | bytes 3981320 | tf_op jit(solution)/shard_map/ppermute | solution.py:54
  312.5 17.7 %collective-permute-start.31 = (bf16[64,2304]{1,0:T(8,128)(2,1)S(1)}, bf16[64,2304]{1,0:T(8,128)(2,1)S(1)}, u32[]{:S(2)}, u32[]{:S(2)}) collective-permute-start(bf16[64,2304]{1,0:T(8,128)(2,1)S(1)} %get-tuple-element.170), channel_id=1, source_target_pairs={{0,1},{1,2},{2,3},{3,0},{4,5},{5,6},{6,7},{7,4},{8,9},{9,10},{10,1... | collective-permute-start | bytes 884744 | tf_op jit(solution)/shard_map/ppermute | solution.py:194
  363.3 233.9 %reduce-scatter.6.cloned.1.call-start = ((), (), s32[]{:S(2)}) async-start(), calls=%async_computation.6 | async-start | bytes 23887872 | tf_op jit(solution)/shard_map/reduce_scatter | solution.py:822
  444.3 233.6 %reduce-scatter.8.cloned.1.call-start = ((), (), s32[]{:S(2)}) async-start(), calls=%async_computation.7 | async-start | bytes 8626176 | tf_op jit(solution)/shard_map/reduce_scatter | solution.py:870
  466.8 20.1 %collective-permute-start.40 = (bf16[64,2304]{1,0:T(8,128)(2,1)S(1)}, bf16[64,2304]{1,0:T(8,128)(2,1)S(1)}, u32[]{:S(2)}, u32[]{:S(2)}) collective-permute-start(bf16[64,2304]{1,0:T(8,128)(2,1)S(1)} %collective-permute-done.39), channel_id=1, source_target_pairs={{0,1},{1,2},{2,3},{3,0},{4,5},{5,6},{6,7},{7,4},{8,9},{9,10},{10,1... | collective-permute-start | bytes 884744 | tf_op jit(solution)/shard_map/ppermute | solution.py:194
  510.3 17.9 %collective-permute-start.46 = (bf16[2,64,2304]{2,1,0:T(8,128)(2,1)}, bf16[2,64,2304]{2,1,0:T(8,128)(2,1)}, u32[]{:S(2)}, u32[]{:S(2)}) collective-permute-start(bf16[2,64,2304]{2,1,0:T(8,128)(2,1)} %pad_maximum_fusion.5), channel_id=1, source_target_pairs={{0,1},{1,2},{2,3},{3,0},{4,5},{5,6},{6,7},{7,4},{8,9},{9,10},{10,1... | collective-permute-start | bytes 1769480 | tf_op jit(solution)/shard_map/ppermute | solution.py:194
  514.1 31.0 %collective-permute-start.50 = (bf16[512,512]{1,0:T(8,128)(2,1)}, bf16[512,512]{1,0:T(8,128)(2,1)}, u32[]{:S(2)}, u32[]{:S(2)}) collective-permute-start(bf16[512,512]{1,0:T(8,128)(2,1)} %get-tuple-element.181), channel_id=1, source_target_pairs={{0,4},{4,0},{8,12},{12,8},{1,5},{5,1},{9,13},{13,9},{2,6},{6,2},{1... | collective-permute-start | bytes 1572872 | tf_op jit(solution)/shard_map/ppermute | solution.py:54
  515.1 30.0 %collective-permute-start.51 = (bf16[512,512]{1,0:T(8,128)(2,1)}, bf16[512,512]{1,0:T(8,128)(2,1)}, u32[]{:S(2)}, u32[]{:S(2)}) collective-permute-start(bf16[512,512]{1,0:T(8,128)(2,1)} %add_convert_fusion), channel_id=1, source_target_pairs={{0,8},{4,12},{8,0},{12,4},{1,9},{5,13},{9,1},{13,5},{2,10},{6,14},... | collective-permute-start | bytes 1572872 | tf_op jit(solution)/shard_map/ppermute | solution.py:147
  553.3 17.7 %collective-permute-start.52 = (bf16[64,2304]{1,0:T(8,128)(2,1)}, bf16[64,2304]{1,0:T(8,128)(2,1)}, u32[]{:S(2)}, u32[]{:S(2)}) collective-permute-start(bf16[64,2304]{1,0:T(8,128)(2,1)} %constant_dynamic-slice_fusion.1), channel_id=1, source_target_pairs={{0,1},{1,2},{2,3},{3,0},{4,5},{5,6},{6,7},{7,4},{8,9},{9,10},{10,1... | collective-permute-start | bytes 884744 | tf_op jit(solution)/shard_map/ppermute | solution.py:172
  599.2 17.7 %collective-permute-start.54 = (bf16[64,2304]{1,0:T(8,128)(2,1)S(1)}, bf16[64,2304]{1,0:T(8,128)(2,1)S(1)}, u32[]{:S(2)}, u32[]{:S(2)}) collective-permute-start(bf16[64,2304]{1,0:T(8,128)(2,1)S(1)} %copy-done.68), channel_id=1, source_target_pairs={{0,1},{1,2},{2,3},{3,0},{4,5},{5,6},{6,7},{7,4},{8,9},{9,10},{10,1... | collective-permute-start | bytes 884744 | tf_op jit(solution)/shard_map/ppermute | solution.py:172
  601.8 40.4 %collective-permute-start.49 = (bf16[2,64,2304]{2,1,0:T(8,128)(2,1)S(1)}, bf16[2,64,2304]{2,1,0:T(8,128)(2,1)S(1)}, u32[]{:S(2)}, u32[]{:S(2)}) collective-permute-start(bf16[2,64,2304]{2,1,0:T(8,128)(2,1)S(1)} %copy-done.73), channel_id=1, source_target_pairs={{0,1},{1,2},{2,3},{3,0},{4,5},{5,6},{6,7},{7,4},{8,9},{9,10},{10,1... | collective-permute-start | bytes 1769480 | tf_op jit(solution)/shard_map/ppermute | solution.py:194
  619.5 22.6 %collective-permute-start.60 = (bf16[64,2304]{1,0:T(8,128)(2,1)S(1)}, bf16[64,2304]{1,0:T(8,128)(2,1)S(1)}, u32[]{:S(2)}, u32[]{:S(2)}) collective-permute-start(bf16[64,2304]{1,0:T(8,128)(2,1)S(1)} %get-tuple-element.160), channel_id=1, source_target_pairs={{0,1},{1,2},{2,3},{3,0},{4,5},{5,6},{6,7},{7,4},{8,9},{9,10},{10,1... | collective-permute-start | bytes 884744 | tf_op jit(solution)/shard_map/ppermute | solution.py:194
  (163 other events, 1665.1 us)
Sparse Core Ops, SparseCore 0:
  15.0 54.0 all-gather.2
  71.6 142.8 all-gather.4
  363.4 80.8 reduce-scatter.3
  447.7 148.3 reduce-scatter.5
  599.4 68.4 reduce-scatter.7

commit v4 on v3

--- a/solution.py
+++ b/solution.py
@@ -867,7 +867,7 @@
     grad_attn = held(grad_attn, grad_gu, *sent)
     for _ in range(left):
         sent = [step(part) for part in sums]
-    grad_attn = lax.psum_scatter(grad_attn, split, scatter_dimension=0, tiled=True).astype(F32)
+    grad_attn = lax.psum_scatter(grad_attn, split, scatter_dimension=0, tiled=True)
     grad_gu = grad_gu.astype(F32)
     moves = []
     for i in both:
@@ -878,15 +878,16 @@
         grad_tokens = [step(move) for move in moves]
         if n == hops - 2:
             layer_out = step(layer_move, *grad_tokens)
-    grad_gains = grad_attn[:, out_cols : out_cols + 4].T
-    grad_qkv, grad_out = grad_attn[:, :lin_cols], grad_attn[:, lin_cols:out_cols]
+    grad_gains = grad_attn[:, out_cols : out_cols + 4].T.astype(F32)
+    grad_out = grad_attn[:, lin_cols:out_cols].astype(F32)
+    grad_qkv = grad_attn[:, :lin_cols]
 
     return (
         layer_out.reshape(1, count, width),
         joined(grad_tokens)[None],
-        grad_qkv[:, :qcols],
-        grad_qkv[:, qcols : qcols + HEAD_DIM],
-        grad_qkv[:, qcols + HEAD_DIM :],
+        grad_qkv[:, :qcols].astype(F32),
+        grad_qkv[:, qcols : qcols + HEAD_DIM].astype(F32),
+        grad_qkv[:, qcols + HEAD_DIM :].astype(F32),
         grad_out.T,
         grad_gu[:, : gate_weight.shape[1]],
         grad_gu[:, gate_weight.shape[1] :],

time: 699 us -> 699 us (level)
  Pallas kernels: 128 us -> 119 us
    unnamed x244 -> x242, local copies, waits for them, and re-layouts: 24.7 us -> 24 us
  transfers between devices with their start and end apart: 71 -> 71, of which waited for: 45 -> 47; matrix products, arithmetic and copies ran while one was open for 18% -> 18% of each run, Pallas kernels for 15% -> 14%
where the time goes in v4:
time: 699 us; the launch traced here: 688 us
  waiting for transfers between devices  344 us (49%)
  Pallas kernels  119 us (17%)
  local copies, waits for them, and re-layouts  79.9 us (11%)
  other arithmetic  60.1 us (9%)
  starting transfers between devices  40.2 us (6%)
  between operations  27.5 us (4%)
  matrix products  17.7 us (3%)
    ppermute x27, waiting for transfers between devices, tp_gather(): piece = lax.ppermute(piece, 'tp', tp_pairs(count))  157 us
    ppermute x24, waiting for transfers between devices, tp_scatter(): got = lax.ppermute(total, 'tp', tp_pairs(count))  97 us
    all_gather x1, waiting for transfers between devices, per_device(): attn_w = lax.all_gather(attn_own, split, axis=0, tiled=True)  51.3 us
    ppermute x4, waiting for transfers between devices, gather_steps(): piece = lax.ppermute(piece, ring.axes, ring.pairs(-1))  28.2 us
    unnamed x242, local copies, waits for them, and re-layouts  24 us
    pallas_call x2, Pallas kernels, d_normed_of(): call(d_normed_kernel, width // TILE, [whole, whole, spec((TILE, units), l...  21.8 us
    pallas_call x2, Pallas kernels, gate_up(): call(gate_up_kernel, tiles, [spec((rows, depth), lambda j: (0, 0)), spec(...  21.5 us
    dynamic_update_slice x8, local copies, waits for them, and re-layouts, put(): return lax.dynamic_update_slice(buffer, piece, starts)  19.3 us
  transfers between devices with their start and end apart: 71, of which 47 were waited for; matrix products, arithmetic and copies ran while one was open for 18% of the time, Pallas kernels for 14%

profile of v4, /device:TPU:0, one launch (start us, length us, event | category | flops | bytes accessed | tf_op | source)
XLA Modules:
  0.0 688.0 jit_solution(11095595943325222629)
XLA Ops:
  17.8 51.3 %all-gather.3.cloned.1.call-done = bf16[2304,1664]{1,0:T(8,128)(2,1)} async-done(((bf16[288,1664]{1,0:T(8,128)(2,1)}), bf16[2304,1664]{1,0:T(8,128)(2,1)}) %all-gather.3.cloned.1.call-update) | async-done | bytes 7667728 | tf_op jit(solution)/shard_map/all_gather | solution.py:664
  100.6 20.3 %collective-permute-done.1.one_ref = bf16[512,512]{1,0:T(8,128)(2,1)} collective-permute-done((bf16[512,512]{1,0:T(8,128)(2,1)}, bf16[512,512]{1,0:T(8,128)(2,1)}, u32[]{:S(2)}, u32[]{:S(2)}) %collective-permute-start.1) | collective-permute-done | bytes 524320 | tf_op jit(solution)/shard_map/ppermute | solution.py:117
  189.3 7.1 %collective-permute-done.6 = bf16[64,2304]{1,0:T(8,128)(2,1)S(1)} collective-permute-done((bf16[64,2304]{1,0:T(8,128)(2,1)S(1)}, bf16[64,2304]{1,0:T(8,128)(2,1)S(1)}, u32[]{:S(2)}, u32[]{:S(2)}) %collective-permute-start.6) | collective-permute-done | bytes 294944 | tf_op jit(solution)/shard_map/ppermute | solution.py:194
  221.8 10.9 %gate_up.2 = (f32[256,2304]{1,0:T(8,128)S(1)}, f32[256,2304]{1,0:T(8,128)S(1)}, bf16[256,2304]{1,0:T(8,128)(2,1)S(1)}) custom-call(bf16[256,2304]{1,0:T(8,128)(2,1)S(1)} %constant_dynamic-update-slice_fusion.42.x_ref, bf16[2304,4608]{1,0:T(8,128)(2,1)} %all-gather.5.cloned.1.call-done.gate_ref.up_ref.wa_ref.wb_ref, ...), custom_call_target="tpu_custom_call" | custom-call | flops 5435817984 | bytes 28311552 | tf_op jit(solution)/shard_map/gate_up/pallas_call | solution.py:315
  254.1 10.6 %gate_up.3 = (f32[256,2304]{1,0:T(8,128)S(1)}, f32[256,2304]{1,0:T(8,128)S(1)}, bf16[256,2304]{1,0:T(8,128)(2,1)S(1)}) custom-call(bf16[256,2304]{1,0:T(8,128)(2,1)S(1)} %get-tuple-element.227, bf16[2304,4608]{1,0:T(8,128)(2,1)} %all-gather.5.cloned.1.call-done.gate_ref.up_ref.wa_ref.wb_ref, ...), custom_call_target="tpu_custom_call" | custom-call | flops 5435817984 | bytes 28311552 | tf_op jit(solution)/shard_map/gate_up/pallas_call | solution.py:315
  266.1 7.1 %down.3 = bf16[256,2304]{1,0:T(8,128)(2,1)S(1)} custom-call(bf16[256,2304]{1,0:T(8,128)(2,1)S(1)} %get-tuple-element.87.x_ref, bf16[2304,2304]{1,0:T(8,128)(2,1)} %constant_dynamic-update-slice_fusion.34.w_ref), custom_call_target="tpu_custom_call" | custom-call | flops 2717908992 | bytes 10616832 | tf_op jit(solution)/shard_map/down/pallas_call | solution.py:338
  276.6 8.4 %collective-permute-done.25 = bf16[64,2304]{1,0:T(8,128)(2,1)S(1)} collective-permute-done((bf16[64,2304]{1,0:T(8,128)(2,1)S(1)}, bf16[64,2304]{1,0:T(8,128)(2,1)S(1)}, u32[]{:S(2)}, u32[]{:S(2)}) %collective-permute-start.25) | collective-permute-done | bytes 294944 | tf_op jit(solution)/shard_map/ppermute | solution.py:172
  313.7 10.2 %collective-permute-done.28 = bf16[64,2304]{1,0:T(8,128)(2,1)S(1)} collective-permute-done((bf16[64,2304]{1,0:T(8,128)(2,1)S(1)}, bf16[64,2304]{1,0:T(8,128)(2,1)S(1)}, u32[]{:S(2)}, u32[]{:S(2)}) %collective-permute-start.28) | collective-permute-done | bytes 294944 | tf_op jit(solution)/shard_map/ppermute | solution.py:194
  355.2 8.1 %grad_down.1 = bf16[2304,2304]{1,0:T(8,128)(2,1)} custom-call(bf16[512,2304]{1,0:T(8,128)(2,1)S(1)} %pad_maximum_fusion.a_ref, bf16[512,2304]{1,0:T(8,128)(2,1)S(1)} %pad_maximum_fusion.1.b_ref), custom_call_target="tpu_custom_call" | custom-call | flops 5435817984 | bytes 10616832 | tf_op jit(solution)/shard_map/grad_down/pallas_call | solution.py:411
  367.9 8.7 %d_gate_up.2 = (bf16[256,2304]{1,0:T(8,128)(2,1)S(1)}, bf16[256,2304]{1,0:T(8,128)(2,1)S(1)}) custom-call(bf16[256,2304]{1,0:T(8,128)(2,1)S(1)} %copy-done.3, bf16[2304,2304]{1,0:T(8,128)(2,1)} %constant_dynamic-update-slice_fusion.34.w_ref, f32[256,2304]{1,0:T(8,128)S(1)} %copy-done.11, f32[256,2304]{1,0:T(8,128)S(1)} %copy-done.13), custom_call_target="tpu_custom_call" | custom-call | flops 2717908992 | bytes 17694720 | tf_op jit(solution)/shard_map/d_gate_up/pallas_call | solution.py:361
  376.7 11.0 %d_normed.2 = bf16[256,2304]{1,0:T(8,128)(2,1)S(1)} custom-call(bf16[256,2304]{1,0:T(8,128)(2,1)S(1)} %get-tuple-element.93.a_ref, bf16[256,2304]{1,0:T(8,128)(2,1)S(1)} %get-tuple-element.94.b_ref, bf16[2304,4608]{1,0:T(8,128)(2,1)} %all-gather.5.cloned.1.call-done.gate_ref.up_ref.wa_ref.wb_ref, ...), custom_call_target="tpu_custom_call" | custom-call | flops 5435817984 | bytes 21233664 | tf_op jit(solution)/shard_map/d_normed/pallas_call | solution.py:387
  387.8 6.9 %d_gate_up.3 = (bf16[256,2304]{1,0:T(8,128)(2,1)S(1)}, bf16[256,2304]{1,0:T(8,128)(2,1)S(1)}) custom-call(bf16[256,2304]{1,0:T(8,128)(2,1)S(1)} %constant_dynamic-update-slice_fusion.22.x_ref, bf16[2304,2304]{1,0:T(8,128)(2,1)} %constant_dynamic-update-slice_fusion.34.w_ref, f32[256,2304]{1,0:T(8,128)S(1)} %copy-done.15, f32[256,2304]{1,0:T(8,128)S(1)} %copy-done.17), custom_call_target="tpu_custom_call" | custom-call | flops 2717908992 | bytes 17694720 | tf_op jit(solution)/shard_map/d_gate_up/pallas_call | solution.py:361
  397.4 10.7 %d_normed.3 = bf16[256,2304]{1,0:T(8,128)(2,1)S(1)} custom-call(bf16[256,2304]{1,0:T(8,128)(2,1)S(1)} %get-tuple-element.100.a_ref, bf16[256,2304]{1,0:T(8,128)(2,1)S(1)} %get-tuple-element.101.b_ref, bf16[2304,4608]{1,0:T(8,128)(2,1)} %all-gather.5.cloned.1.call-done.gate_ref.up_ref.wa_ref.wb_ref, ...), custom_call_target="tpu_custom_call" | custom-call | flops 5435817984 | bytes 21233664 | tf_op jit(solution)/shard_map/d_normed/pallas_call | solution.py:387
  411.2 10.8 %grad_gate_up.1 = (bf16[2304,4608]{1,0:T(8,128)(2,1)}, f32[8,128]{1,0:T(8,128)}) custom-call(bf16[512,2304]{1,0:T(8,128)(2,1)S(1)} %pad_maximum_fusion.2.a_ref, bf16[512,2304]{1,0:T(8,128)(2,1)S(1)} %constant_dynamic-update-slice_fusion.6.b_ref, bf16[512,2304]{1,0:T(8,128)(2,1)S(1)} %constant_dynamic-update-slice_fusion.8.c_ref), custom_call_target="tpu_custom_call" | custom-call | flops 7247757312 | bytes 14155776 | tf_op jit(solution)/shard_map/grad_gate_up/pallas_call | solution.py:439
  427.8 6.8 grad_gate_up_more.1
  453.1 7.0 %collective-permute-done.42 = bf16[64,2304]{1,0:T(8,128)(2,1)S(1)} collective-permute-done((bf16[64,2304]{1,0:T(8,128)(2,1)}, bf16[64,2304]{1,0:T(8,128)(2,1)S(1)}, u32[]{:S(2)}, u32[]{:S(2)}) %collective-permute-start.42) | collective-permute-done | bytes 294944 | tf_op jit(solution)/shard_map/ppermute | solution.py:172
  466.6 9.4 %collective-permute-done.43 = bf16[64,2304]{1,0:T(8,128)(2,1)S(1)} collective-permute-done((bf16[64,2304]{1,0:T(8,128)(2,1)S(1)}, bf16[64,2304]{1,0:T(8,128)(2,1)S(1)}, u32[]{:S(2)}, u32[]{:S(2)}) %collective-permute-start.43) | collective-permute-done | bytes 294944 | tf_op jit(solution)/shard_map/ppermute | solution.py:194
  476.1 9.4 %collective-permute-done.44 = bf16[64,2304]{1,0:T(8,128)(2,1)S(1)} collective-permute-done((bf16[64,2304]{1,0:T(8,128)(2,1)S(1)}, bf16[64,2304]{1,0:T(8,128)(2,1)S(1)}, u32[]{:S(2)}, u32[]{:S(2)}) %collective-permute-start.44) | collective-permute-done | bytes 294944 | tf_op jit(solution)/shard_map/ppermute | solution.py:194
  485.6 8.4 %collective-permute-done.45 = bf16[64,2304]{1,0:T(8,128)(2,1)S(1)} collective-permute-done((bf16[64,2304]{1,0:T(8,128)(2,1)S(1)}, bf16[64,2304]{1,0:T(8,128)(2,1)S(1)}, u32[]{:S(2)}, u32[]{:S(2)}) %collective-permute-start.45) | collective-permute-done | bytes 294944 | tf_op jit(solution)/shard_map/ppermute | solution.py:194
  514.1 7.9 %collective-permute-done.46 = bf16[2,64,2304]{2,1,0:T(8,128)(2,1)} collective-permute-done((bf16[2,64,2304]{2,1,0:T(8,128)(2,1)}, bf16[2,64,2304]{2,1,0:T(8,128)(2,1)}, u32[]{:S(2)}, u32[]{:S(2)}) %collective-permute-start.46) | collective-permute-done | bytes 589856 | tf_op jit(solution)/shard_map/ppermute | solution.py:194
  527.6 10.8 %collective-permute-done.47 = bf16[2,64,2304]{2,1,0:T(8,128)(2,1)S(1)} collective-permute-done((bf16[2,64,2304]{2,1,0:T(8,128)(2,1)}, bf16[2,64,2304]{2,1,0:T(8,128)(2,1)S(1)}, u32[]{:S(2)}, u32[]{:S(2)}) %collective-permute-start.47) | collective-permute-done | bytes 589856 | tf_op jit(solution)/shard_map/ppermute | solution.py:194
  551.2 7.4 %collective-permute-done.57 = bf16[64,2304]{1,0:T(8,128)(2,1)} collective-permute-done((bf16[64,2304]{1,0:T(8,128)(2,1)}, bf16[64,2304]{1,0:T(8,128)(2,1)}, u32[]{:S(2)}, u32[]{:S(2)}) %collective-permute-start.57) | collective-permute-done | bytes 294944 | tf_op jit(solution)/shard_map/ppermute | solution.py:172
  617.7 15.5 %collective-permute-done.55 = bf16[64,2304]{1,0:T(8,128)(2,1)S(1)} collective-permute-done((bf16[64,2304]{1,0:T(8,128)(2,1)S(1)}, bf16[64,2304]{1,0:T(8,128)(2,1)S(1)}, u32[]{:S(2)}, u32[]{:S(2)}) %collective-permute-start.55) | collective-permute-done | bytes 294944 | tf_op jit(solution)/shard_map/ppermute | solution.py:194
  652.4 10.4 %collective-permute-done.62 = bf16[64,2304]{1,0:T(8,128)(2,1)S(1)} collective-permute-done((bf16[64,2304]{1,0:T(8,128)(2,1)S(1)}, bf16[64,2304]{1,0:T(8,128)(2,1)S(1)}, u32[]{:S(2)}, u32[]{:S(2)}) %collective-permute-start.62) | collective-permute-done | bytes 294944 | tf_op jit(solution)/shard_map/ppermute | solution.py:194
  (588 shorter events, 385.2 us)
Async XLA Ops:
  7.2 61.9 %all-gather.3.cloned.1.call-start = ((), (), s32[]{:S(2)}) async-start(), calls=%async_computation.3 | async-start | bytes 8626176 | tf_op jit(solution)/shard_map/all_gather | solution.py:664
  14.9 206.9 %all-gather.5.cloned.1.call-start = ((), (), s32[]{:S(2)}) async-start(), calls=%async_computation.4 | async-start | bytes 23887872 | tf_op jit(solution)/shard_map/all_gather | solution.py:666
  69.1 373.7 %reduce-scatter.4.cloned.1.call-start = ((), (), s32[]{:S(2)}) async-start(), calls=%async_computation.5 | async-start | bytes 11943936 | tf_op jit(solution)/shard_map/reduce_scatter | solution.py:819
  69.2 101.1 %collective-permute-start.14 = (bf16[288,2304]{1,0:T(8,128)(2,1)}, bf16[288,2304]{1,0:T(8,128)(2,1)}, u32[]{:S(2)}, u32[]{:S(2)}) collective-permute-start(bf16[288,2304]{1,0:T(8,128)(2,1)} %bitcast.18), channel_id=1, source_target_pairs={{0,4},{4,0},{8,12},{12,8},{16,20},{20,16},{24,28},{28,24},{1,5},{5... | collective-permute-start | bytes 3981320 | tf_op jit(solution)/shard_map/ppermute | solution.py:54
  94.8 26.1 %collective-permute-start.1 = (bf16[512,512]{1,0:T(8,128)(2,1)}, bf16[512,512]{1,0:T(8,128)(2,1)}, u32[]{:S(2)}, u32[]{:S(2)}) collective-permute-start(bf16[512,512]{1,0:T(8,128)(2,1)} %pad_maximum_fusion.6.one_ref), channel_id=1, source_target_pairs={{0,8},{4,12},{8,0},{12,4},{1,9},{5,13},{9,1},{13,5},{2,10},{6,14},... | collective-permute-start | bytes 1572872 | tf_op jit(solution)/shard_map/ppermute | solution.py:117
  97.8 30.7 %collective-permute-start = (bf16[512,512]{1,0:T(8,128)(2,1)}, bf16[512,512]{1,0:T(8,128)(2,1)}, u32[]{:S(2)}, u32[]{:S(2)}) collective-permute-start(bf16[512,512]{1,0:T(8,128)(2,1)} %pad_maximum_fusion.6.one_ref), channel_id=1, source_target_pairs={{0,4},{4,0},{8,12},{12,8},{1,5},{5,1},{9,13},{13,9},{2,6},{6,2},{1... | collective-permute-start | bytes 1572872 | tf_op jit(solution)/shard_map/ppermute | solution.py:54
  126.6 46.1 %collective-permute-start.15 = (bf16[288,2304]{1,0:T(8,128)(2,1)}, bf16[288,2304]{1,0:T(8,128)(2,1)}, u32[]{:S(2)}, u32[]{:S(2)}) collective-permute-start(bf16[288,2304]{1,0:T(8,128)(2,1)} %bitcast.18), channel_id=1, source_target_pairs={{0,16},{4,12},{8,0},{12,28},{24,8},{28,20},{16,24},{20,4},{1,17},{... | collective-permute-start | bytes 3981320 | tf_op jit(solution)/shard_map/ppermute | solution.py:117
  172.7 43.1 %collective-permute-start.17 = (bf16[288,2304]{1,0:T(8,128)(2,1)}, bf16[288,2304]{1,0:T(8,128)(2,1)}, u32[]{:S(2)}, u32[]{:S(2)}) collective-permute-start(bf16[288,2304]{1,0:T(8,128)(2,1)} %collective-permute-done.15), channel_id=1, source_target_pairs={{0,16},{4,12},{8,0},{12,28},{24,8},{28,20},{16,24},{20,4},{1,17},{... | collective-permute-start | bytes 3981320 | tf_op jit(solution)/shard_map/ppermute | solution.py:117
  174.0 59.9 %collective-permute-start.16 = (bf16[288,2304]{1,0:T(8,128)(2,1)}, bf16[288,2304]{1,0:T(8,128)(2,1)}, u32[]{:S(2)}, u32[]{:S(2)}) collective-permute-start(bf16[288,2304]{1,0:T(8,128)(2,1)} %collective-permute-done.15), channel_id=1, source_target_pairs={{0,4},{4,0},{8,12},{12,8},{16,20},{20,16},{24,28},{28,24},{1,5},{5... | collective-permute-start | bytes 3981320 | tf_op jit(solution)/shard_map/ppermute | solution.py:54
  215.8 18.1 %collective-permute-start.19 = (bf16[288,2304]{1,0:T(8,128)(2,1)}, bf16[288,2304]{1,0:T(8,128)(2,1)}, u32[]{:S(2)}, u32[]{:S(2)}) collective-permute-start(bf16[288,2304]{1,0:T(8,128)(2,1)} %collective-permute-done.17), channel_id=1, source_target_pairs={{0,16},{4,12},{8,0},{12,28},{24,8},{28,20},{16,24},{20,4},{1,17},{... | collective-permute-start | bytes 3981320 | tf_op jit(solution)/shard_map/ppermute | solution.py:117
  217.3 24.6 %collective-permute-start.22 = (bf16[64,2304]{1,0:T(8,128)(2,1)}, bf16[64,2304]{1,0:T(8,128)(2,1)}, u32[]{:S(2)}, u32[]{:S(2)}) collective-permute-start(bf16[64,2304]{1,0:T(8,128)(2,1)} %collective-permute-done.13), channel_id=1, source_target_pairs={{0,1},{1,2},{2,3},{3,0},{4,5},{5,6},{6,7},{7,4},{8,9},{9,10},{10,1... | collective-permute-start | bytes 884744 | tf_op jit(solution)/shard_map/ppermute | solution.py:194
  219.9 19.4 %collective-permute-start.18 = (bf16[288,2304]{1,0:T(8,128)(2,1)}, bf16[288,2304]{1,0:T(8,128)(2,1)}, u32[]{:S(2)}, u32[]{:S(2)}) collective-permute-start(bf16[288,2304]{1,0:T(8,128)(2,1)} %collective-permute-done.17), channel_id=1, source_target_pairs={{0,4},{4,0},{8,12},{12,8},{16,20},{20,16},{24,28},{28,24},{1,5},{5... | collective-permute-start | bytes 3981320 | tf_op jit(solution)/shard_map/ppermute | solution.py:54
  312.5 17.7 %collective-permute-start.31 = (bf16[64,2304]{1,0:T(8,128)(2,1)S(1)}, bf16[64,2304]{1,0:T(8,128)(2,1)S(1)}, u32[]{:S(2)}, u32[]{:S(2)}) collective-permute-start(bf16[64,2304]{1,0:T(8,128)(2,1)S(1)} %get-tuple-element.170), channel_id=1, source_target_pairs={{0,1},{1,2},{2,3},{3,0},{4,5},{5,6},{6,7},{7,4},{8,9},{9,10},{10,1... | collective-permute-start | bytes 884744 | tf_op jit(solution)/shard_map/ppermute | solution.py:194
  363.3 231.4 %reduce-scatter.6.cloned.1.call-start = ((), (), s32[]{:S(2)}) async-start(), calls=%async_computation.6 | async-start | bytes 23887872 | tf_op jit(solution)/shard_map/reduce_scatter | solution.py:822
  442.9 232.2 %reduce-scatter.8.cloned.1.call-start = ((), (), s32[]{:S(2)}) async-start(), calls=%async_computation.7 | async-start | bytes 8626176 | tf_op jit(solution)/shard_map/reduce_scatter | solution.py:870
  465.4 20.1 %collective-permute-start.40 = (bf16[64,2304]{1,0:T(8,128)(2,1)S(1)}, bf16[64,2304]{1,0:T(8,128)(2,1)S(1)}, u32[]{:S(2)}, u32[]{:S(2)}) collective-permute-start(bf16[64,2304]{1,0:T(8,128)(2,1)S(1)} %collective-permute-done.39), channel_id=1, source_target_pairs={{0,1},{1,2},{2,3},{3,0},{4,5},{5,6},{6,7},{7,4},{8,9},{9,10},{10,1... | collective-permute-start | bytes 884744 | tf_op jit(solution)/shard_map/ppermute | solution.py:194
  504.6 17.4 %collective-permute-start.46 = (bf16[2,64,2304]{2,1,0:T(8,128)(2,1)}, bf16[2,64,2304]{2,1,0:T(8,128)(2,1)}, u32[]{:S(2)}, u32[]{:S(2)}) collective-permute-start(bf16[2,64,2304]{2,1,0:T(8,128)(2,1)} %pad_maximum_fusion.5), channel_id=1, source_target_pairs={{0,1},{1,2},{2,3},{3,0},{4,5},{5,6},{6,7},{7,4},{8,9},{9,10},{10,1... | collective-permute-start | bytes 1769480 | tf_op jit(solution)/shard_map/ppermute | solution.py:194
  507.9 30.5 %collective-permute-start.50 = (bf16[512,512]{1,0:T(8,128)(2,1)}, bf16[512,512]{1,0:T(8,128)(2,1)}, u32[]{:S(2)}, u32[]{:S(2)}) collective-permute-start(bf16[512,512]{1,0:T(8,128)(2,1)} %get-tuple-element.181), channel_id=1, source_target_pairs={{0,4},{4,0},{8,12},{12,8},{1,5},{5,1},{9,13},{13,9},{2,6},{6,2},{1... | collective-permute-start | bytes 1572872 | tf_op jit(solution)/shard_map/ppermute | solution.py:54
  509.4 29.0 %collective-permute-start.51 = (bf16[512,512]{1,0:T(8,128)(2,1)}, bf16[512,512]{1,0:T(8,128)(2,1)}, u32[]{:S(2)}, u32[]{:S(2)}) collective-permute-start(bf16[512,512]{1,0:T(8,128)(2,1)} %add_convert_fusion), channel_id=1, source_target_pairs={{0,8},{4,12},{8,0},{12,4},{1,9},{5,13},{9,1},{13,5},{2,10},{6,14},... | collective-permute-start | bytes 1572872 | tf_op jit(solution)/shard_map/ppermute | solution.py:147
  547.2 17.7 %collective-permute-start.52 = (bf16[64,2304]{1,0:T(8,128)(2,1)}, bf16[64,2304]{1,0:T(8,128)(2,1)}, u32[]{:S(2)}, u32[]{:S(2)}) collective-permute-start(bf16[64,2304]{1,0:T(8,128)(2,1)} %constant_dynamic-slice_fusion.1), channel_id=1, source_target_pairs={{0,1},{1,2},{2,3},{3,0},{4,5},{5,6},{6,7},{7,4},{8,9},{9,10},{10,1... | collective-permute-start | bytes 884744 | tf_op jit(solution)/shard_map/ppermute | solution.py:172
  549.8 17.0 %collective-permute-start.64 = (f32[8,2304]{1,0:T(8,128)}, f32[8,2304]{1,0:T(8,128)S(1)}, u32[]{:S(2)}, u32[]{:S(2)}) collective-permute-start(f32[8,2304]{1,0:T(8,128)} %stack.79), channel_id=1, source_target_pairs={{0,1},{1,0},{2,3},{3,2},{4,5},{5,4},{6,7},{7,6},{8,9},{9,8},{10,11... | collective-permute-start | bytes 221192 | tf_op jit(solution)/shard_map/ppermute | solution.py:857
  600.4 39.3 %collective-permute-start.49 = (bf16[2,64,2304]{2,1,0:T(8,128)(2,1)S(1)}, bf16[2,64,2304]{2,1,0:T(8,128)(2,1)S(1)}, u32[]{:S(2)}, u32[]{:S(2)}) collective-permute-start(bf16[2,64,2304]{2,1,0:T(8,128)(2,1)S(1)} %copy-done.72), channel_id=1, source_target_pairs={{0,1},{1,2},{2,3},{3,0},{4,5},{5,6},{6,7},{7,4},{8,9},{9,10},{10,1... | collective-permute-start | bytes 1769480 | tf_op jit(solution)/shard_map/ppermute | solution.py:194
  616.0 17.3 %collective-permute-start.55 = (bf16[64,2304]{1,0:T(8,128)(2,1)S(1)}, bf16[64,2304]{1,0:T(8,128)(2,1)S(1)}, u32[]{:S(2)}, u32[]{:S(2)}) collective-permute-start(bf16[64,2304]{1,0:T(8,128)(2,1)S(1)} %get-tuple-element.158), channel_id=1, source_target_pairs={{0,1},{1,2},{2,3},{3,0},{4,5},{5,6},{6,7},{7,4},{8,9},{9,10},{10,1... | collective-permute-start | bytes 884744 | tf_op jit(solution)/shard_map/ppermute | solution.py:194
  617.0 22.6 %collective-permute-start.60 = (bf16[64,2304]{1,0:T(8,128)(2,1)S(1)}, bf16[64,2304]{1,0:T(8,128)(2,1)S(1)}, u32[]{:S(2)}, u32[]{:S(2)}) collective-permute-start(bf16[64,2304]{1,0:T(8,128)(2,1)S(1)} %get-tuple-element.160), channel_id=1, source_target_pairs={{0,1},{1,2},{2,3},{3,0},{4,5},{5,6},{6,7},{7,4},{8,9},{9,10},{10,1... | collective-permute-start | bytes 884744 | tf_op jit(solution)/shard_map/ppermute | solution.py:194
  (162 other events, 1668.0 us)
Sparse Core Ops, SparseCore 0:
  15.0 54.0 all-gather.2
  71.6 144.3 all-gather.4
  363.4 79.4 reduce-scatter.3
  446.4 148.3 reduce-scatter.5
  598.0 68.4 reduce-scatter.7
